TPU v7x, 32 devices: a whole 2x2x4 slice. The times are simulated.
32 devices in a mesh: cells: 8 (over z, y), tm: 4 (over x, core).
Axes of the slice: x: 2, y: 2, z: 4, core: 2. Of those that a mesh axis runs over, the one named last changes fastest.
Arguments:
- attitude: float32 [4, 8192], P(None, ('cells', 'tm')), may hold values from -6 to 6
- star_partials: float32 [5, 64, 16384], P(None, None, ('cells', 'tm')), may hold values from -6 to 6
- attitude_partials: float32 [4, 64, 16384], P(None, None, ('cells', 'tm')), may hold values from -6 to 6
- observed: float32 [64, 16384], P(None, ('cells', 'tm')), may hold values from -6 to 6
- phase: float32 [64, 16384], P(None, ('cells', 'tm')), may hold values from 0 to 1
- knot_offset: int32 [64, 16384], P(None, ('cells', 'tm')), may hold values from 0 to 12
- cell_counts: int32 [128], P(('cells', 'tm')), may hold values from 40 to 64, as said below
- interval_owner: int32 [128, 64, 1], P(('cells', 'tm')), may hold values from 0 to 31; in each aligned block of 256 rows (0 to 255, 256 to 511, ..., all dimensions but the last counted through in order) at most 12 rows name the same one
- block_slot: int32 [128, 64], P(('cells', 'tm')), may hold values from 0 to 15
Outputs:
- star_step: float32 [5, 16384], P(None, ('cells', 'tm'))
- attitude_step: float32 [4, 8192], P(None, ('cells', 'tm'))
Inputs may be any that keep to these rules, and one draw needn't show every extreme that they name: `interval_owner`: among the 256 transits of the cells of one device no owner is named more than 12 times, and in every draw some owner is named exactly 12 times by the transits of some device. Transits that are not live are listed too. `cell_counts`: some cell has all 64 transits live in every draw.
All inputs are finite; a program needn't handle non-finite values.
Results may differ from a plain program's by a relative error of at most 0.0003.
Values sent between devices are 32-bit elements; how exact they have to be, the bound alone decides.
No kernel may reach another device: no remote copies, remote signals or barrier semaphores. Data moves between devices by JAX's collectives and lax.ppermute only.
A program may use at most 128 MiB of HBM per device.

v0:
```python
import jax
import jax.numpy as jnp
from jax import lax
from jax.sharding import PartitionSpec as P

CS = 128
KB = 16
ITERS = 6


smoothing = 16.0
damping = 2.0
relaxation = 0.5
star_prior = 1.0
highest = lax.Precision.HIGHEST


def padded_2(shard, sides, width):
    for axis, dim in sides:
        size, length = (lax.axis_size(axis), shard.shape[dim])
        up = [(i, (i + 1) % size) for i in range(size - 1)]
        down = [(j, i) for i, j in up]
        last = lax.slice_in_dim(shard, length - width, length, axis=dim)
        leading = lax.slice_in_dim(shard, 0, width, axis=dim)
        before = lax.ppermute(last, axis, up)
        after = lax.ppermute(leading, axis, down)
        shard = jnp.concatenate([before, shard, after], axis=dim)
    return shard


def spline_basis(phase):
    square = phase * phase
    cube = square * phase
    rest = 1.0 - phase
    return (
        rest * rest * rest / 6.0,
        (3.0 * cube - 6.0 * square + 4.0) / 6.0,
        (-3.0 * cube + 3.0 * square + 3.0 * phase + 1.0) / 6.0,
        cube / 6.0,
    )


def design_rows(phase, knot_offset, partials, live):
    knots = lax.broadcasted_iota(jnp.int32, (KB, 1), 0)
    basis = spline_basis(phase)
    spread = jnp.zeros(phase.shape[:-1] + (KB, phase.shape[-1]), jnp.float32)
    for order in range(4):
        hit = knots == knot_offset[..., None, :] + order
        spread = spread + jnp.where(hit, basis[order][..., None, :], 0.0)
    spread = spread * live[..., None, None]
    return jnp.moveaxis(partials, 0, -2)[..., :, None, :] * spread[..., None, :, :]


def cholesky_factor(matrix, size):
    lower = [[None for column in range(size)] for row in range(size)]
    for column in range(size):
        total = matrix[column][column]
        for inner in range(column):
            total = total - lower[column][inner] * lower[column][inner]
        pivot = jnp.sqrt(total)
        lower[column][column] = pivot
        for row in range(column + 1, size):
            accum = matrix[row][column]
            for inner in range(column):
                accum = accum - lower[row][inner] * lower[column][inner]
            lower[row][column] = accum / pivot
    return lower


def cholesky_solve(lower, rhs, size):
    forward = []
    for row in range(size):
        accum = rhs[row]
        for inner in range(row):
            accum = accum - lower[row][inner] * forward[inner]
        forward.append(accum / lower[row][row])
    answer = [None for row in range(size)]
    for row in reversed(range(size)):
        accum = forward[row]
        for inner in range(row + 1, size):
            accum = accum - lower[inner][row] * answer[inner]
        answer[row] = accum / lower[row][row]
    return answer


def star_update(partials, first, live):
    normal = [
        [
            jnp.sum(live * partials[row] * partials[column], axis=0)
            + (star_prior if row == column else 0.0)
            for column in range(5)
        ]
        for row in range(5)
    ]
    rhs = [jnp.sum(partials[row] * first, axis=0) for row in range(5)]
    lower = cholesky_factor(normal, 5)
    step = cholesky_solve(lower, rhs, 5)
    fitted = partials[0] * step[0]
    for row in range(1, 5):
        fitted = fitted + partials[row] * step[row]
    return (jnp.stack(step), first - live * fitted)


def band_products(rows):
    pieces = []
    for shift in range(4):
        left = rows[..., : KB - shift, :]
        right = rows[..., shift:, :]
        product = jnp.einsum("...mas,...nas->...mna", left, right, precision=highest)
        filler = jnp.zeros(product.shape[:-1] + (shift,), jnp.float32)
        pieces.append(jnp.concatenate([product, filler], axis=-1))
    return jnp.stack(pieces, axis=-2)


def band_apply(band, vector):
    result = jnp.einsum("bmna,nba->mba", band[:, :, :, 0, :], vector, precision=highest)
    for shift in range(1, 4):
        filler = jnp.zeros(vector.shape[:-1] + (shift,), jnp.float32)
        ahead = jnp.concatenate([vector[..., shift:], filler], axis=-1)
        result = result + jnp.einsum(
            "bmna,nba->mba", band[:, :, :, shift, :], ahead, precision=highest
        )
        lagged = jnp.einsum("bnma,nba->mba", band[:, :, :, shift, :], vector, precision=highest)
        result = result + jnp.concatenate([filler, lagged[..., : KB - shift]], axis=-1)
    return result


def diagonal_factor(band):
    shifted = 2.0 * smoothing + damping
    entries = [
        [band[:, row, column, 0, :] + (shifted if row == column else 0.0) for column in range(4)]
        for row in range(4)
    ]
    return cholesky_factor(entries, 4)


def sweep(band, lower, gradient, solution, padded):
    count = band.shape[0]
    applied = band_apply(band, solution.reshape(4, count, KB))
    regular = smoothing * (2.0 * solution - padded[:, :-2] - padded[:, 2:]) + damping * solution
    misfit = gradient - applied - regular.reshape(4, count, KB)
    correction = cholesky_solve(lower, [misfit[row] for row in range(4)], 4)
    return solution + relaxation * jnp.stack(correction).reshape(4, count * KB)


def cell_work(items):
    cell_phase, cell_offset, cell_axis, cell_star, cell_observed, cell_live, cell_values = items
    rows = design_rows(cell_phase, cell_offset, cell_axis, cell_live)
    predicted = jnp.einsum("tmas,tma->ts", rows, cell_values, precision=highest)
    first = cell_live[:, None] * cell_observed - predicted
    step, second = star_update(cell_star, first, cell_live[:, None])
    gradient = jnp.einsum("tmas,ts->tma", rows, second, precision=highest)
    normal = band_products(rows).reshape(rows.shape[0], 64 * KB)
    return (step, normal, gradient.reshape(rows.shape[0], 4 * KB))


def per_device(
    attitude,
    star_partials,
    attitude_partials,
    observed,
    phase,
    knot_offset,
    cell_counts,
    interval_owner,
    block_slot,
):
    cell_groups = lax.axis_size("cells")
    time_groups = lax.axis_size("tm")
    devices = cell_groups * time_groups
    cells_here = cell_counts.shape[0]
    transits = observed.shape[0]
    blocks_here = attitude.shape[1] // KB
    total = cells_here * transits
    capacity = max(2, 3 * total // (2 * devices))
    owners = interval_owner.reshape(total)
    slots = block_slot.reshape(total)
    order = lax.broadcasted_iota(jnp.int32, (total, total), 0)
    other = lax.broadcasted_iota(jnp.int32, (total, total), 1)
    same = (owners[:, None] == owners[None, :]) & (other < order)
    rank = jnp.sum(same.astype(jnp.int32), axis=1)
    position = owners * capacity + rank
    requests = jnp.zeros((devices * capacity,), jnp.int32).at[position].set(slots)
    requested = lax.all_to_all(
        lax.all_to_all(
            requests.reshape(cell_groups, time_groups, capacity),
            "cells",
            split_axis=0,
            concat_axis=0,
            tiled=True,
        ),
        "tm",
        split_axis=1,
        concat_axis=1,
        tiled=True,
    )
    whole = lax.all_gather(attitude, ("cells", "tm"), axis=1, tiled=True)
    global_ids = owners * blocks_here + slots
    values = whole.reshape(4, -1, KB)[:, global_ids, :].transpose(1, 0, 2)
    transit = lax.broadcasted_iota(jnp.int32, (cells_here, transits), 1)
    live = jnp.where(transit < cell_counts[:, None], 1.0, 0.0).astype(jnp.float32)
    items = (
        phase.reshape(transits, cells_here, CS).transpose(1, 0, 2),
        knot_offset.reshape(transits, cells_here, CS).transpose(1, 0, 2),
        attitude_partials.reshape(4, transits, cells_here, CS).transpose(2, 0, 1, 3),
        star_partials.reshape(5, transits, cells_here, CS).transpose(2, 0, 1, 3),
        observed.reshape(transits, cells_here, CS).transpose(1, 0, 2),
        live,
        values.reshape(cells_here, transits, 4, KB),
    )
    steps, normals, gradients = lax.map(cell_work, items)
    payload = normals.reshape(total, normals.shape[-1])
    gradient_rows = gradients.reshape(total, 4 * KB)
    outgoing = (
        jnp.zeros((devices * capacity, payload.shape[1]), jnp.float32).at[position].set(payload)
    )
    outgoing_grad = (
        jnp.zeros((devices * capacity, 4 * KB), jnp.float32).at[position].set(gradient_rows)
    )
    arrived, arrived_grad = (
        lax.all_to_all(
            lax.all_to_all(
                outgoing.reshape(cell_groups, time_groups, capacity, payload.shape[1]),
                "cells",
                split_axis=0,
                concat_axis=0,
                tiled=True,
            ),
            "tm",
            split_axis=1,
            concat_axis=1,
            tiled=True,
        ),
        lax.all_to_all(
            lax.all_to_all(
                outgoing_grad.reshape(cell_groups, time_groups, capacity, 4 * KB),
                "cells",
                split_axis=0,
                concat_axis=0,
                tiled=True,
            ),
            "tm",
            split_axis=1,
            concat_axis=1,
            tiled=True,
        ),
    )
    member_rows = lax.broadcasted_iota(jnp.int32, (blocks_here, devices * capacity), 0)
    member = (member_rows == requested.reshape(1, devices * capacity)).astype(jnp.float32)
    block_normal = jnp.dot(
        member,
        arrived.reshape(devices * capacity, payload.shape[1]),
        precision=highest,
        preferred_element_type=jnp.float32,
    )
    block_grad = jnp.dot(
        member,
        arrived_grad.reshape(devices * capacity, 4 * KB),
        precision=highest,
        preferred_element_type=jnp.float32,
    )
    band = block_normal.reshape(blocks_here, 4, 4, 4, KB)
    gradient = block_grad.reshape(blocks_here, 4, KB).transpose(1, 0, 2)
    lower = diagonal_factor(band)
    solution = jnp.zeros((4, blocks_here * KB), jnp.float32)
    for index in range(ITERS):
        padded = padded_2(solution, ((("cells", "tm"), 1),), 1)
        solution = sweep(band, lower, gradient, solution, padded)
    star_step = steps.transpose(1, 0, 2).reshape(5, cells_here * CS)
    return (star_step, solution)


def solution(mesh):
    placed = (
        P(None, ("cells", "tm")),
        P(None, None, ("cells", "tm")),
        P(None, None, ("cells", "tm")),
        P(None, ("cells", "tm")),
        P(None, ("cells", "tm")),
        P(None, ("cells", "tm")),
        P(("cells", "tm")),
        P(("cells", "tm"), None, None),
        P(("cells", "tm"), None),
    )
    return jax.shard_map(
        per_device,
        mesh=mesh,
        in_specs=placed,
        out_specs=(P(None, ("cells", "tm")), P(None, ("cells", "tm"))),
        check_vma=False,
    )
```

profile of v0, /device:TPU:0, one launch (start us, length us, event | category | flops | bytes accessed | tf_op | source)
XLA Modules:
  0.0 481.9 jit_solution(1023052929936181640)
XLA Ops:
  5.8 7.3 %all-to-all-start = ((s32[8,4,12]{2,1,0:T(4,128)}), s32[8,4,12]{2,1,0:T(4,128)S(1)}, u32[]{:S(2)}, u32[]{:S(2)}) async-start(s32[8,4,12]{2,1,0:T(4,128)} %reshape.1704), calls=%async_computation | async-start | bytes 32768 | tf_op jit(solution)/shard_map/all_to_all | solution.py:185
  15.9 42.5 %all_gather.3 = f32[4,8192]{1,0:T(4,128)S(1)} all-gather(f32[4,256]{1,0:T(4,128)} %param.11), channel_id=1, replica_groups=mesh['cells'=8,'tm'=4] {'cells','tm'}, dimensions={1}, use_global_device_ids=true | all-gather | bytes 135168 | tf_op jit(solution)/shard_map/all_gather | solution.py:197
  69.6 270.7 %while.14 = (s32[]{:T(128)}, f32[4,5,128]{2,1,0:T(8,128)}, f32[4,64,1024]{2,1,0:T(8,128)}, f32[4,64,64]{2,1,0:T(8,128)}, f32[4,5,64,128]{3,0,2,1:T(4,128)S(1)}, ...) while((s32[]{:T(128)}, f32[4,5,128]{2,1,0:T(8,128)}, ...), condition=%wide.region_21.22_spmd, body=%wide.region_0.21_spmd.sunk | while | flops 108887808 | bytes 30208528 | solution.py:211
  97.7 14.7 %fusion.334 = f32[64,1,4,16]{3,1,2,0:T(1,128)S(1)} fusion(f32[64,128,1,1]{1,2,3,0:T(1,128)S(1)} %bitcast.1036, f32[64,4,16,128]{3,1,2,0:T(4,128)S(1)} %broadcast_multiply_fusion.3), kind=kOutput, calls=%fused_computation.15.clone.1 | convolution fusion | flops 6291456 | bytes 2146304 | tf_op jit(solution)/shard_map/while/body/eval_jaxpr/tmas,ts->tma/dot_general | solution.py:152
  113.2 5.5 %fusion.330 = f32[64,4,4,13]{1,2,3,0:T(4,128)S(1)} fusion(f32[64,4,16,128]{3,1,2,0:T(4,128)S(1)} %broadcast_multiply_fusion.3, f32[64,16,128]{2,1,0:T(8,128)S(1)} %add_multiply_fusion.2, f32[64,4,128]{2,1,0:T(4,128)S(1)} %bitcast.1026), kind=kOutput, calls=%fused_computation.25.clone.1 | convolution fusion | flops 20971520 | bytes 2412544 | tf_op jit(solution)/shard_map/while/body/eval_jaxpr/...mas,...nas->...mna/dot_general | solution.py:109
  123.0 7.0 %fusion.331 = f32[64,4,4,14]{1,2,3,0:T(4,128)} fusion(f32[64,4,16,128]{3,1,2,0:T(4,128)S(1)} %broadcast_multiply_fusion.3, f32[64,16,128]{2,1,0:T(8,128)S(1)} %add_multiply_fusion.2, f32[64,4,128]{2,1,0:T(4,128)S(1)} %bitcast.1027), kind=kOutput, calls=%fused_computation.24.clone.1 | convolution fusion | flops 22544384 | bytes 2547712 | tf_op jit(solution)/shard_map/while/body/eval_jaxpr/...mas,...nas->...mna/dot_general | solution.py:109
  130.0 6.4 %fusion.332 = f32[64,4,4,15]{1,2,3,0:T(4,128)S(1)} fusion(f32[64,4,16,128]{3,1,2,0:T(4,128)S(1)} %broadcast_multiply_fusion.3, f32[64,16,128]{2,1,0:T(8,128)S(1)} %add_multiply_fusion.2, f32[64,4,128]{2,1,0:T(4,128)S(1)} %bitcast.1028), kind=kOutput, calls=%fused_computation.23.clone.1 | convolution fusion | flops 24117248 | bytes 2682880 | tf_op jit(solution)/shard_map/while/body/eval_jaxpr/...mas,...nas->...mna/dot_general | solution.py:109
  141.6 7.0 %fusion.333 = f32[64,4,4,1,16]{1,2,4,0,3:T(4,128)S(1)} fusion(f32[64,16,128]{2,1,0:T(8,128)S(1)} %add_multiply_fusion.2, f32[64,4,128]{2,1,0:T(4,128)S(1)} %bitcast.1029), kind=kOutput, calls=%fused_computation.22.clone.1 | convolution fusion | flops 25690112 | bytes 720896 | tf_op jit(solution)/shard_map/while/body/eval_jaxpr/...mas,...nas->...mna/dot_general | solution.py:109
  157.5 14.7 %fusion.334 = f32[64,1,4,16]{3,1,2,0:T(1,128)S(1)} fusion(f32[64,128,1,1]{1,2,3,0:T(1,128)S(1)} %bitcast.1036, f32[64,4,16,128]{3,1,2,0:T(4,128)S(1)} %broadcast_multiply_fusion.3), kind=kOutput, calls=%fused_computation.15.clone.1 | convolution fusion | flops 6291456 | bytes 2146304 | tf_op jit(solution)/shard_map/while/body/eval_jaxpr/tmas,ts->tma/dot_general | solution.py:152
  173.0 5.5 %fusion.330 = f32[64,4,4,13]{1,2,3,0:T(4,128)S(1)} fusion(f32[64,4,16,128]{3,1,2,0:T(4,128)S(1)} %broadcast_multiply_fusion.3, f32[64,16,128]{2,1,0:T(8,128)S(1)} %add_multiply_fusion.2, f32[64,4,128]{2,1,0:T(4,128)S(1)} %bitcast.1026), kind=kOutput, calls=%fused_computation.25.clone.1 | convolution fusion | flops 20971520 | bytes 2412544 | tf_op jit(solution)/shard_map/while/body/eval_jaxpr/...mas,...nas->...mna/dot_general | solution.py:109
  182.8 7.0 %fusion.331 = f32[64,4,4,14]{1,2,3,0:T(4,128)} fusion(f32[64,4,16,128]{3,1,2,0:T(4,128)S(1)} %broadcast_multiply_fusion.3, f32[64,16,128]{2,1,0:T(8,128)S(1)} %add_multiply_fusion.2, f32[64,4,128]{2,1,0:T(4,128)S(1)} %bitcast.1027), kind=kOutput, calls=%fused_computation.24.clone.1 | convolution fusion | flops 22544384 | bytes 2547712 | tf_op jit(solution)/shard_map/while/body/eval_jaxpr/...mas,...nas->...mna/dot_general | solution.py:109
  189.9 6.4 %fusion.332 = f32[64,4,4,15]{1,2,3,0:T(4,128)S(1)} fusion(f32[64,4,16,128]{3,1,2,0:T(4,128)S(1)} %broadcast_multiply_fusion.3, f32[64,16,128]{2,1,0:T(8,128)S(1)} %add_multiply_fusion.2, f32[64,4,128]{2,1,0:T(4,128)S(1)} %bitcast.1028), kind=kOutput, calls=%fused_computation.23.clone.1 | convolution fusion | flops 24117248 | bytes 2682880 | tf_op jit(solution)/shard_map/while/body/eval_jaxpr/...mas,...nas->...mna/dot_general | solution.py:109
  201.5 7.0 %fusion.333 = f32[64,4,4,1,16]{1,2,4,0,3:T(4,128)S(1)} fusion(f32[64,16,128]{2,1,0:T(8,128)S(1)} %add_multiply_fusion.2, f32[64,4,128]{2,1,0:T(4,128)S(1)} %bitcast.1029), kind=kOutput, calls=%fused_computation.22.clone.1 | convolution fusion | flops 25690112 | bytes 720896 | tf_op jit(solution)/shard_map/while/body/eval_jaxpr/...mas,...nas->...mna/dot_general | solution.py:109
  217.4 14.7 %fusion.334 = f32[64,1,4,16]{3,1,2,0:T(1,128)S(1)} fusion(f32[64,128,1,1]{1,2,3,0:T(1,128)S(1)} %bitcast.1036, f32[64,4,16,128]{3,1,2,0:T(4,128)S(1)} %broadcast_multiply_fusion.3), kind=kOutput, calls=%fused_computation.15.clone.1 | convolution fusion | flops 6291456 | bytes 2146304 | tf_op jit(solution)/shard_map/while/body/eval_jaxpr/tmas,ts->tma/dot_general | solution.py:152
  242.7 7.0 %fusion.331 = f32[64,4,4,14]{1,2,3,0:T(4,128)} fusion(f32[64,4,16,128]{3,1,2,0:T(4,128)S(1)} %broadcast_multiply_fusion.3, f32[64,16,128]{2,1,0:T(8,128)S(1)} %add_multiply_fusion.2, f32[64,4,128]{2,1,0:T(4,128)S(1)} %bitcast.1027), kind=kOutput, calls=%fused_computation.24.clone.1 | convolution fusion | flops 22544384 | bytes 2547712 | tf_op jit(solution)/shard_map/while/body/eval_jaxpr/...mas,...nas->...mna/dot_general | solution.py:109
  249.7 6.4 %fusion.332 = f32[64,4,4,15]{1,2,3,0:T(4,128)S(1)} fusion(f32[64,4,16,128]{3,1,2,0:T(4,128)S(1)} %broadcast_multiply_fusion.3, f32[64,16,128]{2,1,0:T(8,128)S(1)} %add_multiply_fusion.2, f32[64,4,128]{2,1,0:T(4,128)S(1)} %bitcast.1028), kind=kOutput, calls=%fused_computation.23.clone.1 | convolution fusion | flops 24117248 | bytes 2682880 | tf_op jit(solution)/shard_map/while/body/eval_jaxpr/...mas,...nas->...mna/dot_general | solution.py:109
  261.4 7.0 %fusion.333 = f32[64,4,4,1,16]{1,2,4,0,3:T(4,128)S(1)} fusion(f32[64,16,128]{2,1,0:T(8,128)S(1)} %add_multiply_fusion.2, f32[64,4,128]{2,1,0:T(4,128)S(1)} %bitcast.1029), kind=kOutput, calls=%fused_computation.22.clone.1 | convolution fusion | flops 25690112 | bytes 720896 | tf_op jit(solution)/shard_map/while/body/eval_jaxpr/...mas,...nas->...mna/dot_general | solution.py:109
  277.2 14.7 %fusion.334 = f32[64,1,4,16]{3,1,2,0:T(1,128)S(1)} fusion(f32[64,128,1,1]{1,2,3,0:T(1,128)S(1)} %bitcast.1036, f32[64,4,16,128]{3,1,2,0:T(4,128)S(1)} %broadcast_multiply_fusion.3), kind=kOutput, calls=%fused_computation.15.clone.1 | convolution fusion | flops 6291456 | bytes 2146304 | tf_op jit(solution)/shard_map/while/body/eval_jaxpr/tmas,ts->tma/dot_general | solution.py:152
  302.5 7.0 %fusion.331 = f32[64,4,4,14]{1,2,3,0:T(4,128)} fusion(f32[64,4,16,128]{3,1,2,0:T(4,128)S(1)} %broadcast_multiply_fusion.3, f32[64,16,128]{2,1,0:T(8,128)S(1)} %add_multiply_fusion.2, f32[64,4,128]{2,1,0:T(4,128)S(1)} %bitcast.1027), kind=kOutput, calls=%fused_computation.24.clone.1 | convolution fusion | flops 22544384 | bytes 2547712 | tf_op jit(solution)/shard_map/while/body/eval_jaxpr/...mas,...nas->...mna/dot_general | solution.py:109
  309.6 6.4 %fusion.332 = f32[64,4,4,15]{1,2,3,0:T(4,128)S(1)} fusion(f32[64,4,16,128]{3,1,2,0:T(4,128)S(1)} %broadcast_multiply_fusion.3, f32[64,16,128]{2,1,0:T(8,128)S(1)} %add_multiply_fusion.2, f32[64,4,128]{2,1,0:T(4,128)S(1)} %bitcast.1028), kind=kOutput, calls=%fused_computation.23.clone.1 | convolution fusion | flops 24117248 | bytes 2682880 | tf_op jit(solution)/shard_map/while/body/eval_jaxpr/...mas,...nas->...mna/dot_general | solution.py:109
  321.2 7.0 %fusion.333 = f32[64,4,4,1,16]{1,2,4,0,3:T(4,128)S(1)} fusion(f32[64,16,128]{2,1,0:T(8,128)S(1)} %add_multiply_fusion.2, f32[64,4,128]{2,1,0:T(4,128)S(1)} %bitcast.1029), kind=kOutput, calls=%fused_computation.22.clone.1 | convolution fusion | flops 25690112 | bytes 720896 | tf_op jit(solution)/shard_map/while/body/eval_jaxpr/...mas,...nas->...mna/dot_general | solution.py:109
  353.4 5.7 %all-to-all-start.4 = ((f32[8,4,12,1024]{3,1,2,0:T(4,128)}), f32[8,4,12,1024]{3,1,2,0:T(4,128)S(1)}, u32[]{:S(2)}, u32[]{:S(2)}) async-start(f32[8,4,12,1024]{3,1,2,0:T(4,128)} %copy.105), calls=%async_computation.4 | async-start | bytes 3145728 | tf_op jit(solution)/shard_map/all_to_all | solution.py:222
  361.4 34.8 %all-to-all-done.4 = f32[8,4,12,1024]{3,1,2,0:T(4,128)S(1)} async-done(((f32[8,4,12,1024]{3,1,2,0:T(4,128)}), f32[8,4,12,1024]{3,1,2,0:T(4,128)S(1)}, u32[]{:S(2)}, u32[]{:S(2)}) %all-to-all-start.4) | async-done | bytes 1572896 | tf_op jit(solution)/shard_map/all_to_all | solution.py:222
  415.2 13.1 %all-to-all-done.5 = f32[8,4,12,1024]{3,0,2,1:T(8,128)} async-done(((f32[8,4,12,1024]{3,0,2,1:T(8,128)}), f32[8,4,12,1024]{3,0,2,1:T(8,128)}, u32[]{:S(2)}, u32[]{:S(2)}) %all-to-all-start.5) | async-done | bytes 1572896 | tf_op jit(solution)/shard_map/all_to_all | solution.py:221
  (377 shorter events, 193.9 us)
Async XLA Ops:
  0.6 62.5 %copy-start.4 = (f32[5,64,512]{2,1,0:T(8,128)S(1)}, f32[5,64,512]{2,1,0:T(8,128)}, u32[]{:S(2)}) copy-start(f32[5,64,512]{2,1,0:T(8,128)} %param.12) | copy-start | bytes 1966084
  3.7 11.5 %copy-start.5 = (s32[256,1]{0,1:T(1,128)}, s32[256,1]{0,1:T(1,128)S(1)}, u32[]{:S(2)}) copy-start(s32[256,1]{0,1:T(1,128)S(1)} %compare_select_fusion) | copy-start | bytes 3076
  5.8 59.9 %all-to-all-start = ((s32[8,4,12]{2,1,0:T(4,128)}), s32[8,4,12]{2,1,0:T(4,128)S(1)}, u32[]{:S(2)}, u32[]{:S(2)}) async-start(s32[8,4,12]{2,1,0:T(4,128)} %reshape.1704), calls=%async_computation | async-start | bytes 32768 | tf_op jit(solution)/shard_map/all_to_all | solution.py:185
  66.3 276.4 %all-to-all-start.1 = ((s32[8,4,12]{2,0,1:T(8,128)}), s32[8,4,12]{2,0,1:T(8,128)S(1)}, u32[]{:S(2)}, u32[]{:S(2)}) async-start(s32[8,4,12]{2,0,1:T(8,128)} %copy.96), calls=%async_computation.1 | async-start | bytes 32768 | tf_op jit(solution)/shard_map/all_to_all | solution.py:184
  91.3 2.3 copy-start
  91.3 2.3 copy-start.2
  151.2 2.3 copy-start.2
  211.1 2.3 copy-start.2
  342.8 10.6 %all-to-all-start.2 = ((f32[8,1,3072]{2,1,0:T(1,128)}), f32[8,1,3072]{2,1,0:T(1,128)S(1)}, u32[]{:S(2)}, u32[]{:S(2)}) async-start(f32[8,1,3072]{2,1,0:T(1,128)} %reshape.1864), calls=%async_computation.2 | async-start | bytes 196608 | tf_op jit(solution)/shard_map/all_to_all | solution.py:235
  353.4 42.9 %all-to-all-start.4 = ((f32[8,4,12,1024]{3,1,2,0:T(4,128)}), f32[8,4,12,1024]{3,1,2,0:T(4,128)S(1)}, u32[]{:S(2)}, u32[]{:S(2)}) async-start(f32[8,4,12,1024]{3,1,2,0:T(4,128)} %copy.105), calls=%async_computation.4 | async-start | bytes 3145728 | tf_op jit(solution)/shard_map/all_to_all | solution.py:222
  396.2 7.6 %all-to-all-start.3 = ((f32[4,1,6144]{2,1,0:T(1,128)}), f32[4,1,6144]{2,1,0:T(1,128)S(1)}, u32[]{:S(2)}, u32[]{:S(2)}) async-start(f32[4,1,6144]{2,1,0:T(1,128)} %reshape.1866), calls=%async_computation.3 | async-start | bytes 196608 | tf_op jit(solution)/shard_map/all_to_all | solution.py:234
  403.8 24.5 %all-to-all-start.5 = ((f32[8,4,12,1024]{3,0,2,1:T(8,128)}), f32[8,4,12,1024]{3,0,2,1:T(8,128)}, u32[]{:S(2)}, u32[]{:S(2)}) async-start(f32[8,4,12,1024]{3,0,2,1:T(8,128)} %copy.106), calls=%async_computation.5 | async-start | bytes 3145728 | tf_op jit(solution)/shard_map/all_to_all | solution.py:221
  408.2 4.3 collective-permute-start.1
  409.5 3.8 collective-permute-start
  438.6 5.4 %collective-permute-start.2 = (f32[4,1]{1,0:T(4,128)S(1)}, f32[4,1]{1,0:T(4,128)S(1)}, u32[]{:S(2)}, u32[]{:S(2)}) collective-permute-start(f32[4,1]{1,0:T(4,128)S(1)} %get-tuple-element.314), channel_id=1, source_target_pairs={{0,1},{1,2},{2,3},{3,4},{4,5},{5,6},{6,7},{7,8},{8,9},{9,10},{10,1... | collective-permute-start | bytes 56 | tf_op jit(solution)/shard_map/ppermute | solution.py:25
  442.5 3.1 collective-permute-start.3
  446.6 5.3 %collective-permute-start.4 = (f32[4,1]{1,0:T(4,128)S(1)}, f32[4,1]{1,0:T(4,128)S(1)}, u32[]{:S(2)}, u32[]{:S(2)}) collective-permute-start(f32[4,1]{1,0:T(4,128)S(1)} %get-tuple-element.312), channel_id=1, source_target_pairs={{0,1},{1,2},{2,3},{3,4},{4,5},{5,6},{6,7},{7,8},{8,9},{9,10},{10,1... | collective-permute-start | bytes 56 | tf_op jit(solution)/shard_map/ppermute | solution.py:25
  450.4 3.1 collective-permute-start.5
  454.5 6.8 %collective-permute-start.6 = (f32[4,1]{1,0:T(4,128)S(1)}, f32[4,1]{1,0:T(4,128)S(1)}, u32[]{:S(2)}, u32[]{:S(2)}) collective-permute-start(f32[4,1]{1,0:T(4,128)S(1)} %get-tuple-element.310), channel_id=1, source_target_pairs={{0,1},{1,2},{2,3},{3,4},{4,5},{5,6},{6,7},{7,8},{8,9},{9,10},{10,1... | collective-permute-start | bytes 56 | tf_op jit(solution)/shard_map/ppermute | solution.py:25
  459.8 3.1 collective-permute-start.7
  463.9 6.2 %collective-permute-start.8 = (f32[4,1]{1,0:T(4,128)S(1)}, f32[4,1]{1,0:T(4,128)S(1)}, u32[]{:S(2)}, u32[]{:S(2)}) collective-permute-start(f32[4,1]{1,0:T(4,128)S(1)} %get-tuple-element.308), channel_id=1, source_target_pairs={{0,1},{1,2},{2,3},{3,4},{4,5},{5,6},{6,7},{7,8},{8,9},{9,10},{10,1... | collective-permute-start | bytes 56 | tf_op jit(solution)/shard_map/ppermute | solution.py:25
  468.6 3.1 collective-permute-start.9
  472.7 6.2 %collective-permute-start.10 = (f32[4,1]{1,0:T(4,128)S(1)}, f32[4,1]{1,0:T(4,128)S(1)}, u32[]{:S(2)}, u32[]{:S(2)}) collective-permute-start(f32[4,1]{1,0:T(4,128)S(1)} %get-tuple-element.306), channel_id=1, source_target_pairs={{0,1},{1,2},{2,3},{3,4},{4,5},{5,6},{6,7},{7,8},{8,9},{9,10},{10,1... | collective-permute-start | bytes 56 | tf_op jit(solution)/shard_map/ppermute | solution.py:25
  477.4 3.1 collective-permute-start.11
  (12 other events, 18.8 us)
where the time goes:
time: 492 us; the launch traced here: 482 us
  matrix products  174 us (35%)
  local copies, waits for them, and re-layouts  98.2 us (20%)
  starting transfers between devices  60.4 us (12%)
  waiting for transfers between devices  59.2 us (12%)
  blocking collectives  42.5 us (9%)
  loops' own time  31.9 us (6%)
  other arithmetic  13.9 us (3%)
    dot_general x16, matrix products, band_products(): jnp.einsum('...mas,...nas->...mna', left, right, precision=highest)  104 us
    dot_general x4, matrix products, cell_work(): gradient = jnp.einsum('tmas,ts->tma', rows, second, precision=highest)  58.6 us
    another operation x28, local copies, waits for them, and re-layouts, band_products(): return jnp.stack(pieces, axis=-2)  43.3 us
    all_gather x1, blocking collectives, per_device(): whole = lax.all_gather(attitude, ('cells', 'tm'), axis=1, tiled=True)  42.5 us
    all_to_all x1, waiting for transfers between devices, per_device(): lax.all_to_all(outgoing.reshape(cell_groups, time_groups, capacity, paylo...  34.8 us
    another operation x1, loops' own time, per_device(): steps, normals, gradients = lax.map(cell_work, items)  31.9 us
    ppermute x6, starting transfers between devices, padded_2(): before = lax.ppermute(last, axis, up)  25.5 us
    all_to_all x1, waiting for transfers between devices, per_device(): lax.all_to_all(lax.all_to_all(outgoing.reshape(cell_groups, time_groups,...  13.1 us
  transfers between devices with their start and end apart: 18, of which 10 were waited for; matrix products, arithmetic and copies ran while one was open for 55% of the time, Pallas kernels for 0%

commit v1 on v0

v1 whole, which is shorter than its diff:
```python
import functools

import jax
import jax.numpy as jnp
from jax import lax
from jax.experimental import pallas as pl
from jax.experimental.pallas import tpu as pltpu
from jax.sharding import PartitionSpec as P

CS = 128
KB = 16
ITERS = 6
LANES = 128
PAIRS = tuple((m, n) for m in range(4) for n in range(m, 4))
ROWS = 5
VMEM_LIMIT = 48 * 1024 * 1024

smoothing = 16.0
damping = 2.0
relaxation = 0.5
star_prior = 1.0


def spline_basis(phase):
    square = phase * phase
    cube = square * phase
    rest = 1.0 - phase
    return (
        rest * rest * rest * (1.0 / 6.0),
        (3.0 * cube - 6.0 * square + 4.0) * (1.0 / 6.0),
        (-3.0 * cube + 3.0 * square + 3.0 * phase + 1.0) * (1.0 / 6.0),
        cube * (1.0 / 6.0),
    )


def cholesky_factor(matrix, size):
    lower = [[None for column in range(size)] for row in range(size)]
    inverse = [None for column in range(size)]
    for column in range(size):
        total = matrix[column][column]
        for inner in range(column):
            total = total - lower[column][inner] * lower[column][inner]
        inverse[column] = 1.0 / jnp.sqrt(total)
        for row in range(column + 1, size):
            accum = matrix[row][column]
            for inner in range(column):
                accum = accum - lower[row][inner] * lower[column][inner]
            lower[row][column] = accum * inverse[column]
    return lower, inverse


def cholesky_solve(lower, inverse, rhs, size):
    forward = []
    for row in range(size):
        accum = rhs[row]
        for inner in range(row):
            accum = accum - lower[row][inner] * forward[inner]
        forward.append(accum * inverse[row])
    answer = [None for row in range(size)]
    for row in reversed(range(size)):
        accum = forward[row]
        for inner in range(row + 1, size):
            accum = accum - lower[inner][row] * answer[inner]
        answer[row] = accum * inverse[row]
    return answer


def split(value):
    high = value.astype(jnp.bfloat16)
    low = (value - high.astype(jnp.float32)).astype(jnp.bfloat16)
    return high, low


def pair_rows(value):
    return jnp.broadcast_to(value, (KB, LANES))


def product(weights, matrix_high, matrix_low):
    return lax.dot_general(
        weights,
        jnp.concatenate([matrix_high, matrix_low], axis=1),
        (((1,), (1,)), ((), ())),
        preferred_element_type=jnp.float32,
    )


def normal_kernel(
    spread, counts, home, halo, phase_ref, offset_ref, axis_ref, out_ref, total, weights, basis, offsets
):
    transits, stars = phase_ref.shape
    cells = stars // LANES
    knots = lax.broadcasted_iota(jnp.int32, (KB, LANES), 0)
    left_half = lax.broadcasted_iota(jnp.int32, (8, LANES), 1) < 64
    total[...] = jnp.zeros_like(total)
    weights[...] = jnp.zeros_like(weights)
    groups = transits // 8

    def group(index, carry):
        cell = index // groups
        first = pl.multiple_of((index % groups) * 8, 8)
        rows = pl.ds(first, 8)
        columns = pl.ds(pl.multiple_of(cell * LANES, LANES), LANES)
        number = first + lax.broadcasted_iota(jnp.int32, (8, LANES), 0)
        live = jnp.where(number < counts[cell], 1.0, 0.0)
        values = spline_basis(phase_ref[rows, columns])
        for shift in range(4):
            for order in range(4 - shift):
                basis[shift * 4 + order] = values[order] * values[order + shift]
        offsets[...] = offset_ref[rows, columns]
        parts = [axis_ref[m, rows, columns] for m in range(4)]
        lively = [part * live for part in parts]
        for place, (m, n) in enumerate(PAIRS):
            row = place if place < ROWS else place + 3
            weights[pl.ds(row, 8, stride=16), :] = lively[m] * parts[n]
        for j in range(8):
            relative = knots - pair_rows(offsets[pl.ds(j, 1), :])
            hits = [relative == order for order in range(4)]
            highs, lows = [], []
            for shift in range(4):
                piece = jnp.zeros((KB, LANES), jnp.float32)
                for order in range(4 - shift):
                    value = pair_rows(basis[shift * 4 + order, pl.ds(j, 1), :])
                    piece = jnp.where(hits[order], value, piece)
                high, low = split(piece)
                highs.append(high)
                lows.append(low)
            weight_high, weight_low = split(weights[pl.ds(j * 16, 16), :])
            left = jnp.concatenate([weight_high, weight_low], axis=0)
            right = jnp.concatenate([weight_high, jnp.zeros_like(weight_low)], axis=0)
            result = product(
                jnp.concatenate([left, right], axis=1),
                jnp.concatenate(highs + highs, axis=0),
                jnp.concatenate(lows + lows, axis=0),
            )
            band = jnp.where(
                left_half, result[0:8] + result[16:24], result[8:16] + result[24:32]
            )
            transit = cell * transits + first + j
            for place in (home[transit], halo[transit]):
                block = pl.ds(pl.multiple_of(place * 8, 8), 8)
                total[block, :] = total[block, :] + band
        return carry

    lax.fori_loop(0, cells * groups, group, 0)

    def pack(index, carry):
        source = pl.multiple_of(index * 64, 64)
        target = pl.multiple_of(index * 8 * ROWS, 8)
        for j in range(8):
            out_ref[pl.ds(target + j * ROWS, ROWS), :] = total[pl.ds(source + j * 8, ROWS), :]
        return carry

    lax.fori_loop(0, out_ref.shape[0] // (8 * ROWS), pack, 0)


def star_kernel(
    spread,
    counts,
    home,
    halo,
    ids,
    attitude_ref,
    phase_ref,
    offset_ref,
    axis_ref,
    star_ref,
    observed_ref,
    step_ref,
    out_ref,
    total,
    table,
    first_order,
    sums,
    steps,
    weights,
    basis,
    offsets,
):
    transits, stars = phase_ref.shape
    cells = stars // LANES
    groups = transits // 8
    knots = lax.broadcasted_iota(jnp.int32, (KB, LANES), 0)
    lanes_block = lax.broadcasted_iota(jnp.int32, (8, LANES), 1) // KB
    total[...] = jnp.zeros_like(total)
    weights[...] = jnp.zeros_like(weights)
    sums[...] = jnp.zeros_like(sums)
    entries = [(row, column) for row in range(5) for column in range(row + 1)]

    def predict_cell(cell, carry):
        columns = pl.ds(pl.multiple_of(cell * LANES, LANES), LANES)

        def predict(index, accumulated):
            first = pl.multiple_of(index * 8, 8)
            rows = pl.ds(first, 8)
            for j in range(8):
                block = ids[cell * transits + first + j]
                row = attitude_ref[pl.ds(block // 2, 1), :]
                table[pl.ds(j, 1), :] = pltpu.roll(row, (block % 2) * 64, axis=1)
            looked = table[...]
            number = first + lax.broadcasted_iota(jnp.int32, (8, LANES), 0)
            live = jnp.where(number < counts[cell], 1.0, 0.0)
            values = spline_basis(phase_ref[rows, columns])
            offset = offset_ref[rows, columns]
            predicted = jnp.zeros((8, LANES), jnp.float32)
            for m in range(4):
                spline = jnp.zeros((8, LANES), jnp.float32)
                for order in range(4):
                    found = jnp.take_along_axis(looked, offset + (m * KB + order), axis=1)
                    spline = spline + found * values[order]
                predicted = predicted + spline * axis_ref[m, rows, columns]
            first_value = live * (observed_ref[rows, columns] - predicted)
            first_order[rows, columns] = first_value
            parts = [star_ref[row, rows, columns] for row in range(5)]
            lively = [part * live for part in parts]
            added = [lively[row] * parts[column] for row, column in entries]
            added += [part * first_value for part in parts]
            return tuple(old + new for old, new in zip(accumulated, added))

        start = tuple(jnp.zeros((8, LANES), jnp.float32) for entry in range(20))
        accumulated = lax.fori_loop(0, groups, predict, start)
        for entry in range(20):
            sums[entry, pl.ds(cell, 1), :] = jnp.sum(accumulated[entry], axis=0, keepdims=True)
        return carry

    lax.fori_loop(0, cells, predict_cell, 0)

    normal = [[None for column in range(5)] for row in range(5)]
    for entry, (row, column) in enumerate(entries):
        normal[row][column] = sums[entry] + (star_prior if row == column else 0.0)
    lower, inverse = cholesky_factor(normal, 5)
    answer = cholesky_solve(lower, inverse, [sums[15 + row] for row in range(5)], 5)
    for row in range(5):
        steps[row] = answer[row]
        for cell in range(cells):
            step_ref[row : row + 1, cell * LANES : (cell + 1) * LANES] = answer[row][
                cell : cell + 1
            ]

    def group(index, carry):
        cell = index // groups
        first = pl.multiple_of((index % groups) * 8, 8)
        rows = pl.ds(first, 8)
        columns = pl.ds(pl.multiple_of(cell * LANES, LANES), LANES)
        number = first + lax.broadcasted_iota(jnp.int32, (8, LANES), 0)
        live = jnp.where(number < counts[cell], 1.0, 0.0)
        fitted = jnp.zeros((8, LANES), jnp.float32)
        for row in range(5):
            step = jnp.broadcast_to(steps[row, pl.ds(cell, 1), :], (8, LANES))
            fitted = fitted + star_ref[row, rows, columns] * step
        second = first_order[rows, columns] - live * fitted
        for m in range(4):
            value = axis_ref[m, rows, columns] * second
            high = value.astype(jnp.bfloat16).astype(jnp.float32)
            weights[pl.ds(m, 8, stride=16), :] = high
            weights[pl.ds(4 + m, 8, stride=16), :] = value - high
        values = spline_basis(phase_ref[rows, columns])
        for order in range(4):
            basis[order] = values[order]
        offsets[...] = offset_ref[rows, columns]
        for j in range(8):
            relative = knots - pair_rows(offsets[pl.ds(j, 1), :])
            piece = jnp.zeros((KB, LANES), jnp.float32)
            for order in range(4):
                value = pair_rows(basis[order, pl.ds(j, 1), :])
                piece = jnp.where(relative == order, value, piece)
            high, low = split(piece)
            weight = weights[pl.ds(j * 16, 16), :]
            right = jnp.where(knots < 4, weight, 0.0)
            result = product(
                jnp.concatenate([weight, right], axis=1).astype(jnp.bfloat16),
                jnp.concatenate([high] * 8, axis=0),
                jnp.concatenate([low] * 8, axis=0),
            )[0:8]
            transit = cell * transits + first + j
            for place in (home[transit], halo[transit]):
                owner = place // spread
                slot = place % spread
                chosen = jnp.where(lanes_block == slot % 8, result, 0.0)
                tile = owner * ((spread + 7) // 8) + slot // 8
                block = pl.ds(pl.multiple_of(tile * 8, 8), 8)
                total[block, :] = total[block, :] + chosen
        return carry

    lax.fori_loop(0, cells * groups, group, 0)

    def pack(index, carry):
        source = pl.multiple_of(index * 16, 16)
        first_tile = total[pl.ds(source, 8), :]
        second_tile = total[pl.ds(source + 8, 8), :]
        target = pl.multiple_of(index * 8, 8)
        out_ref[pl.ds(target, 4), :] = first_tile[0:4] + first_tile[4:8]
        out_ref[pl.ds(target + 4, 4), :] = second_tile[0:4] + second_tile[4:8]
        return carry

    lax.fori_loop(0, out_ref.shape[0] // 8, pack, 0)


def sweep_kernel(spread, ends, band_ref, gradient_ref, out_ref, band):
    width = band.shape[2]
    tiles = width // LANES
    lane_block = lax.broadcasted_iota(jnp.int32, (8, LANES), 1) // KB
    filler = jnp.zeros((8 - ROWS, LANES), jnp.float32)
    for half in range(2):
        for shift in range(4):
            start = half * 64 + shift * KB
            for tile in range(tiles):
                merged = jnp.zeros((8, LANES), jnp.float32)
                for place in range(min(8, spread - tile * 8)):
                    block = tile * 8 + place
                    piece = jnp.concatenate(
                        [band_ref[block * ROWS : (block + 1) * ROWS, :], filler], axis=0
                    )
                    moved = (place * KB - start) % LANES
                    if moved:
                        piece = pltpu.roll(piece, moved, axis=1)
                    merged = jnp.where(lane_block == place, piece, merged)
                band[shift, half * 8 : half * 8 + 8, tile * LANES : (tile + 1) * LANES] = merged
    index = {}
    for place, (m, n) in enumerate(PAIRS):
        row = place if place < ROWS else place + 3
        index[(m, n)] = row
        index[(n, m)] = row

    def row_of(shift, m, n):
        return band[shift, index[(m, n)] : index[(m, n)] + 1, :]

    ahead = [
        [jnp.concatenate([row_of(shift, m, n) for n in range(4)], axis=0) for m in range(4)]
        for shift in range(4)
    ]
    behind = [
        [pltpu.roll(ahead[shift][m], shift, axis=1) if shift else None for m in range(4)]
        for shift in range(4)
    ]
    shifted = 2.0 * smoothing + damping
    diagonal = [
        [row_of(0, row, column) + (shifted if row == column else 0.0) for column in range(4)]
        for row in range(4)
    ]
    lower, inverse = cholesky_factor(diagonal, 4)
    gradient = jnp.concatenate(
        [gradient_ref[tile * 4 : (tile + 1) * 4, :] for tile in range(tiles)], axis=1
    )
    lane = lax.broadcasted_iota(jnp.int32, (4, width), 1)
    keep = jnp.where((lane >= ends[0]) & (lane < ends[1]), relaxation, 0.0)
    answer = jnp.zeros((4, width), jnp.float32)
    for sweep in range(ITERS):
        misfit = gradient
        if sweep:
            moved = {}
            for shift in range(1, 4):
                moved[shift] = pltpu.roll(answer, width - shift, axis=1)
                moved[-shift] = pltpu.roll(answer, shift, axis=1)
            applied = []
            for m in range(4):
                terms = ahead[0][m] * answer
                for shift in range(1, 4):
                    terms = terms + ahead[shift][m] * moved[shift]
                    terms = terms + behind[shift][m] * moved[-shift]
                applied.append(jnp.sum(terms, axis=0, keepdims=True))
            regular = smoothing * (2.0 * answer - moved[-1] - moved[1]) + damping * answer
            misfit = gradient - regular - jnp.concatenate(applied, axis=0)
        correction = cholesky_solve(lower, inverse, [misfit[m : m + 1] for m in range(4)], 4)
        answer = answer + keep * jnp.concatenate(correction, axis=0)
    out_ref[...] = answer[:, KB : KB + out_ref.shape[1]]


def in_vmem(count):
    return [pl.BlockSpec(memory_space=pltpu.VMEM) for operand in range(count)]


def in_smem(count):
    return [pl.BlockSpec(memory_space=pltpu.SMEM) for operand in range(count)]


def params():
    return pltpu.CompilerParams(vmem_limit_bytes=VMEM_LIMIT)


def halving_sum(parts, axes, devices):
    me = lax.axis_index(axes)
    for bit in range(devices.bit_length() - 1):
        half = parts.shape[0] // 2
        upper = (me >> bit) & 1
        kept = lax.dynamic_slice_in_dim(parts, upper * half, half, 0)
        sent = lax.dynamic_slice_in_dim(parts, (1 - upper) * half, half, 0)
        pairs = [(i, i ^ (1 << bit)) for i in range(devices)]
        parts = kept + lax.ppermute(sent, axes, pairs)
    return parts


def per_device(
    attitude,
    star_partials,
    attitude_partials,
    observed,
    phase,
    knot_offset,
    cell_counts,
    interval_owner,
    block_slot,
):
    axes = ("cells", "tm")
    devices = lax.axis_size("cells") * lax.axis_size("tm")
    levels = devices.bit_length() - 1
    cells = cell_counts.shape[0]
    transits = observed.shape[0]
    total = cells * transits
    stars = cells * CS
    blocks = attitude.shape[1] // KB
    spread = blocks + 2
    tiles = (spread + 7) // 8
    width = tiles * LANES
    me = lax.axis_index(axes)

    owners = interval_owner.reshape(total)
    slots = block_slot.reshape(total)

    def position(owner):
        reversed_bits = jnp.zeros_like(owner)
        for bit in range(levels):
            reversed_bits = reversed_bits | (((owner >> bit) & 1) << (levels - 1 - bit))
        return reversed_bits * spread

    nowhere = devices * spread
    home = position(owners) + slots + 1
    before = jnp.where(owners > 0, position(jnp.maximum(owners - 1, 0)) + spread - 1, nowhere)
    after = jnp.where(owners < devices - 1, position(jnp.minimum(owners + 1, devices - 1)), nowhere)
    halo = jnp.where(slots == 0, before, jnp.where(slots == blocks - 1, after, nowhere))
    ids = owners * blocks + slots

    table = attitude.reshape(4, blocks, KB).transpose(1, 0, 2).reshape(blocks // 2, 8 * KB)
    whole = lax.all_to_all(
        jnp.broadcast_to(table[None], (devices,) + table.shape),
        axes,
        split_axis=0,
        concat_axis=0,
        tiled=True,
    ).reshape(devices * blocks // 2, 8 * KB)

    f32 = jnp.float32
    normals = pl.pallas_call(
        functools.partial(normal_kernel, spread),
        out_shape=jax.ShapeDtypeStruct((devices * spread * ROWS, LANES), f32),
        in_specs=in_smem(3) + in_vmem(3),
        out_specs=in_vmem(1)[0],
        scratch_shapes=[
            pltpu.VMEM(((devices * spread + 1) * 8, LANES), f32),
            pltpu.VMEM((8 * 16, LANES), f32),
            pltpu.VMEM((16, 8, LANES), f32),
            pltpu.VMEM((8, LANES), jnp.int32),
        ],
        compiler_params=params(),
        name="normals",
    )(cell_counts, home, halo, phase, knot_offset, attitude_partials)

    star_step, gradients = pl.pallas_call(
        functools.partial(star_kernel, spread),
        out_shape=[
            jax.ShapeDtypeStruct((5, stars), f32),
            jax.ShapeDtypeStruct((devices * tiles * 4, LANES), f32),
        ],
        in_specs=in_smem(4) + in_vmem(6),
        out_specs=in_vmem(2),
        scratch_shapes=[
            pltpu.VMEM(((devices + 1) * tiles * 8, LANES), f32),
            pltpu.VMEM((8, LANES), f32),
            pltpu.VMEM((transits, stars), f32),
            pltpu.VMEM((20, 8, LANES), f32),
            pltpu.VMEM((5, 8, LANES), f32),
            pltpu.VMEM((8 * 16, LANES), f32),
            pltpu.VMEM((4, 8, LANES), f32),
            pltpu.VMEM((8, LANES), jnp.int32),
        ],
        compiler_params=params(),
        name="stars",
    )(
        cell_counts,
        home,
        halo,
        ids,
        whole,
        phase,
        knot_offset,
        attitude_partials,
        star_partials,
        observed,
    )

    band = halving_sum(normals, axes, devices)
    gradient = halving_sum(gradients, axes, devices)
    ends = jnp.stack(
        [
            jnp.where(me == 0, KB, 0),
            jnp.where(me == devices - 1, (spread - 1) * KB, spread * KB),
        ]
    ).astype(jnp.int32)
    attitude_step = pl.pallas_call(
        functools.partial(sweep_kernel, spread),
        out_shape=jax.ShapeDtypeStruct((4, blocks * KB), f32),
        in_specs=in_smem(1) + in_vmem(2),
        out_specs=in_vmem(1)[0],
        scratch_shapes=[pltpu.VMEM((4, 16, width), f32)],
        compiler_params=params(),
        name="sweeps",
    )(ends, band, gradient)
    return (star_step, attitude_step)


def solution(mesh):
    split_axes = ("cells", "tm")
    placed = (
        P(None, split_axes),
        P(None, None, split_axes),
        P(None, None, split_axes),
        P(None, split_axes),
        P(None, split_axes),
        P(None, split_axes),
        P(split_axes),
        P(split_axes, None, None),
        P(split_axes, None),
    )
    return jax.shard_map(
        per_device,
        mesh=mesh,
        in_specs=placed,
        out_specs=(P(None, split_axes), P(None, split_axes)),
        check_vma=False,
    )
```

time: 492 us -> 80.3 us (0.16); the launches traced: 482 us -> 79.9 us
  matrix products: 174 us -> 0 us
  local copies, waits for them, and re-layouts: 98.2 us -> 6.39 us
  blocking collectives: 42.5 us -> 0 us
  waiting for transfers between devices: 59.2 us -> 18.3 us
  starting transfers between devices: 60.4 us -> 21.3 us
  Pallas kernels: 0 us -> 32.1 us
  loops' own time: 31.9 us -> 0 us
  other arithmetic: 13.9 us -> 1.04 us
    dot_general x26 -> x0, matrix products: 174 us -> none  [the longest x16 104 us: band_products(): jnp.einsum('...mas,...nas->...mna', left, right, precision=highest)]
    all_to_all x6 -> x1, waiting for transfers between devices: 50.4 us -> 0.01 us  [per_device(): lax.all_to_all(jnp.broadcast_to(table[None], (devices,) + table.shape), a...]
    another operation x57 -> x0, local copies, waits for them, and re-layouts: 45.3 us -> none  [the longest x28 43.3 us: band_products(): return jnp.stack(pieces, axis=-2)]
    all_gather x1 -> x0, blocking collectives: 42.5 us -> none  [per_device(): whole = lax.all_gather(attitude, ('cells', 'tm'), axis=1, tiled=True)]
    pallas_call x0 -> x3, Pallas kernels: none -> 32.1 us  [the longest x1 18.4 us: per_device(): pl.pallas_call(functools.partial(star_kernel, spread), out_shape=[jax.Sha...]
    another operation x1 -> x0, loops' own time: 31.9 us -> none  [per_device(): steps, normals, gradients = lax.map(cell_work, items)]
    all_to_all x6 -> x1, starting transfers between devices: 27.2 us -> 7.3 us  [per_device(): lax.all_to_all(jnp.broadcast_to(table[None], (devices,) + table.shape), a...]
    ppermute x12 -> x10, starting transfers between devices: 33.2 us -> 14 us  [halving_sum(): parts = kept + lax.ppermute(sent, axes, pairs)]
  transfers between devices with their start and end apart: 18 -> 11, of which waited for: 10 -> 7; matrix products, arithmetic and copies ran while one was open for 55% -> 3% of each run, Pallas kernels for 0% -> 14%
where the time goes in v1:
time: 80.3 us; the launch traced here: 79.9 us
  Pallas kernels  32.1 us (40%)
  starting transfers between devices  21.3 us (27%)
  waiting for transfers between devices  18.3 us (23%)
  local copies, waits for them, and re-layouts  6.39 us (8%)
  other arithmetic  1.04 us (1%)
  between operations  0.84 us (1%)
    pallas_call x1, Pallas kernels, per_device(): pl.pallas_call(functools.partial(star_kernel, spread), out_shape=[jax.Sha...  18.4 us
    ppermute x10, waiting for transfers between devices, halving_sum(): parts = kept + lax.ppermute(sent, axes, pairs)  18.3 us
    ppermute x10, starting transfers between devices, halving_sum(): parts = kept + lax.ppermute(sent, axes, pairs)  14 us
    pallas_call x1, Pallas kernels, per_device(): pl.pallas_call(functools.partial(normal_kernel, spread), out_shape=jax.Sh...  11.4 us
    all_to_all x1, starting transfers between devices, per_device(): lax.all_to_all(jnp.broadcast_to(table[None], (devices,) + table.shape), a...  7.3 us
    unnamed x20, local copies, waits for them, and re-layouts  3.53 us
    pallas_call x1, Pallas kernels, per_device(): pl.pallas_call(functools.partial(sweep_kernel, spread), out_shape=jax.Sha...  2.27 us
  transfers between devices with their start and end apart: 11, of which 7 were waited for; matrix products, arithmetic and copies ran while one was open for 3% of the time, Pallas kernels for 14%

profile of v1, /device:TPU:0, one launch (start us, length us, event | category | flops | bytes accessed | tf_op | source)
XLA Modules:
  0.0 79.9 jit_solution(1748145868299121541)
XLA Ops:
  0.7 0.8 %reshape.101 = f32[4,16,16]{2,1,0:T(8,128)S(1)} reshape(f32[4,256]{1,0:T(4,128)} %param.9) | data formatting | bytes 8192 | tf_op jit(solution)/shard_map/reshape | solution.py:432
  1.6 0.7 broadcast_in_dim.15
  2.2 7.3 %all-to-all-start = ((f32[32,8,128]{2,1,0:T(8,128)}), f32[32,8,128]{2,1,0:T(8,128)S(1)}, u32[]{:S(2)}, u32[]{:S(2)}) async-start(f32[32,8,128]{2,1,0:T(8,128)} %broadcast_in_dim.15), calls=%async_computation | async-start | bytes 262144 | tf_op jit(solution)/shard_map/all_to_all | solution.py:433
  9.6 0.7 multiply_reduce_fusion.1
  10.3 0.8 reshape.100
  11.4 1.0 %copy-done = f32[4,64,512]{2,1,0:T(8,128)S(1)} copy-done((f32[4,64,512]{2,1,0:T(8,128)S(1)}, f32[4,64,512]{2,1,0:T(8,128)}, u32[]{:S(2)}) %copy-start) | copy-done | bytes 524312
  12.5 0.9 %copy-done.3 = f32[64,512]{1,0:T(8,128)S(1)} copy-done((f32[64,512]{1,0:T(8,128)S(1)}, f32[64,512]{1,0:T(8,128)}, u32[]{:S(2)}) %copy-start.3) | copy-done | bytes 131096
  13.4 0.9 %copy-done.5 = s32[64,512]{1,0:T(8,128)S(1)} copy-done((s32[64,512]{1,0:T(8,128)S(1)}, s32[64,512]{1,0:T(8,128)}, u32[]{:S(2)}) %copy-start.5) | copy-done | bytes 131096
  14.9 11.4 %normals.1 = f32[2880,128]{1,0:T(8,128)S(1)} custom-call(s32[4]{0:T(128)S(1)} %copy-done.8, s32[256]{0:T(256)S(1)} %get-tuple-element.12.home, s32[256]{0:T(256)S(1)} %get-tuple-element.11.halo, f32[64,512]{1,0:T(8,128)S(1)} %copy-done.3, s32[64,512]{1,0:T(8,128)S(1)} %copy-done.5, f32[4,64,512]{2,1,0:T(8,128)S(1)} %copy-done), custom_call_target="tpu_custom_call" | custom-call | tf_op jit(solution)/shard_map/normals/pallas_call | solution.py:442
  26.4 18.4 %stars.1 = (f32[5,512]{1,0:T(8,128)}, f32[384,128]{1,0:T(8,128)S(1)}) custom-call(s32[4]{0:T(128)S(1)} %copy-done.9, s32[256]{0:T(256)S(1)} %get-tuple-element.12.home, s32[256]{0:T(256)S(1)} %get-tuple-element.11.halo, s32[256]{0:T(256)S(1)} %get-tuple-element.10.ids, f32[256,128]{1,0:T(8,128)S(1)} %bitcast.6, f32[64,512]{1,0:T(8,128)S(1)} %copy-done.4, ...), custom_call_target="tpu_custom_call" | custom-call | tf_op jit(solution)/shard_map/stars/pallas_call | solution.py:457
  45.5 0.7 collective-permute-done.5
  46.2 1.8 %collective-permute-start.6 = (f32[96,128]{1,0:T(8,128)S(1)}, f32[96,128]{1,0:T(8,128)S(1)}, u32[]{:S(2)}, u32[]{:S(2)}) collective-permute-start(f32[96,128]{1,0:T(8,128)S(1)} %constant_dynamic-slice_fusion.3), channel_id=1, source_target_pairs={{0,2},{1,3},{2,0},{3,1},{4,6},{5,7},{6,4},{7,5},{8,10},{9,11},{10,... | collective-permute-start | bytes 147464 | tf_op jit(solution)/shard_map/ppermute | solution.py:388
  48.1 2.3 %collective-permute-done.6 = f32[96,128]{1,0:T(8,128)S(1)} collective-permute-done((f32[96,128]{1,0:T(8,128)S(1)}, f32[96,128]{1,0:T(8,128)S(1)}, u32[]{:S(2)}, u32[]{:S(2)}) %collective-permute-start.6) | collective-permute-done | bytes 49184 | tf_op jit(solution)/shard_map/ppermute | solution.py:388
  50.4 1.8 %collective-permute-start.7 = (f32[48,128]{1,0:T(8,128)S(1)}, f32[48,128]{1,0:T(8,128)S(1)}, u32[]{:S(2)}, u32[]{:S(2)}) collective-permute-start(f32[48,128]{1,0:T(8,128)S(1)} %constant_dynamic-slice_fusion.2), channel_id=1, source_target_pairs={{0,4},{1,5},{2,6},{3,7},{4,0},{5,1},{6,2},{7,3},{8,12},{9,13},{10,... | collective-permute-start | bytes 73736 | tf_op jit(solution)/shard_map/ppermute | solution.py:388
  52.4 1.5 %collective-permute-start.1 = (f32[720,128]{1,0:T(8,128)S(1)}, f32[720,128]{1,0:T(8,128)S(1)}, u32[]{:S(2)}, u32[]{:S(2)}) collective-permute-start(f32[720,128]{1,0:T(8,128)S(1)} %constant_dynamic-slice_fusion.8), channel_id=1, source_target_pairs={{0,2},{1,3},{2,0},{3,1},{4,6},{5,7},{6,4},{7,5},{8,10},{9,11},{10,... | collective-permute-start | bytes 1105928 | tf_op jit(solution)/shard_map/ppermute | solution.py:388
  54.3 1.8 %collective-permute-start.8 = (f32[24,128]{1,0:T(8,128)S(1)}, f32[24,128]{1,0:T(8,128)S(1)}, u32[]{:S(2)}, u32[]{:S(2)}) collective-permute-start(f32[24,128]{1,0:T(8,128)S(1)} %constant_dynamic-slice_fusion.1), channel_id=1, source_target_pairs={{0,8},{1,9},{2,10},{3,11},{4,12},{5,13},{6,14},{7,15},{8,0},{9,1},... | collective-permute-start | bytes 36872 | tf_op jit(solution)/shard_map/ppermute | solution.py:388
  56.2 5.5 %collective-permute-done.1 = f32[720,128]{1,0:T(8,128)S(1)} collective-permute-done((f32[720,128]{1,0:T(8,128)S(1)}, f32[720,128]{1,0:T(8,128)S(1)}, u32[]{:S(2)}, u32[]{:S(2)}) %collective-permute-start.1) | collective-permute-done | bytes 368672 | tf_op jit(solution)/shard_map/ppermute | solution.py:388
  62.2 5.2 %collective-permute-done.2 = f32[360,128]{1,0:T(8,128)S(1)} collective-permute-done((f32[360,128]{1,0:T(8,128)S(1)}, f32[360,128]{1,0:T(8,128)S(1)}, u32[]{:S(2)}, u32[]{:S(2)}) %collective-permute-start.2) | collective-permute-done | bytes 184352 | tf_op jit(solution)/shard_map/ppermute | solution.py:388
  67.4 1.5 %collective-permute-start.3 = (f32[180,128]{1,0:T(8,128)S(1)}, f32[180,128]{1,0:T(8,128)S(1)}, u32[]{:S(2)}, u32[]{:S(2)}) collective-permute-start(f32[180,128]{1,0:T(8,128)S(1)} %constant_dynamic-slice_fusion.6), channel_id=1, source_target_pairs={{0,8},{1,9},{2,10},{3,11},{4,12},{5,13},{6,14},{7,15},{8,0},{9,1},... | collective-permute-start | bytes 276488 | tf_op jit(solution)/shard_map/ppermute | solution.py:388
  68.9 2.4 %collective-permute-start.9 = (f32[12,128]{1,0:T(8,128)S(1)}, f32[12,128]{1,0:T(8,128)S(1)}, u32[]{:S(2)}, u32[]{:S(2)}) collective-permute-start(f32[12,128]{1,0:T(8,128)S(1)} %constant_dynamic-slice_fusion), channel_id=1, source_target_pairs={{0,16},{1,17},{2,18},{3,19},{4,20},{5,21},{6,22},{7,23},{8,24},{9,... | collective-permute-start | bytes 18440 | tf_op jit(solution)/shard_map/ppermute | solution.py:388
  71.4 1.2 %collective-permute-done.3 = f32[180,128]{1,0:T(8,128)S(1)} collective-permute-done((f32[180,128]{1,0:T(8,128)S(1)}, f32[180,128]{1,0:T(8,128)S(1)}, u32[]{:S(2)}, u32[]{:S(2)}) %collective-permute-start.3) | collective-permute-done | bytes 92192 | tf_op jit(solution)/shard_map/ppermute | solution.py:388
  72.6 1.9 %collective-permute-start.4 = (f32[90,128]{1,0:T(8,128)S(1)}, f32[90,128]{1,0:T(8,128)S(1)}, u32[]{:S(2)}, u32[]{:S(2)}) collective-permute-start(f32[90,128]{1,0:T(8,128)S(1)} %constant_dynamic-slice_fusion.5), channel_id=1, source_target_pairs={{0,16},{1,17},{2,18},{3,19},{4,20},{5,21},{6,22},{7,23},{8,24},{9,... | collective-permute-start | bytes 138248 | tf_op jit(solution)/shard_map/ppermute | solution.py:388
  74.5 3.1 %collective-permute-done.4 = f32[90,128]{1,0:T(8,128)S(1)} collective-permute-done((f32[90,128]{1,0:T(8,128)S(1)}, f32[90,128]{1,0:T(8,128)S(1)}, u32[]{:S(2)}, u32[]{:S(2)}) %collective-permute-start.4) | collective-permute-done | bytes 46112 | tf_op jit(solution)/shard_map/ppermute | solution.py:388
  77.7 2.3 %sweeps.1 = f32[4,256]{1,0:T(4,128)} custom-call(s32[2]{0:T(128)S(1)} %pad_add_fusion.ends, f32[90,128]{1,0:T(8,128)S(1)} %dynamic-slice_add_fusion.6.band_ref, f32[12,128]{1,0:T(8,128)S(1)} %dynamic-slice_add_fusion.9.gradient_ref), custom_call_target="tpu_custom_call" | custom-call | tf_op jit(solution)/shard_map/sweeps/pallas_call | solution.py:498
  (53 shorter events, 3.0 us)
Async XLA Ops:
  0.6 25.7 %copy-start.9 = (s32[4]{0:T(128)S(1)}, s32[4]{0:T(128)}, u32[]{:S(2)}) copy-start(s32[4]{0:T(128)} %counts.3) | copy-start | bytes 52
  0.6 25.7 %copy-start.1 = (f32[4,64,512]{2,1,0:T(8,128)S(1)}, f32[4,64,512]{2,1,0:T(8,128)}, u32[]{:S(2)}) copy-start(f32[4,64,512]{2,1,0:T(8,128)} %axis_ref.3) | copy-start | bytes 1572868
  2.2 24.1 %all-to-all-start = ((f32[32,8,128]{2,1,0:T(8,128)}), f32[32,8,128]{2,1,0:T(8,128)S(1)}, u32[]{:S(2)}, u32[]{:S(2)}) async-start(f32[32,8,128]{2,1,0:T(8,128)} %broadcast_in_dim.15), calls=%async_computation | async-start | bytes 262144 | tf_op jit(solution)/shard_map/all_to_all | solution.py:433
  11.4 1.0 %copy-start = (f32[4,64,512]{2,1,0:T(8,128)S(1)}, f32[4,64,512]{2,1,0:T(8,128)}, u32[]{:S(2)}) copy-start(f32[4,64,512]{2,1,0:T(8,128)} %axis_ref.3) | copy-start | bytes 1572868
  12.5 0.9 %copy-start.3 = (f32[64,512]{1,0:T(8,128)S(1)}, f32[64,512]{1,0:T(8,128)}, u32[]{:S(2)}) copy-start(f32[64,512]{1,0:T(8,128)} %phase_ref.3) | copy-start | bytes 393220
  13.4 0.9 %copy-start.5 = (s32[64,512]{1,0:T(8,128)S(1)}, s32[64,512]{1,0:T(8,128)}, u32[]{:S(2)}) copy-start(s32[64,512]{1,0:T(8,128)} %offset_ref.3) | copy-start | bytes 393220
  14.3 0.7 copy-start.8
  14.9 11.4 %copy-start.2 = (f32[5,64,512]{2,1,0:T(8,128)S(1)}, f32[5,64,512]{2,1,0:T(8,128)}, u32[]{:S(2)}) copy-start(f32[5,64,512]{2,1,0:T(8,128)} %star_ref.1) | copy-start | bytes 1966084
  14.9 11.4 %copy-start.4 = (f32[64,512]{1,0:T(8,128)S(1)}, f32[64,512]{1,0:T(8,128)}, u32[]{:S(2)}) copy-start(f32[64,512]{1,0:T(8,128)} %phase_ref.3) | copy-start | bytes 393220
  14.9 11.4 %copy-start.6 = (s32[64,512]{1,0:T(8,128)S(1)}, s32[64,512]{1,0:T(8,128)}, u32[]{:S(2)}) copy-start(s32[64,512]{1,0:T(8,128)} %offset_ref.3) | copy-start | bytes 393220
  14.9 11.5 %copy-start.7 = (f32[64,512]{1,0:T(8,128)S(1)}, f32[64,512]{1,0:T(8,128)}, u32[]{:S(2)}) copy-start(f32[64,512]{1,0:T(8,128)} %observed_ref.1) | copy-start | bytes 393220
  44.8 1.4 %collective-permute-start.5 = (f32[192,128]{1,0:T(8,128)S(1)}, f32[192,128]{1,0:T(8,128)S(1)}, u32[]{:S(2)}, u32[]{:S(2)}) collective-permute-start(f32[192,128]{1,0:T(8,128)S(1)} %constant_dynamic-slice_fusion.4), channel_id=1, source_target_pairs={{0,1},{1,0},{2,3},{3,2},{4,5},{5,4},{6,7},{7,6},{8,9},{9,8},{10,11... | collective-permute-start | bytes 294920 | tf_op jit(solution)/shard_map/ppermute | solution.py:388
  45.2 7.1 %collective-permute-start = (f32[1440,128]{1,0:T(8,128)S(1)}, f32[1440,128]{1,0:T(8,128)S(1)}, u32[]{:S(2)}, u32[]{:S(2)}) collective-permute-start(f32[1440,128]{1,0:T(8,128)S(1)} %constant_dynamic-slice_fusion.9), channel_id=1, source_target_pairs={{0,1},{1,0},{2,3},{3,2},{4,5},{5,4},{6,7},{7,6},{8,9},{9,8},{10,11... | collective-permute-start | bytes 2211848 | tf_op jit(solution)/shard_map/ppermute | solution.py:388
  46.2 4.2 %collective-permute-start.6 = (f32[96,128]{1,0:T(8,128)S(1)}, f32[96,128]{1,0:T(8,128)S(1)}, u32[]{:S(2)}, u32[]{:S(2)}) collective-permute-start(f32[96,128]{1,0:T(8,128)S(1)} %constant_dynamic-slice_fusion.3), channel_id=1, source_target_pairs={{0,2},{1,3},{2,0},{3,1},{4,6},{5,7},{6,4},{7,5},{8,10},{9,11},{10,... | collective-permute-start | bytes 147464 | tf_op jit(solution)/shard_map/ppermute | solution.py:388
  50.4 3.9 %collective-permute-start.7 = (f32[48,128]{1,0:T(8,128)S(1)}, f32[48,128]{1,0:T(8,128)S(1)}, u32[]{:S(2)}, u32[]{:S(2)}) collective-permute-start(f32[48,128]{1,0:T(8,128)S(1)} %constant_dynamic-slice_fusion.2), channel_id=1, source_target_pairs={{0,4},{1,5},{2,6},{3,7},{4,0},{5,1},{6,2},{7,3},{8,12},{9,13},{10,... | collective-permute-start | bytes 73736 | tf_op jit(solution)/shard_map/ppermute | solution.py:388
  52.4 9.3 %collective-permute-start.1 = (f32[720,128]{1,0:T(8,128)S(1)}, f32[720,128]{1,0:T(8,128)S(1)}, u32[]{:S(2)}, u32[]{:S(2)}) collective-permute-start(f32[720,128]{1,0:T(8,128)S(1)} %constant_dynamic-slice_fusion.8), channel_id=1, source_target_pairs={{0,2},{1,3},{2,0},{3,1},{4,6},{5,7},{6,4},{7,5},{8,10},{9,11},{10,... | collective-permute-start | bytes 1105928 | tf_op jit(solution)/shard_map/ppermute | solution.py:388
  54.3 7.8 %collective-permute-start.8 = (f32[24,128]{1,0:T(8,128)S(1)}, f32[24,128]{1,0:T(8,128)S(1)}, u32[]{:S(2)}, u32[]{:S(2)}) collective-permute-start(f32[24,128]{1,0:T(8,128)S(1)} %constant_dynamic-slice_fusion.1), channel_id=1, source_target_pairs={{0,8},{1,9},{2,10},{3,11},{4,12},{5,13},{6,14},{7,15},{8,0},{9,1},... | collective-permute-start | bytes 36872 | tf_op jit(solution)/shard_map/ppermute | solution.py:388
  61.7 5.6 %collective-permute-start.2 = (f32[360,128]{1,0:T(8,128)S(1)}, f32[360,128]{1,0:T(8,128)S(1)}, u32[]{:S(2)}, u32[]{:S(2)}) collective-permute-start(f32[360,128]{1,0:T(8,128)S(1)} %constant_dynamic-slice_fusion.7), channel_id=1, source_target_pairs={{0,4},{1,5},{2,6},{3,7},{4,0},{5,1},{6,2},{7,3},{8,12},{9,13},{10,... | collective-permute-start | bytes 552968 | tf_op jit(solution)/shard_map/ppermute | solution.py:388
  67.4 5.2 %collective-permute-start.3 = (f32[180,128]{1,0:T(8,128)S(1)}, f32[180,128]{1,0:T(8,128)S(1)}, u32[]{:S(2)}, u32[]{:S(2)}) collective-permute-start(f32[180,128]{1,0:T(8,128)S(1)} %constant_dynamic-slice_fusion.6), channel_id=1, source_target_pairs={{0,8},{1,9},{2,10},{3,11},{4,12},{5,13},{6,14},{7,15},{8,0},{9,1},... | collective-permute-start | bytes 276488 | tf_op jit(solution)/shard_map/ppermute | solution.py:388
  68.9 5.6 %collective-permute-start.9 = (f32[12,128]{1,0:T(8,128)S(1)}, f32[12,128]{1,0:T(8,128)S(1)}, u32[]{:S(2)}, u32[]{:S(2)}) collective-permute-start(f32[12,128]{1,0:T(8,128)S(1)} %constant_dynamic-slice_fusion), channel_id=1, source_target_pairs={{0,16},{1,17},{2,18},{3,19},{4,20},{5,21},{6,22},{7,23},{8,24},{9,... | collective-permute-start | bytes 18440 | tf_op jit(solution)/shard_map/ppermute | solution.py:388
  72.6 5.1 %collective-permute-start.4 = (f32[90,128]{1,0:T(8,128)S(1)}, f32[90,128]{1,0:T(8,128)S(1)}, u32[]{:S(2)}, u32[]{:S(2)}) collective-permute-start(f32[90,128]{1,0:T(8,128)S(1)} %constant_dynamic-slice_fusion.5), channel_id=1, source_target_pairs={{0,16},{1,17},{2,18},{3,19},{4,20},{5,21},{6,22},{7,23},{8,24},{9,... | collective-permute-start | bytes 138248 | tf_op jit(solution)/shard_map/ppermute | solution.py:388

commit v2 on v1

--- a/solution.py
+++ b/solution.py
@@ -13,6 +13,7 @@
 LANES = 128
 PAIRS = tuple((m, n) for m in range(4) for n in range(m, 4))
 ROWS = 5
+UNROLL = 4
 VMEM_LIMIT = 48 * 1024 * 1024
 
 smoothing = 16.0
@@ -71,6 +72,17 @@
     return high, low
 
 
+def over_groups(cells, groups, body, unroll):
+    def cell_body(cell, carry):
+        def group_body(index, inner):
+            body(cell, index)
+            return inner
+
+        return lax.fori_loop(0, groups, group_body, carry, unroll=unroll)
+
+    lax.fori_loop(0, cells, cell_body, 0)
+
+
 def pair_rows(value):
     return jnp.broadcast_to(value, (KB, LANES))
 
@@ -90,14 +102,12 @@
     transits, stars = phase_ref.shape
     cells = stars // LANES
     knots = lax.broadcasted_iota(jnp.int32, (KB, LANES), 0)
-    left_half = lax.broadcasted_iota(jnp.int32, (8, LANES), 1) < 64
     total[...] = jnp.zeros_like(total)
     weights[...] = jnp.zeros_like(weights)
     groups = transits // 8
 
-    def group(index, carry):
-        cell = index // groups
-        first = pl.multiple_of((index % groups) * 8, 8)
+    def group(cell, index):
+        first = pl.multiple_of(index * 8, 8)
         rows = pl.ds(first, 8)
         columns = pl.ds(pl.multiple_of(cell * LANES, LANES), LANES)
         number = first + lax.broadcasted_iota(jnp.int32, (8, LANES), 0)
@@ -129,19 +139,17 @@
             right = jnp.concatenate([weight_high, jnp.zeros_like(weight_low)], axis=0)
             result = product(
                 jnp.concatenate([left, right], axis=1),
-                jnp.concatenate(highs + highs, axis=0),
-                jnp.concatenate(lows + lows, axis=0),
+                jnp.concatenate(highs, axis=0),
+                jnp.concatenate(lows, axis=0),
             )
-            band = jnp.where(
-                left_half, result[0:8] + result[16:24], result[8:16] + result[24:32]
+            band = jnp.concatenate(
+                [result[0:8] + result[16:24], result[8:16] + result[24:32]], axis=1
             )
-            transit = cell * transits + first + j
-            for place in (home[transit], halo[transit]):
+            for place in (home[cell, first + j], halo[cell, first + j]):
                 block = pl.ds(pl.multiple_of(place * 8, 8), 8)
                 total[block, :] = total[block, :] + band
-        return carry
-
-    lax.fori_loop(0, cells * groups, group, 0)
+
+    over_groups(cells, groups, group, UNROLL)
 
     def pack(index, carry):
         source = pl.multiple_of(index * 64, 64)
@@ -158,7 +166,8 @@
     counts,
     home,
     halo,
-    ids,
+    owners,
+    slots,
     attitude_ref,
     phase_ref,
     offset_ref,
@@ -184,6 +193,7 @@
     total[...] = jnp.zeros_like(total)
     weights[...] = jnp.zeros_like(weights)
     sums[...] = jnp.zeros_like(sums)
+    sublane = lax.broadcasted_iota(jnp.int32, (8, LANES), 0)
     entries = [(row, column) for row in range(5) for column in range(row + 1)]
 
     def predict_cell(cell, carry):
@@ -192,20 +202,24 @@
         def predict(index, accumulated):
             first = pl.multiple_of(index * 8, 8)
             rows = pl.ds(first, 8)
+            shift = jnp.zeros((8, LANES), jnp.int32)
             for j in range(8):
-                block = ids[cell * transits + first + j]
-                row = attitude_ref[pl.ds(block // 2, 1), :]
-                table[pl.ds(j, 1), :] = pltpu.roll(row, (block % 2) * 64, axis=1)
-            looked = table[...]
+                owner = owners[cell, first + j]
+                slot = slots[cell, first + j]
+                column = pl.multiple_of((slot >> 3) * LANES, LANES)
+                table[index, pl.ds(j, 4, stride=8), :] = attitude_ref[owner, :, pl.ds(column, LANES)]
+                shift = jnp.where(sublane == j, (slot & 7) * KB, shift)
             number = first + lax.broadcasted_iota(jnp.int32, (8, LANES), 0)
             live = jnp.where(number < counts[cell], 1.0, 0.0)
             values = spline_basis(phase_ref[rows, columns])
-            offset = offset_ref[rows, columns]
+            offset = offset_ref[rows, columns] + shift
+            places = [offset + order for order in range(4)]
             predicted = jnp.zeros((8, LANES), jnp.float32)
             for m in range(4):
                 spline = jnp.zeros((8, LANES), jnp.float32)
+                looked = table[index, m * 8 : m * 8 + 8, :]
                 for order in range(4):
-                    found = jnp.take_along_axis(looked, offset + (m * KB + order), axis=1)
+                    found = jnp.take_along_axis(looked, places[order], axis=1)
                     spline = spline + found * values[order]
                 predicted = predicted + spline * axis_ref[m, rows, columns]
             first_value = live * (observed_ref[rows, columns] - predicted)
@@ -217,7 +231,7 @@
             return tuple(old + new for old, new in zip(accumulated, added))
 
         start = tuple(jnp.zeros((8, LANES), jnp.float32) for entry in range(20))
-        accumulated = lax.fori_loop(0, groups, predict, start)
+        accumulated = lax.fori_loop(0, groups, predict, start, unroll=8)
         for entry in range(20):
             sums[entry, pl.ds(cell, 1), :] = jnp.sum(accumulated[entry], axis=0, keepdims=True)
         return carry
@@ -236,9 +250,8 @@
                 cell : cell + 1
             ]
 
-    def group(index, carry):
-        cell = index // groups
-        first = pl.multiple_of((index % groups) * 8, 8)
+    def group(cell, index):
+        first = pl.multiple_of(index * 8, 8)
         rows = pl.ds(first, 8)
         columns = pl.ds(pl.multiple_of(cell * LANES, LANES), LANES)
         number = first + lax.broadcasted_iota(jnp.int32, (8, LANES), 0)
@@ -268,20 +281,16 @@
             right = jnp.where(knots < 4, weight, 0.0)
             result = product(
                 jnp.concatenate([weight, right], axis=1).astype(jnp.bfloat16),
-                jnp.concatenate([high] * 8, axis=0),
-                jnp.concatenate([low] * 8, axis=0),
+                jnp.concatenate([high] * 4, axis=0),
+                jnp.concatenate([low] * 4, axis=0),
             )[0:8]
-            transit = cell * transits + first + j
-            for place in (home[transit], halo[transit]):
-                owner = place // spread
-                slot = place % spread
-                chosen = jnp.where(lanes_block == slot % 8, result, 0.0)
-                tile = owner * ((spread + 7) // 8) + slot // 8
-                block = pl.ds(pl.multiple_of(tile * 8, 8), 8)
+            result = jnp.concatenate([result, result], axis=1)
+            for place in (home[cell, first + j], halo[cell, first + j]):
+                chosen = jnp.where(lanes_block == (place & 7), result, 0.0)
+                block = pl.ds(pl.multiple_of((place >> 3) * 8, 8), 8)
                 total[block, :] = total[block, :] + chosen
-        return carry
-
-    lax.fori_loop(0, cells * groups, group, 0)
+
+    over_groups(cells, groups, group, UNROLL)
 
     def pack(index, carry):
         source = pl.multiple_of(index * 16, 16)
@@ -295,7 +304,7 @@
     lax.fori_loop(0, out_ref.shape[0] // 8, pack, 0)
 
 
-def sweep_kernel(spread, ends, band_ref, gradient_ref, out_ref, band):
+def sweep_kernel(spread, axes, band_ref, gradient_ref, out_ref, band):
     width = band.shape[2]
     tiles = width // LANES
     lane_block = lax.broadcasted_iota(jnp.int32, (8, LANES), 1) // KB
@@ -342,7 +351,10 @@
         [gradient_ref[tile * 4 : (tile + 1) * 4, :] for tile in range(tiles)], axis=1
     )
     lane = lax.broadcasted_iota(jnp.int32, (4, width), 1)
-    keep = jnp.where((lane >= ends[0]) & (lane < ends[1]), relaxation, 0.0)
+    me = lax.axis_index(axes)
+    start = jnp.where(me == 0, KB, 0)
+    stop = jnp.where(me == lax.axis_size(axes) - 1, (spread - 1) * KB, spread * KB)
+    keep = jnp.where((lane >= start) & (lane < stop), relaxation, 0.0)
     answer = jnp.zeros((4, width), jnp.float32)
     for sweep in range(ITERS):
         misfit = gradient
@@ -373,19 +385,106 @@
     return [pl.BlockSpec(memory_space=pltpu.SMEM) for operand in range(count)]
 
 
+def work(microseconds):
+    return pl.CostEstimate(flops=0, bytes_accessed=microseconds * 3_600_000, transcendentals=0)
+
+
 def params():
     return pltpu.CompilerParams(vmem_limit_bytes=VMEM_LIMIT)
 
 
-def halving_sum(parts, axes, devices):
+def call_normals(counts, home, halo, phase, knot_offset, partials, devices, spread):
+    f32 = jnp.float32
+    return pl.pallas_call(
+        functools.partial(normal_kernel, spread),
+        out_shape=jax.ShapeDtypeStruct((devices * spread * ROWS, LANES), f32),
+        in_specs=in_smem(3) + in_vmem(3),
+        out_specs=in_vmem(1)[0],
+        scratch_shapes=[
+            pltpu.VMEM(((devices * spread + 1) * 8, LANES), f32),
+            pltpu.VMEM((8 * 16, LANES), f32),
+            pltpu.VMEM((16, 8, LANES), f32),
+            pltpu.VMEM((8, LANES), jnp.int32),
+        ],
+        compiler_params=params(),
+        cost_estimate=work(8),
+        name="normals",
+    )(counts, home, halo, phase, knot_offset, partials)
+
+
+def call_stars(
+    counts,
+    home,
+    halo,
+    owners,
+    slots,
+    attitude,
+    phase,
+    knot_offset,
+    partials,
+    star_partials,
+    observed,
+    devices,
+    spread,
+):
+    f32 = jnp.float32
+    tiles = (spread + 7) // 8
+    transits, stars = phase.shape
+    return pl.pallas_call(
+        functools.partial(star_kernel, spread),
+        out_shape=[
+            jax.ShapeDtypeStruct((5, stars), f32),
+            jax.ShapeDtypeStruct((devices * tiles * 4, LANES), f32),
+        ],
+        in_specs=in_smem(5) + in_vmem(6),
+        out_specs=in_vmem(2),
+        scratch_shapes=[
+            pltpu.VMEM(((devices + 1) * tiles * 8, LANES), f32),
+            pltpu.VMEM((transits // 8, 32, LANES), f32),
+            pltpu.VMEM((transits, stars), f32),
+            pltpu.VMEM((20, 8, LANES), f32),
+            pltpu.VMEM((5, 8, LANES), f32),
+            pltpu.VMEM((8 * 16, LANES), f32),
+            pltpu.VMEM((4, 8, LANES), f32),
+            pltpu.VMEM((8, LANES), jnp.int32),
+        ],
+        compiler_params=params(),
+        cost_estimate=work(10),
+        name="stars",
+    )(
+        counts,
+        home,
+        halo,
+        owners,
+        slots,
+        attitude,
+        phase,
+        knot_offset,
+        partials,
+        star_partials,
+        observed,
+    )
+
+
+def exchange_sum(parts, axes, devices):
     me = lax.axis_index(axes)
-    for bit in range(devices.bit_length() - 1):
-        half = parts.shape[0] // 2
-        upper = (me >> bit) & 1
-        kept = lax.dynamic_slice_in_dim(parts, upper * half, half, 0)
-        sent = lax.dynamic_slice_in_dim(parts, (1 - upper) * half, half, 0)
-        pairs = [(i, i ^ (1 << bit)) for i in range(devices)]
-        parts = kept + lax.ppermute(sent, axes, pairs)
+    bits = list(range(devices.bit_length() - 1))
+    groups = [bits[:1]] + [bits[start : start + 2] for start in range(1, len(bits), 2)]
+    for group in groups:
+        members = 1 << len(group)
+        rows = parts.shape[0] // members
+        mine = 0
+        for bit in group:
+            mine = mine * 2 + ((me >> bit) & 1)
+        added = lax.dynamic_slice_in_dim(parts, mine * rows, rows, 0)
+        arrived = []
+        for other in range(1, members):
+            mask = sum(1 << bit for place, bit in enumerate(reversed(group)) if (other >> place) & 1)
+            sent = lax.dynamic_slice_in_dim(parts, (mine ^ other) * rows, rows, 0)
+            arrived.append(lax.ppermute(sent, axes, [(i, i ^ mask) for i in range(devices)]))
+        for part in arrived:
+            added = added + part
+        parts = added
     return parts
 
 
@@ -405,16 +504,13 @@
     levels = devices.bit_length() - 1
     cells = cell_counts.shape[0]
     transits = observed.shape[0]
-    total = cells * transits
-    stars = cells * CS
     blocks = attitude.shape[1] // KB
     spread = blocks + 2
     tiles = (spread + 7) // 8
     width = tiles * LANES
-    me = lax.axis_index(axes)
-
-    owners = interval_owner.reshape(total)
-    slots = block_slot.reshape(total)
+
+    owners = interval_owner.reshape(cells, transits)
+    slots = block_slot
 
     def position(owner):
         reversed_bits = jnp.zeros_like(owner)
@@ -427,83 +523,47 @@
     before = jnp.where(owners > 0, position(jnp.maximum(owners - 1, 0)) + spread - 1, nowhere)
     after = jnp.where(owners < devices - 1, position(jnp.minimum(owners + 1, devices - 1)), nowhere)
     halo = jnp.where(slots == 0, before, jnp.where(slots == blocks - 1, after, nowhere))
-    ids = owners * blocks + slots
-
-    table = attitude.reshape(4, blocks, KB).transpose(1, 0, 2).reshape(blocks // 2, 8 * KB)
+
+    def lane_place(place):
+        return place // spread * (8 * tiles) + place % spread
+
     whole = lax.all_to_all(
-        jnp.broadcast_to(table[None], (devices,) + table.shape),
+        jnp.broadcast_to(attitude[None], (devices,) + attitude.shape),
         axes,
         split_axis=0,
         concat_axis=0,
         tiled=True,
-    ).reshape(devices * blocks // 2, 8 * KB)
-
-    f32 = jnp.float32
-    normals = pl.pallas_call(
-        functools.partial(normal_kernel, spread),
-        out_shape=jax.ShapeDtypeStruct((devices * spread * ROWS, LANES), f32),
-        in_specs=in_smem(3) + in_vmem(3),
-        out_specs=in_vmem(1)[0],
-        scratch_shapes=[
-            pltpu.VMEM(((devices * spread + 1) * 8, LANES), f32),
-            pltpu.VMEM((8 * 16, LANES), f32),
-            pltpu.VMEM((16, 8, LANES), f32),
-            pltpu.VMEM((8, LANES), jnp.int32),
-        ],
-        compiler_params=params(),
-        name="normals",
-    )(cell_counts, home, halo, phase, knot_offset, attitude_partials)
-
-    star_step, gradients = pl.pallas_call(
-        functools.partial(star_kernel, spread),
-        out_shape=[
-            jax.ShapeDtypeStruct((5, stars), f32),
-            jax.ShapeDtypeStruct((devices * tiles * 4, LANES), f32),
-        ],
-        in_specs=in_smem(4) + in_vmem(6),
-        out_specs=in_vmem(2),
-        scratch_shapes=[
-            pltpu.VMEM(((devices + 1) * tiles * 8, LANES), f32),
-            pltpu.VMEM((8, LANES), f32),
-            pltpu.VMEM((transits, stars), f32),
-            pltpu.VMEM((20, 8, LANES), f32),
-            pltpu.VMEM((5, 8, LANES), f32),
-            pltpu.VMEM((8 * 16, LANES), f32),
-            pltpu.VMEM((4, 8, LANES), f32),
-            pltpu.VMEM((8, LANES), jnp.int32),
-        ],
-        compiler_params=params(),
-        name="stars",
-    )(
+    )
+    normals = call_normals(
+        cell_counts, home, halo, phase, knot_offset, attitude_partials, devices, spread
+    )
+    star_step, gradients = call_stars(
         cell_counts,
-        home,
-        halo,
-        ids,
+        lane_place(home),
+        lane_place(halo),
+        owners,
+        slots,
         whole,
         phase,
         knot_offset,
         attitude_partials,
         star_partials,
         observed,
-    )
-
-    band = halving_sum(normals, axes, devices)
-    gradient = halving_sum(gradients, axes, devices)
-    ends = jnp.stack(
-        [
-            jnp.where(me == 0, KB, 0),
-            jnp.where(me == devices - 1, (spread - 1) * KB, spread * KB),
-        ]
-    ).astype(jnp.int32)
+        devices,
+        spread,
+    )
+
+    band = exchange_sum(normals, axes, devices)
+    gradient = exchange_sum(gradients, axes, devices)
     attitude_step = pl.pallas_call(
-        functools.partial(sweep_kernel, spread),
-        out_shape=jax.ShapeDtypeStruct((4, blocks * KB), f32),
-        in_specs=in_smem(1) + in_vmem(2),
+        functools.partial(sweep_kernel, spread, axes),
+        out_shape=jax.ShapeDtypeStruct((4, blocks * KB), jnp.float32),
+        in_specs=in_vmem(2),
         out_specs=in_vmem(1)[0],
-        scratch_shapes=[pltpu.VMEM((4, 16, width), f32)],
+        scratch_shapes=[pltpu.VMEM((4, 16, width), jnp.float32)],
         compiler_params=params(),
         name="sweeps",
-    )(ends, band, gradient)
+    )(band, gradient)
     return (star_step, attitude_step)
 
 

time: 80.3 us -> 57.6 us (0.72)
  Pallas kernels: 32.1 us -> 15.9 us
  waiting for transfers between devices: 18.3 us -> 7.91 us
  starting transfers between devices: 21.3 us -> 24.6 us
  other arithmetic: 1.04 us -> 2.02 us
    pallas_call x3, Pallas kernels: 32.1 us -> 15.9 us  [the longest x1 8.1 us: call_stars(): pl.pallas_call(functools.partial(star_kernel, spread), out_shape=[jax.Sha...]
    ppermute x10 -> x14, waiting for transfers between devices: 18.3 us -> 7.9 us  [exchange_sum(): lax.ppermute(sent, axes, [(i, i ^ mask) for i in range(devices)])]
    ppermute x10 -> x14, starting transfers between devices: 14 us -> 17.3 us  [exchange_sum(): lax.ppermute(sent, axes, [(i, i ^ mask) for i in range(devices)])]
    add x11 -> x7, other arithmetic: 0.22 us -> 2.02 us  [the longest x6 1.29 us: exchange_sum(): added = added + part]
    reshape x3 -> x0, local copies, waits for them, and re-layouts: 1.6 us -> none  [the longest x2 0.84 us: per_device(): attitude.reshape(4, blocks, KB).transpose(1, 0, 2)]
    dynamic_slice x10 -> x6, local copies, waits for them, and re-layouts: 0.18 us -> 1.07 us  [exchange_sum(): sent = lax.dynamic_slice_in_dim(parts, (mine ^ other) * rows, rows, 0)]
    unnamed x20 -> x24, local copies, waits for them, and re-layouts: 3.53 us -> 3.54 us
  transfers between devices with their start and end apart: 11 -> 15, of which waited for: 7 -> 4; matrix products, arithmetic and copies ran while one was open for 3% -> 5% of each run, Pallas kernels for 14% -> 25%
where the time goes in v2:
time: 57.6 us; the launch traced here: 57.3 us
  starting transfers between devices  24.6 us (43%)
  Pallas kernels  15.9 us (28%)
  waiting for transfers between devices  7.91 us (14%)
  local copies, waits for them, and re-layouts  5.97 us (10%)
  other arithmetic  2.02 us (4%)
  between operations  0.83 us (1%)
    ppermute x14, starting transfers between devices, exchange_sum(): lax.ppermute(sent, axes, [(i, i ^ mask) for i in range(devices)])  17.3 us
    pallas_call x1, Pallas kernels, call_stars(): pl.pallas_call(functools.partial(star_kernel, spread), out_shape=[jax.Sha...  8.1 us
    ppermute x14, waiting for transfers between devices, exchange_sum(): lax.ppermute(sent, axes, [(i, i ^ mask) for i in range(devices)])  7.9 us
    all_to_all x1, starting transfers between devices, per_device(): lax.all_to_all(jnp.broadcast_to(attitude[None], (devices,) + attitude.sha...  7.3 us
    pallas_call x1, Pallas kernels, call_normals(): pl.pallas_call(functools.partial(normal_kernel, spread), out_shape=jax.Sh...  6.09 us
    unnamed x24, local copies, waits for them, and re-layouts  3.54 us
    pallas_call x1, Pallas kernels, per_device(): pl.pallas_call(functools.partial(sweep_kernel, spread, axes), out_shape=j...  1.73 us
    broadcast_in_dim x1, local copies, waits for them, and re-layouts, per_device(): jnp.broadcast_to(attitude[None], (devices,) + attitude.shape)  1.36 us
  transfers between devices with their start and end apart: 15, of which 4 were waited for; matrix products, arithmetic and copies ran while one was open for 5% of the time, Pallas kernels for 25%

profile of v2, /device:TPU:0, one launch (start us, length us, event | category | flops | bytes accessed | tf_op | source)
XLA Modules:
  0.0 57.3 jit_solution(5190037103256317124)
XLA Ops:
  0.6 1.4 %broadcast_in_dim.13 = f32[32,4,256]{2,1,0:T(4,128)} broadcast(f32[4,256]{1,0:T(4,128)} %param.9), dimensions={1,2} | broadcast | bytes 135168 | tf_op jit(solution)/shard_map/broadcast_in_dim | solution.py:531
  2.0 7.3 %all-to-all-start = ((f32[32,4,256]{2,1,0:T(4,128)}), f32[32,4,256]{2,1,0:T(4,128)S(1)}, u32[]{:S(2)}, u32[]{:S(2)}) async-start(f32[32,4,256]{2,1,0:T(4,128)} %broadcast_in_dim.13), calls=%async_computation | async-start | bytes 262144 | tf_op jit(solution)/shard_map/all_to_all | solution.py:530
  9.3 0.7 %fusion.1 = (s32[4,64]{1,0:T(4,128)S(1)}, s32[4,64]{1,0:T(4,128)S(1)}, s32[4,64]{1,0:T(4,128)S(1)}, s32[4,64]{1,0:T(4,128)S(1)}) fusion(s32[4,64]{1,0:T(4,128)} %bitcast.1, s32[4,64]{1,0:T(4,128)} %slots.1), kind=kLoop, calls=%fused_computation.25 | loop fusion | flops 26368 | bytes 6144 | tf_op jit(solution)/shard_map/add | solution.py:528
  10.0 1.0 %copy-done = f32[4,64,512]{2,1,0:T(8,128)S(1)} copy-done((f32[4,64,512]{2,1,0:T(8,128)S(1)}, f32[4,64,512]{2,1,0:T(8,128)}, u32[]{:S(2)}) %copy-start) | copy-done | bytes 524312
  11.1 0.9 %copy-done.3 = f32[64,512]{1,0:T(8,128)S(1)} copy-done((f32[64,512]{1,0:T(8,128)S(1)}, f32[64,512]{1,0:T(8,128)}, u32[]{:S(2)}) %copy-start.3) | copy-done | bytes 131096
  12.0 0.9 %copy-done.5 = s32[64,512]{1,0:T(8,128)S(1)} copy-done((s32[64,512]{1,0:T(8,128)S(1)}, s32[64,512]{1,0:T(8,128)}, u32[]{:S(2)}) %copy-start.5) | copy-done | bytes 131096
  13.6 6.1 %normals.1 = f32[2880,128]{1,0:T(8,128)S(1)} custom-call(s32[4]{0:T(128)S(1)} %copy-done.10, s32[4,64]{1,0:T(4,128)S(1)} %get-tuple-element.23.home, s32[4,64]{1,0:T(4,128)S(1)} %get-tuple-element.7.halo, f32[64,512]{1,0:T(8,128)S(1)} %copy-done.3, s32[64,512]{1,0:T(8,128)S(1)} %copy-done.5, f32[4,64,512]{2,1,0:T(8,128)S(1)} %copy-done), custom_call_target="tpu_custom_call" | custom-call | bytes 28800000 | tf_op jit(solution)/shard_map/normals/pallas_call | solution.py:398
  19.7 0.9 %constant_dynamic-slice_fusion.13 = f32[1440,128]{1,0:T(8,128)} fusion(f32[2880,128]{1,0:T(8,128)S(1)} %normals.1, s32[]{:T(128)S(6)} %select_n.101), kind=kLoop, calls=%fused_computation.19 | loop fusion | bytes 1474564 | tf_op jit(solution)/shard_map/dynamic_slice | solution.py:483
  21.0 8.1 %stars.1 = (f32[5,512]{1,0:T(8,128)}, f32[384,128]{1,0:T(8,128)S(1)}) custom-call(s32[4]{0:T(128)S(1)} %copy-done.11, s32[4,64]{1,0:T(4,128)S(1)} %get-tuple-element.22.home, s32[4,64]{1,0:T(4,128)S(1)} %get-tuple-element.6.halo, s32[4,64]{1,0:T(4,128)S(1)} %bitcast.2, s32[4,64]{1,0:T(4,128)S(1)} %copy-done.9, f32[32,4,256]{2,1,0:T(4,128)S(1)} %all-to-all-done.attitude_ref, ...), custom_call_target="tpu_custom_call" | custom-call | bytes 36000000 | tf_op jit(solution)/shard_map/stars/pallas_call | solution.py:433
  29.4 1.0 %collective-permute-done.7 = f32[192,128]{1,0:T(8,128)S(1)} collective-permute-done((f32[192,128]{1,0:T(8,128)S(1)}, f32[192,128]{1,0:T(8,128)S(1)}, u32[]{:S(2)}, u32[]{:S(2)}) %collective-permute-start.7) | collective-permute-done | bytes 98336 | tf_op jit(solution)/shard_map/ppermute | solution.py:484
  30.5 1.8 %collective-permute-start.8 = (f32[48,128]{1,0:T(8,128)S(1)}, f32[48,128]{1,0:T(8,128)S(1)}, u32[]{:S(2)}, u32[]{:S(2)}) collective-permute-start(f32[48,128]{1,0:T(8,128)S(1)} %get-tuple-element.16), channel_id=1, source_target_pairs={{0,4},{1,5},{2,6},{3,7},{4,0},{5,1},{6,2},{7,3},{8,12},{9,13},{10,... | collective-permute-start | bytes 73736 | tf_op jit(solution)/shard_map/ppermute | solution.py:484
  32.2 1.4 %collective-permute-start.10 = (f32[48,128]{1,0:T(8,128)S(1)}, f32[48,128]{1,0:T(8,128)S(1)}, u32[]{:S(2)}, u32[]{:S(2)}) collective-permute-start(f32[48,128]{1,0:T(8,128)S(1)} %get-tuple-element.17), channel_id=1, source_target_pairs={{0,6},{1,7},{2,4},{3,5},{4,2},{5,3},{6,0},{7,1},{8,14},{9,15},{10,... | collective-permute-start | bytes 73736 | tf_op jit(solution)/shard_map/ppermute | solution.py:484
  34.0 1.2 %dynamic-slice_add_fusion = f32[1440,128]{1,0:T(8,128)S(1)} fusion(f32[1440,128]{1,0:T(8,128)} %collective-permute-done, f32[2880,128]{1,0:T(8,128)S(1)} %normals.1, s32[]{:T(128)S(6)} %select_n.100), kind=kLoop, calls=%fused_computation | loop fusion | flops 184320 | bytes 2211844 | tf_op jit(solution)/shard_map/add | solution.py:486
  35.3 1.8 %collective-permute-start.1 = (f32[360,128]{1,0:T(8,128)S(1)}, f32[360,128]{1,0:T(8,128)S(1)}, u32[]{:S(2)}, u32[]{:S(2)}) collective-permute-start(f32[360,128]{1,0:T(8,128)S(1)} %get-tuple-element.10), channel_id=1, source_target_pairs={{0,4},{1,5},{2,6},{3,7},{4,0},{5,1},{6,2},{7,3},{8,12},{9,13},{10,... | collective-permute-start | bytes 552968 | tf_op jit(solution)/shard_map/ppermute | solution.py:484
  37.0 1.4 %collective-permute-start.3 = (f32[360,128]{1,0:T(8,128)S(1)}, f32[360,128]{1,0:T(8,128)S(1)}, u32[]{:S(2)}, u32[]{:S(2)}) collective-permute-start(f32[360,128]{1,0:T(8,128)S(1)} %get-tuple-element.11), channel_id=1, source_target_pairs={{0,6},{1,7},{2,4},{3,5},{4,2},{5,3},{6,0},{7,1},{8,14},{9,15},{10,... | collective-permute-start | bytes 552968 | tf_op jit(solution)/shard_map/ppermute | solution.py:484
  38.9 2.6 %collective-permute-start.11 = (f32[12,128]{1,0:T(8,128)S(1)}, f32[12,128]{1,0:T(8,128)S(1)}, u32[]{:S(2)}, u32[]{:S(2)}) collective-permute-start(f32[12,128]{1,0:T(8,128)S(1)} %get-tuple-element.19), channel_id=1, source_target_pairs={{0,16},{1,17},{2,18},{3,19},{4,20},{5,21},{6,22},{7,23},{8,24},{9,... | collective-permute-start | bytes 18440 | tf_op jit(solution)/shard_map/ppermute | solution.py:484
  41.5 1.5 %collective-permute-start.13 = (f32[12,128]{1,0:T(8,128)S(1)}, f32[12,128]{1,0:T(8,128)S(1)}, u32[]{:S(2)}, u32[]{:S(2)}) collective-permute-start(f32[12,128]{1,0:T(8,128)S(1)} %get-tuple-element.20), channel_id=1, source_target_pairs={{0,24},{1,25},{2,26},{3,27},{4,28},{5,29},{6,30},{7,31},{8,16},{9,... | collective-permute-start | bytes 18440 | tf_op jit(solution)/shard_map/ppermute | solution.py:484
  43.0 2.2 %collective-permute-done.1 = f32[360,128]{1,0:T(8,128)S(1)} collective-permute-done((f32[360,128]{1,0:T(8,128)S(1)}, f32[360,128]{1,0:T(8,128)S(1)}, u32[]{:S(2)}, u32[]{:S(2)}) %collective-permute-start.1) | collective-permute-done | bytes 184352 | tf_op jit(solution)/shard_map/ppermute | solution.py:484
  45.2 1.8 %collective-permute-start.12 = (f32[12,128]{1,0:T(8,128)S(1)}, f32[12,128]{1,0:T(8,128)S(1)}, u32[]{:S(2)}, u32[]{:S(2)}) collective-permute-start(f32[12,128]{1,0:T(8,128)S(1)} %get-tuple-element.21), channel_id=1, source_target_pairs={{0,8},{1,9},{2,10},{3,11},{4,12},{5,13},{6,14},{7,15},{8,0},{9,1},... | collective-permute-start | bytes 18440 | tf_op jit(solution)/shard_map/ppermute | solution.py:484
  47.1 2.5 %collective-permute-start.4 = (f32[90,128]{1,0:T(8,128)S(1)}, f32[90,128]{1,0:T(8,128)S(1)}, u32[]{:S(2)}, u32[]{:S(2)}) collective-permute-start(f32[90,128]{1,0:T(8,128)S(1)} %get-tuple-element.13), channel_id=1, source_target_pairs={{0,16},{1,17},{2,18},{3,19},{4,20},{5,21},{6,22},{7,23},{8,24},{9,... | collective-permute-start | bytes 138248 | tf_op jit(solution)/shard_map/ppermute | solution.py:484
  49.6 1.2 %collective-permute-start.6 = (f32[90,128]{1,0:T(8,128)S(1)}, f32[90,128]{1,0:T(8,128)S(1)}, u32[]{:S(2)}, u32[]{:S(2)}) collective-permute-start(f32[90,128]{1,0:T(8,128)S(1)} %get-tuple-element.14), channel_id=1, source_target_pairs={{0,24},{1,25},{2,26},{3,27},{4,28},{5,29},{6,30},{7,31},{8,16},{9,... | collective-permute-start | bytes 138248 | tf_op jit(solution)/shard_map/ppermute | solution.py:484
  50.9 2.3 %collective-permute-done.4 = f32[90,128]{1,0:T(8,128)S(1)} collective-permute-done((f32[90,128]{1,0:T(8,128)S(1)}, f32[90,128]{1,0:T(8,128)S(1)}, u32[]{:S(2)}, u32[]{:S(2)}) %collective-permute-start.4) | collective-permute-done | bytes 46112 | tf_op jit(solution)/shard_map/ppermute | solution.py:484
  53.2 2.3 %collective-permute-done.6 = f32[90,128]{1,0:T(8,128)S(1)} collective-permute-done((f32[90,128]{1,0:T(8,128)S(1)}, f32[90,128]{1,0:T(8,128)S(1)}, u32[]{:S(2)}, u32[]{:S(2)}) %collective-permute-start.6) | collective-permute-done | bytes 46112 | tf_op jit(solution)/shard_map/ppermute | solution.py:484
  55.5 1.7 %sweeps.1 = f32[4,256]{1,0:T(4,128)} custom-call(f32[90,128]{1,0:T(8,128)S(1)} %add_add_fusion.1.band_ref, f32[12,128]{1,0:T(8,128)S(1)} %add_add_fusion.3.gradient_ref), custom_call_target="tpu_custom_call" | custom-call | tf_op jit(solution)/shard_map/sweeps/pallas_call | solution.py:558
  (47 shorter events, 2.3 us)
Async XLA Ops:
  2.0 18.9 %all-to-all-start = ((f32[32,4,256]{2,1,0:T(4,128)}), f32[32,4,256]{2,1,0:T(4,128)S(1)}, u32[]{:S(2)}, u32[]{:S(2)}) async-start(f32[32,4,256]{2,1,0:T(4,128)} %broadcast_in_dim.13), calls=%async_computation | async-start | bytes 262144 | tf_op jit(solution)/shard_map/all_to_all | solution.py:530
  10.0 1.0 %copy-start = (f32[4,64,512]{2,1,0:T(8,128)S(1)}, f32[4,64,512]{2,1,0:T(8,128)}, u32[]{:S(2)}) copy-start(f32[4,64,512]{2,1,0:T(8,128)} %axis_ref.3) | copy-start | bytes 1572868
  13.5 7.4 %copy-start.1 = (f32[4,64,512]{2,1,0:T(8,128)S(1)}, f32[4,64,512]{2,1,0:T(8,128)}, u32[]{:S(2)}) copy-start(f32[4,64,512]{2,1,0:T(8,128)} %axis_ref.3) | copy-start | bytes 1572868
  13.5 7.4 %copy-start.2 = (f32[5,64,512]{2,1,0:T(8,128)S(1)}, f32[5,64,512]{2,1,0:T(8,128)}, u32[]{:S(2)}) copy-start(f32[5,64,512]{2,1,0:T(8,128)} %star_ref.1) | copy-start | bytes 1966084
  13.6 7.4 %copy-start.4 = (f32[64,512]{1,0:T(8,128)S(1)}, f32[64,512]{1,0:T(8,128)}, u32[]{:S(2)}) copy-start(f32[64,512]{1,0:T(8,128)} %phase_ref.3) | copy-start | bytes 393220
  13.6 7.4 %copy-start.6 = (s32[64,512]{1,0:T(8,128)S(1)}, s32[64,512]{1,0:T(8,128)}, u32[]{:S(2)}) copy-start(s32[64,512]{1,0:T(8,128)} %offset_ref.3) | copy-start | bytes 393220
  13.6 7.4 %copy-start.7 = (f32[64,512]{1,0:T(8,128)S(1)}, f32[64,512]{1,0:T(8,128)}, u32[]{:S(2)}) copy-start(f32[64,512]{1,0:T(8,128)} %observed_ref.1) | copy-start | bytes 393220
  13.6 7.4 %copy-start.8 = (s32[4,64,1]{1,2,0:T(1,128)S(1)}, s32[4,64,1]{1,2,0:T(1,128)}, u32[]{:S(2)}) copy-start(s32[4,64,1]{1,2,0:T(1,128)} %param.16) | copy-start | bytes 3076
  13.6 7.4 %copy-start.9 = (s32[4,64]{1,0:T(4,128)S(1)}, s32[4,64]{1,0:T(4,128)}, u32[]{:S(2)}) copy-start(s32[4,64]{1,0:T(4,128)} %slots.1) | copy-start | bytes 3076
  13.6 7.4 %copy-start.11 = (s32[4]{0:T(128)S(1)}, s32[4]{0:T(128)}, u32[]{:S(2)}) copy-start(s32[4]{0:T(128)} %counts.3) | copy-start | bytes 52
  20.6 13.4 %collective-permute-start = (f32[1440,128]{1,0:T(8,128)}, f32[1440,128]{1,0:T(8,128)}, u32[]{:S(2)}, u32[]{:S(2)}) collective-permute-start(f32[1440,128]{1,0:T(8,128)} %constant_dynamic-slice_fusion.13), channel_id=1, source_target_pairs={{0,1},{1,0},{2,3},{3,2},{4,5},{5,4},{6,7},{7,6},{8,9},{9,8},{10,11... | collective-permute-start | bytes 2211848 | tf_op jit(solution)/shard_map/ppermute | solution.py:484
  29.1 1.4 %collective-permute-start.7 = (f32[192,128]{1,0:T(8,128)S(1)}, f32[192,128]{1,0:T(8,128)S(1)}, u32[]{:S(2)}, u32[]{:S(2)}) collective-permute-start(f32[192,128]{1,0:T(8,128)S(1)} %constant_dynamic-slice_fusion.6), channel_id=1, source_target_pairs={{0,1},{1,0},{2,3},{3,2},{4,5},{5,4},{6,7},{7,6},{8,9},{9,8},{10,11... | collective-permute-start | bytes 294920 | tf_op jit(solution)/shard_map/ppermute | solution.py:484
  30.5 8.0 %collective-permute-start.8 = (f32[48,128]{1,0:T(8,128)S(1)}, f32[48,128]{1,0:T(8,128)S(1)}, u32[]{:S(2)}, u32[]{:S(2)}) collective-permute-start(f32[48,128]{1,0:T(8,128)S(1)} %get-tuple-element.16), channel_id=1, source_target_pairs={{0,4},{1,5},{2,6},{3,7},{4,0},{5,1},{6,2},{7,3},{8,12},{9,13},{10,... | collective-permute-start | bytes 73736 | tf_op jit(solution)/shard_map/ppermute | solution.py:484
  32.2 6.6 %collective-permute-start.10 = (f32[48,128]{1,0:T(8,128)S(1)}, f32[48,128]{1,0:T(8,128)S(1)}, u32[]{:S(2)}, u32[]{:S(2)}) collective-permute-start(f32[48,128]{1,0:T(8,128)S(1)} %get-tuple-element.17), channel_id=1, source_target_pairs={{0,6},{1,7},{2,4},{3,5},{4,2},{5,3},{6,0},{7,1},{8,14},{9,15},{10,... | collective-permute-start | bytes 73736 | tf_op jit(solution)/shard_map/ppermute | solution.py:484
  33.7 5.2 %collective-permute-start.9 = (f32[48,128]{1,0:T(8,128)S(1)}, f32[48,128]{1,0:T(8,128)S(1)}, u32[]{:S(2)}, u32[]{:S(2)}) collective-permute-start(f32[48,128]{1,0:T(8,128)S(1)} %get-tuple-element.18), channel_id=1, source_target_pairs={{0,2},{1,3},{2,0},{3,1},{4,6},{5,7},{6,4},{7,5},{8,10},{9,11},{10,... | collective-permute-start | bytes 73736 | tf_op jit(solution)/shard_map/ppermute | solution.py:484
  35.3 9.9 %collective-permute-start.1 = (f32[360,128]{1,0:T(8,128)S(1)}, f32[360,128]{1,0:T(8,128)S(1)}, u32[]{:S(2)}, u32[]{:S(2)}) collective-permute-start(f32[360,128]{1,0:T(8,128)S(1)} %get-tuple-element.10), channel_id=1, source_target_pairs={{0,4},{1,5},{2,6},{3,7},{4,0},{5,1},{6,2},{7,3},{8,12},{9,13},{10,... | collective-permute-start | bytes 552968 | tf_op jit(solution)/shard_map/ppermute | solution.py:484
  37.0 10.0 %collective-permute-start.3 = (f32[360,128]{1,0:T(8,128)S(1)}, f32[360,128]{1,0:T(8,128)S(1)}, u32[]{:S(2)}, u32[]{:S(2)}) collective-permute-start(f32[360,128]{1,0:T(8,128)S(1)} %get-tuple-element.11), channel_id=1, source_target_pairs={{0,6},{1,7},{2,4},{3,5},{4,2},{5,3},{6,0},{7,1},{8,14},{9,15},{10,... | collective-permute-start | bytes 552968 | tf_op jit(solution)/shard_map/ppermute | solution.py:484
  38.5 8.6 %collective-permute-start.2 = (f32[360,128]{1,0:T(8,128)S(1)}, f32[360,128]{1,0:T(8,128)S(1)}, u32[]{:S(2)}, u32[]{:S(2)}) collective-permute-start(f32[360,128]{1,0:T(8,128)S(1)} %get-tuple-element.12), channel_id=1, source_target_pairs={{0,2},{1,3},{2,0},{3,1},{4,6},{5,7},{6,4},{7,5},{8,10},{9,11},{10,... | collective-permute-start | bytes 552968 | tf_op jit(solution)/shard_map/ppermute | solution.py:484
  38.9 11.9 %collective-permute-start.11 = (f32[12,128]{1,0:T(8,128)S(1)}, f32[12,128]{1,0:T(8,128)S(1)}, u32[]{:S(2)}, u32[]{:S(2)}) collective-permute-start(f32[12,128]{1,0:T(8,128)S(1)} %get-tuple-element.19), channel_id=1, source_target_pairs={{0,16},{1,17},{2,18},{3,19},{4,20},{5,21},{6,22},{7,23},{8,24},{9,... | collective-permute-start | bytes 18440 | tf_op jit(solution)/shard_map/ppermute | solution.py:484
  41.5 9.3 %collective-permute-start.13 = (f32[12,128]{1,0:T(8,128)S(1)}, f32[12,128]{1,0:T(8,128)S(1)}, u32[]{:S(2)}, u32[]{:S(2)}) collective-permute-start(f32[12,128]{1,0:T(8,128)S(1)} %get-tuple-element.20), channel_id=1, source_target_pairs={{0,24},{1,25},{2,26},{3,27},{4,28},{5,29},{6,30},{7,31},{8,16},{9,... | collective-permute-start | bytes 18440 | tf_op jit(solution)/shard_map/ppermute | solution.py:484
  45.2 5.6 %collective-permute-start.12 = (f32[12,128]{1,0:T(8,128)S(1)}, f32[12,128]{1,0:T(8,128)S(1)}, u32[]{:S(2)}, u32[]{:S(2)}) collective-permute-start(f32[12,128]{1,0:T(8,128)S(1)} %get-tuple-element.21), channel_id=1, source_target_pairs={{0,8},{1,9},{2,10},{3,11},{4,12},{5,13},{6,14},{7,15},{8,0},{9,1},... | collective-permute-start | bytes 18440 | tf_op jit(solution)/shard_map/ppermute | solution.py:484
  47.1 6.0 %collective-permute-start.4 = (f32[90,128]{1,0:T(8,128)S(1)}, f32[90,128]{1,0:T(8,128)S(1)}, u32[]{:S(2)}, u32[]{:S(2)}) collective-permute-start(f32[90,128]{1,0:T(8,128)S(1)} %get-tuple-element.13), channel_id=1, source_target_pairs={{0,16},{1,17},{2,18},{3,19},{4,20},{5,21},{6,22},{7,23},{8,24},{9,... | collective-permute-start | bytes 138248 | tf_op jit(solution)/shard_map/ppermute | solution.py:484
  49.6 5.9 %collective-permute-start.6 = (f32[90,128]{1,0:T(8,128)S(1)}, f32[90,128]{1,0:T(8,128)S(1)}, u32[]{:S(2)}, u32[]{:S(2)}) collective-permute-start(f32[90,128]{1,0:T(8,128)S(1)} %get-tuple-element.14), channel_id=1, source_target_pairs={{0,24},{1,25},{2,26},{3,27},{4,28},{5,29},{6,30},{7,31},{8,16},{9,... | collective-permute-start | bytes 138248 | tf_op jit(solution)/shard_map/ppermute | solution.py:484
  50.8 4.7 %collective-permute-start.5 = (f32[90,128]{1,0:T(8,128)S(1)}, f32[90,128]{1,0:T(8,128)S(1)}, u32[]{:S(2)}, u32[]{:S(2)}) collective-permute-start(f32[90,128]{1,0:T(8,128)S(1)} %get-tuple-element.15), channel_id=1, source_target_pairs={{0,8},{1,9},{2,10},{3,11},{4,12},{5,13},{6,14},{7,15},{8,0},{9,1},... | collective-permute-start | bytes 138248 | tf_op jit(solution)/shard_map/ppermute | solution.py:484
  (3 other events, 2.5 us)

commit v3 on v2

--- a/solution.py
+++ b/solution.py
@@ -12,9 +12,9 @@
 ITERS = 6
 LANES = 128
 PAIRS = tuple((m, n) for m in range(4) for n in range(m, 4))
+HOME, HALO, HOME_LANES, HALO_LANES, OWNER, SLOT, COUNT = range(7)
 ROWS = 5
 UNROLL = 4
-VMEM_LIMIT = 48 * 1024 * 1024
 
 smoothing = 16.0
 damping = 2.0
@@ -96,8 +96,58 @@
     )
 
 
+def facts_kernel(blocks, counts, attitude_ref, owners_ref, slots_ref, facts_ref, wide_ref):
+    devices = wide_ref.shape[0]
+    levels = devices.bit_length() - 1
+    spread = blocks + 2
+    lanes = (spread + 7) // 8 * 8
+    owners = owners_ref[...]
+    slots = slots_ref[...]
+    cells = owners.shape[0]
+
+    def reverse(owner):
+        reversed_bits = jnp.zeros_like(owner)
+        for bit in range(levels):
+            reversed_bits = reversed_bits | (((owner >> bit) & 1) << (levels - 1 - bit))
+        return reversed_bits
+
+    first = slots == 0
+    final = slots == blocks - 1
+    neighbour = owners + jnp.where(first, -1, jnp.where(final, 1, 0))
+    nowhere = (neighbour == owners) | (neighbour < 0) | (neighbour >= devices)
+    home_owner = reverse(owners)
+    halo_owner = jnp.where(nowhere, devices, reverse(neighbour))
+    home_place = slots + 1
+    halo_place = jnp.where(first & ~nowhere, spread - 1, 0)
+    facts_ref[HOME] = home_owner * spread + home_place
+    facts_ref[HALO] = halo_owner * spread + halo_place
+    facts_ref[HOME_LANES] = home_owner * lanes + home_place
+    facts_ref[HALO_LANES] = halo_owner * lanes + halo_place
+    facts_ref[OWNER] = owners
+    facts_ref[SLOT] = slots
+    for cell in range(cells):
+        facts_ref[COUNT, cell : cell + 1, :] = jnp.full((1, owners.shape[1]), counts[cell], jnp.int32)
+    attitude = attitude_ref[...]
+
+    def copy(index, carry):
+        wide_ref[index] = attitude
+        return carry
+
+    lax.fori_loop(0, devices, copy, 0, unroll=8)
+
+
 def normal_kernel(
-    spread, counts, home, halo, phase_ref, offset_ref, axis_ref, out_ref, total, weights, basis, offsets
+    axes,
+    facts,
+    phase_ref,
+    offset_ref,
+    axis_ref,
+    kept_ref,
+    sent_ref,
+    total,
+    weights,
+    basis,
+    offsets,
 ):
     transits, stars = phase_ref.shape
     cells = stars // LANES
@@ -111,7 +161,7 @@
         rows = pl.ds(first, 8)
         columns = pl.ds(pl.multiple_of(cell * LANES, LANES), LANES)
         number = first + lax.broadcasted_iota(jnp.int32, (8, LANES), 0)
-        live = jnp.where(number < counts[cell], 1.0, 0.0)
+        live = jnp.where(number < facts[COUNT, cell, 0], 1.0, 0.0)
         values = spline_basis(phase_ref[rows, columns])
         for shift in range(4):
             for order in range(4 - shift):
@@ -145,37 +195,74 @@
             band = jnp.concatenate(
                 [result[0:8] + result[16:24], result[8:16] + result[24:32]], axis=1
             )
-            for place in (home[cell, first + j], halo[cell, first + j]):
+            for place in (facts[HOME, cell, first + j], facts[HALO, cell, first + j]):
                 block = pl.ds(pl.multiple_of(place * 8, 8), 8)
                 total[block, :] = total[block, :] + band
 
     over_groups(cells, groups, group, UNROLL)
 
+    mine = lax.axis_index(axes) & 1
+    half = kept_ref.shape[0] // ROWS * 8
+
     def pack(index, carry):
-        source = pl.multiple_of(index * 64, 64)
         target = pl.multiple_of(index * 8 * ROWS, 8)
-        for j in range(8):
-            out_ref[pl.ds(target + j * ROWS, ROWS), :] = total[pl.ds(source + j * 8, ROWS), :]
+        for out_ref, part in ((kept_ref, mine), (sent_ref, 1 - mine)):
+            source = pl.multiple_of(part * half + index * 64, 64)
+            for j in range(8):
+                out_ref[pl.ds(target + j * ROWS, ROWS), :] = total[pl.ds(source + j * 8, ROWS), :]
         return carry
 
-    lax.fori_loop(0, out_ref.shape[0] // (8 * ROWS), pack, 0)
+    lax.fori_loop(0, half // 64, pack, 0)
+
+
+ENTRIES = tuple((row, column) for row in range(5) for column in range(row + 1))
+
+
+def factor_kernel(facts, star_ref, factors_ref, sums):
+    transits, stars = star_ref.shape[1:]
+    sums[...] = jnp.zeros_like(sums)
+
+    def cell_body(cell, carry):
+        columns = pl.ds(pl.multiple_of(cell * LANES, LANES), LANES)
+
+        def add(index, accumulated):
+            first = pl.multiple_of(index * 8, 8)
+            number = first + lax.broadcasted_iota(jnp.int32, (8, LANES), 0)
+            live = jnp.where(number < facts[COUNT, cell, 0], 1.0, 0.0)
+            parts = [star_ref[row, pl.ds(first, 8), columns] for row in range(5)]
+            lively = [part * live for part in parts]
+            return tuple(
+                old + lively[row] * parts[column] for old, (row, column) in zip(accumulated, ENTRIES)
+            )
+
+        start = tuple(jnp.zeros((8, LANES), jnp.float32) for entry in ENTRIES)
+        accumulated = lax.fori_loop(0, transits // 8, add, start, unroll=4)
+        for entry in range(len(ENTRIES)):
+            sums[entry, pl.ds(cell, 1), :] = jnp.sum(accumulated[entry], axis=0, keepdims=True)
+        return carry
+
+    lax.fori_loop(0, stars // LANES, cell_body, 0)
+    normal = [[None for column in range(5)] for row in range(5)]
+    for entry, (row, column) in enumerate(ENTRIES):
+        normal[row][column] = sums[entry] + (star_prior if row == column else 0.0)
+    lower, inverse = cholesky_factor(normal, 5)
+    for entry, (row, column) in enumerate(ENTRIES):
+        factors_ref[entry] = inverse[row] if row == column else lower[row][column]
 
 
 def star_kernel(
-    spread,
-    counts,
-    home,
-    halo,
-    owners,
-    slots,
+    axes,
+    facts,
     attitude_ref,
+    factors_ref,
     phase_ref,
     offset_ref,
     axis_ref,
     star_ref,
     observed_ref,
     step_ref,
-    out_ref,
+    kept_ref,
+    sent_ref,
     total,
     table,
     first_order,
@@ -194,7 +281,6 @@
     weights[...] = jnp.zeros_like(weights)
     sums[...] = jnp.zeros_like(sums)
     sublane = lax.broadcasted_iota(jnp.int32, (8, LANES), 0)
-    entries = [(row, column) for row in range(5) for column in range(row + 1)]
 
     def predict_cell(cell, carry):
         columns = pl.ds(pl.multiple_of(cell * LANES, LANES), LANES)
@@ -204,13 +290,13 @@
             rows = pl.ds(first, 8)
             shift = jnp.zeros((8, LANES), jnp.int32)
             for j in range(8):
-                owner = owners[cell, first + j]
-                slot = slots[cell, first + j]
+                owner = facts[OWNER, cell, first + j]
+                slot = facts[SLOT, cell, first + j]
                 column = pl.multiple_of((slot >> 3) * LANES, LANES)
                 table[index, pl.ds(j, 4, stride=8), :] = attitude_ref[owner, :, pl.ds(column, LANES)]
                 shift = jnp.where(sublane == j, (slot & 7) * KB, shift)
             number = first + lax.broadcasted_iota(jnp.int32, (8, LANES), 0)
-            live = jnp.where(number < counts[cell], 1.0, 0.0)
+            live = jnp.where(number < facts[COUNT, cell, 0], 1.0, 0.0)
             values = spline_basis(phase_ref[rows, columns])
             offset = offset_ref[rows, columns] + shift
             places = [offset + order for order in range(4)]
@@ -225,24 +311,21 @@
             first_value = live * (observed_ref[rows, columns] - predicted)
             first_order[rows, columns] = first_value
             parts = [star_ref[row, rows, columns] for row in range(5)]
-            lively = [part * live for part in parts]
-            added = [lively[row] * parts[column] for row, column in entries]
-            added += [part * first_value for part in parts]
-            return tuple(old + new for old, new in zip(accumulated, added))
-
-        start = tuple(jnp.zeros((8, LANES), jnp.float32) for entry in range(20))
+            return tuple(old + part * first_value for old, part in zip(accumulated, parts))
+
+        start = tuple(jnp.zeros((8, LANES), jnp.float32) for row in range(5))
         accumulated = lax.fori_loop(0, groups, predict, start, unroll=8)
-        for entry in range(20):
+        for entry in range(5):
             sums[entry, pl.ds(cell, 1), :] = jnp.sum(accumulated[entry], axis=0, keepdims=True)
         return carry
 
     lax.fori_loop(0, cells, predict_cell, 0)
 
-    normal = [[None for column in range(5)] for row in range(5)]
-    for entry, (row, column) in enumerate(entries):
-        normal[row][column] = sums[entry] + (star_prior if row == column else 0.0)
-    lower, inverse = cholesky_factor(normal, 5)
-    answer = cholesky_solve(lower, inverse, [sums[15 + row] for row in range(5)], 5)
+    lower = [[None for column in range(5)] for row in range(5)]
+    for entry, (row, column) in enumerate(ENTRIES):
+        lower[row][column] = factors_ref[entry]
+    inverse = [lower[row][row] for row in range(5)]
+    answer = cholesky_solve(lower, inverse, [sums[row] for row in range(5)], 5)
     for row in range(5):
         steps[row] = answer[row]
         for cell in range(cells):
@@ -255,7 +338,7 @@
         rows = pl.ds(first, 8)
         columns = pl.ds(pl.multiple_of(cell * LANES, LANES), LANES)
         number = first + lax.broadcasted_iota(jnp.int32, (8, LANES), 0)
-        live = jnp.where(number < counts[cell], 1.0, 0.0)
+        live = jnp.where(number < facts[COUNT, cell, 0], 1.0, 0.0)
         fitted = jnp.zeros((8, LANES), jnp.float32)
         for row in range(5):
             step = jnp.broadcast_to(steps[row, pl.ds(cell, 1), :], (8, LANES))
@@ -285,26 +368,70 @@
                 jnp.concatenate([low] * 4, axis=0),
             )[0:8]
             result = jnp.concatenate([result, result], axis=1)
-            for place in (home[cell, first + j], halo[cell, first + j]):
+            for place in (facts[HOME_LANES, cell, first + j], facts[HALO_LANES, cell, first + j]):
                 chosen = jnp.where(lanes_block == (place & 7), result, 0.0)
                 block = pl.ds(pl.multiple_of((place >> 3) * 8, 8), 8)
                 total[block, :] = total[block, :] + chosen
 
     over_groups(cells, groups, group, UNROLL)
 
+    mine = lax.axis_index(axes) & 1
+    half = kept_ref.shape[0] * 2
+
     def pack(index, carry):
-        source = pl.multiple_of(index * 16, 16)
-        first_tile = total[pl.ds(source, 8), :]
-        second_tile = total[pl.ds(source + 8, 8), :]
         target = pl.multiple_of(index * 8, 8)
-        out_ref[pl.ds(target, 4), :] = first_tile[0:4] + first_tile[4:8]
-        out_ref[pl.ds(target + 4, 4), :] = second_tile[0:4] + second_tile[4:8]
+        for out_ref, part in ((kept_ref, mine), (sent_ref, 1 - mine)):
+            source = pl.multiple_of(part * half + index * 16, 16)
+            for j in range(2):
+                tile = total[pl.ds(source + j * 8, 8), :]
+                out_ref[pl.ds(target + j * 4, 4), :] = tile[0:4] + tile[4:8]
         return carry
 
-    lax.fori_loop(0, out_ref.shape[0] // 8, pack, 0)
-
-
-def sweep_kernel(spread, axes, band_ref, gradient_ref, out_ref, band):
+    lax.fori_loop(0, half // 16, pack, 0)
+
+
+def share_of(axes, group):
+    me = lax.axis_index(axes)
+    mine = 0
+    for bit in group:
+        mine = mine * 2 + ((me >> bit) & 1)
+    return mine
+
+
+def add_kernel(axes, group, families, *refs):
+    mine = share_of(axes, group)
+    members = 1 << len(group)
+    outputs = refs[-members:]
+    first = 0
+    base = 0
+    for count, rows in families:
+        inputs = refs[first : first + count]
+        first += count
+        step = 40 if rows % 40 == 0 else rows
+        for other, out_ref in enumerate(outputs):
+            start = (mine ^ other) * rows
+
+            def add(index, carry, out_ref=out_ref, inputs=inputs, start=start, step=step, base=base):
+                source = pl.ds(start + index * step, step)
+                added = inputs[0][source, :]
+                for ref in inputs[1:]:
+                    added = added + ref[source, :]
+                out_ref[pl.ds(base + index * step, step), :] = added
+                return carry
+
+            if step == rows:
+                add(0, 0)
+            else:
+                lax.fori_loop(0, rows // step, add, 0)
+        base += rows
+
+
+def sweep_kernel(spread, axes, *refs):
+    *parts, out_ref, band_ref, band = refs
+    added = parts[0][...]
+    for part in parts[1:]:
+        added = added + part[...]
+    band_ref[...] = added
     width = band.shape[2]
     tiles = width // LANES
     lane_block = lax.broadcasted_iota(jnp.int32, (8, LANES), 1) // KB
@@ -348,7 +475,11 @@
     ]
     lower, inverse = cholesky_factor(diagonal, 4)
     gradient = jnp.concatenate(
-        [gradient_ref[tile * 4 : (tile + 1) * 4, :] for tile in range(tiles)], axis=1
+        [
+            band_ref[spread * ROWS + tile * 4 : spread * ROWS + (tile + 1) * 4, :]
+            for tile in range(tiles)
+        ],
+        axis=1,
     )
     lane = lax.broadcasted_iota(jnp.int32, (4, width), 1)
     me = lax.axis_index(axes)
@@ -389,36 +520,83 @@
     return pl.CostEstimate(flops=0, bytes_accessed=microseconds * 3_600_000, transcendentals=0)
 
 
-def params():
-    return pltpu.CompilerParams(vmem_limit_bytes=VMEM_LIMIT)
-
-
-def call_normals(counts, home, halo, phase, knot_offset, partials, devices, spread):
+def params(rows=0):
+    return pltpu.CompilerParams(vmem_limit_bytes=min(56 << 20, (16 << 20) + 2 * rows * LANES * 4))
+
+
+def call_facts(counts, attitude, owners, slots, devices):
+    shape = (COUNT + 1,) + owners.shape
+    return pl.pallas_call(
+        functools.partial(facts_kernel, attitude.shape[1] // KB),
+        out_shape=[
+            jax.ShapeDtypeStruct(shape, jnp.int32),
+            jax.ShapeDtypeStruct((devices,) + attitude.shape, jnp.float32),
+        ],
+        in_specs=in_smem(1) + in_vmem(3),
+        out_specs=in_vmem(2),
+        compiler_params=pltpu.CompilerParams(vmem_limit_bytes=62 << 20),
+        cost_estimate=work(1),
+        name="facts",
+    )(counts, attitude, owners, slots)
+
+
+def call_normals(axes, facts, phase, knot_offset, partials, devices, spread):
     f32 = jnp.float32
+    half = jax.ShapeDtypeStruct((devices // 2 * spread * ROWS, LANES), f32)
+    blocks = devices * spread
     return pl.pallas_call(
-        functools.partial(normal_kernel, spread),
-        out_shape=jax.ShapeDtypeStruct((devices * spread * ROWS, LANES), f32),
-        in_specs=in_smem(3) + in_vmem(3),
-        out_specs=in_vmem(1)[0],
+        functools.partial(normal_kernel, axes),
+        out_shape=[half, half],
+        in_specs=in_smem(1) + in_vmem(3),
+        out_specs=in_vmem(2),
         scratch_shapes=[
-            pltpu.VMEM(((devices * spread + 1) * 8, LANES), f32),
+            pltpu.VMEM(((blocks + 1) * 8, LANES), f32),
             pltpu.VMEM((8 * 16, LANES), f32),
             pltpu.VMEM((16, 8, LANES), f32),
             pltpu.VMEM((8, LANES), jnp.int32),
         ],
-        compiler_params=params(),
+        compiler_params=params(blocks * 13),
         cost_estimate=work(8),
         name="normals",
-    )(counts, home, halo, phase, knot_offset, partials)
+    )(facts, phase, knot_offset, partials)
+
+
+def call_add(axes, group, families):
+    members = 1 << len(group)
+    rows = sum(count for arrays, count in families)
+    out = jax.ShapeDtypeStruct((rows, LANES), jnp.float32)
+    arrays = [array for family, count in families for array in family]
+    return pl.pallas_call(
+        functools.partial(
+            add_kernel, axes, group, [(len(family), count) for family, count in families]
+        ),
+        out_shape=[out] * members,
+        in_specs=in_vmem(len(arrays)),
+        out_specs=in_vmem(members),
+        compiler_params=params(rows * members * 3),
+        cost_estimate=work(0),
+        name="shares",
+    )(*arrays)
+
+
+def call_factors(facts, star_partials):
+    return pl.pallas_call(
+        factor_kernel,
+        out_shape=jax.ShapeDtypeStruct((len(ENTRIES), 8, LANES), jnp.float32),
+        in_specs=in_smem(1) + in_vmem(1),
+        out_specs=in_vmem(1)[0],
+        scratch_shapes=[pltpu.VMEM((len(ENTRIES), 8, LANES), jnp.float32)],
+        compiler_params=params(),
+        cost_estimate=work(20),
+        name="factors",
+    )(facts, star_partials)
 
 
 def call_stars(
-    counts,
-    home,
-    halo,
-    owners,
-    slots,
+    axes,
+    facts,
     attitude,
+    factors,
     phase,
     knot_offset,
     partials,
@@ -430,34 +608,33 @@
     f32 = jnp.float32
     tiles = (spread + 7) // 8
     transits, stars = phase.shape
+    half = jax.ShapeDtypeStruct((devices // 2 * tiles * 4, LANES), f32)
     return pl.pallas_call(
-        functools.partial(star_kernel, spread),
+        functools.partial(star_kernel, axes),
         out_shape=[
             jax.ShapeDtypeStruct((5, stars), f32),
-            jax.ShapeDtypeStruct((devices * tiles * 4, LANES), f32),
+            half,
+            half,
         ],
-        in_specs=in_smem(5) + in_vmem(6),
-        out_specs=in_vmem(2),
+        in_specs=in_smem(1) + in_vmem(7),
+        out_specs=in_vmem(3),
         scratch_shapes=[
             pltpu.VMEM(((devices + 1) * tiles * 8, LANES), f32),
             pltpu.VMEM((transits // 8, 32, LANES), f32),
             pltpu.VMEM((transits, stars), f32),
-            pltpu.VMEM((20, 8, LANES), f32),
+            pltpu.VMEM((5, 8, LANES), f32),
             pltpu.VMEM((5, 8, LANES), f32),
             pltpu.VMEM((8 * 16, LANES), f32),
             pltpu.VMEM((4, 8, LANES), f32),
             pltpu.VMEM((8, LANES), jnp.int32),
         ],
-        compiler_params=params(),
+        compiler_params=params((devices + 1) * tiles * 12),
         cost_estimate=work(10),
         name="stars",
     )(
-        counts,
-        home,
-        halo,
-        owners,
-        slots,
+        facts,
         attitude,
+        factors,
         phase,
         knot_offset,
         partials,
@@ -466,26 +643,12 @@
     )
 
 
-def exchange_sum(parts, axes, devices):
-    me = lax.axis_index(axes)
-    bits = list(range(devices.bit_length() - 1))
-    groups = [bits[:1]] + [bits[start : start + 2] for start in range(1, len(bits), 2)]
-    for group in groups:
-        members = 1 << len(group)
-        rows = parts.shape[0] // members
-        mine = 0
-        for bit in group:
-            mine = mine * 2 + ((me >> bit) & 1)
-        added = lax.dynamic_slice_in_dim(parts, mine * rows, rows, 0)
-        arrived = []
-        for other in range(1, members):
-            mask = sum(1 << bit for place, bit in enumerate(reversed(group)) if (other >> place) & 1)
-            sent = lax.dynamic_slice_in_dim(parts, (mine ^ other) * rows, rows, 0)
-            arrived.append(lax.ppermute(sent, axes, [(i, i ^ mask) for i in range(devices)]))
-        for part in arrived:
-            added = added + part
-        parts = added
-    return parts
+def swap(arrays, group, axes, devices):
+    arrived = []
+    for other, array in enumerate(arrays, start=1):
+        mask = sum(1 << bit for place, bit in enumerate(reversed(group)) if (other >> place) & 1)
+        arrived.append(lax.ppermute(array, axes, [(i, i ^ mask) for i in range(devices)]))
+    return arrived
 
 
 def per_device(
@@ -510,40 +673,31 @@
     width = tiles * LANES
 
     owners = interval_owner.reshape(cells, transits)
-    slots = block_slot
-
-    def position(owner):
-        reversed_bits = jnp.zeros_like(owner)
-        for bit in range(levels):
-            reversed_bits = reversed_bits | (((owner >> bit) & 1) << (levels - 1 - bit))
-        return reversed_bits * spread
-
-    nowhere = devices * spread
-    home = position(owners) + slots + 1
-    before = jnp.where(owners > 0, position(jnp.maximum(owners - 1, 0)) + spread - 1, nowhere)
-    after = jnp.where(owners < devices - 1, position(jnp.minimum(owners + 1, devices - 1)), nowhere)
-    halo = jnp.where(slots == 0, before, jnp.where(slots == blocks - 1, after, nowhere))
-
-    def lane_place(place):
-        return place // spread * (8 * tiles) + place % spread
-
-    whole = lax.all_to_all(
-        jnp.broadcast_to(attitude[None], (devices,) + attitude.shape),
+    facts, wide = call_facts(cell_counts, attitude, owners, block_slot, devices)
+    whole = lax.all_to_all(wide, axes, split_axis=0, concat_axis=0, tiled=True)
+    bits = list(range(devices.bit_length() - 1))
+    groups = [bits[:1]] + [bits[start : start + 2] for start in range(1, len(bits), 2)]
+    last = len(groups) - 1
+    left = [devices >> (group[-1] + 1) for group in groups]
+    chunks = (spread * ROWS, tiles * 4)
+
+    def advance(arrays, chunk, index):
+        kept, *sent = call_add(axes, groups[index], [(arrays, chunk * left[index])])
+        return [kept] + swap(sent, groups[index], axes, devices)
+
+    factors = call_factors(facts, star_partials)
+    facts, factors = lax.optimization_barrier((facts, factors))
+    kept, sent = call_normals(
+        axes, facts, phase, knot_offset, attitude_partials, devices, spread
+    )
+    kept, sent, whole = lax.optimization_barrier((kept, sent, whole))
+    normals = [kept] + swap([sent], groups[0], axes, devices)
+    *normals, whole = lax.optimization_barrier((*normals, whole))
+    star_step, kept, sent = call_stars(
         axes,
-        split_axis=0,
-        concat_axis=0,
-        tiled=True,
-    )
-    normals = call_normals(
-        cell_counts, home, halo, phase, knot_offset, attitude_partials, devices, spread
-    )
-    star_step, gradients = call_stars(
-        cell_counts,
-        lane_place(home),
-        lane_place(halo),
-        owners,
-        slots,
+        facts,
         whole,
+        factors,
         phase,
         knot_offset,
         attitude_partials,
@@ -552,18 +706,29 @@
         devices,
         spread,
     )
-
-    band = exchange_sum(normals, axes, devices)
-    gradient = exchange_sum(gradients, axes, devices)
+    normals = advance(normals, chunks[0], 1)
+    *normals, kept, sent = lax.optimization_barrier((*normals, kept, sent))
+    for index in range(2, last):
+        normals = advance(normals, chunks[0], index)
+    gradients = [kept] + swap([sent], groups[0], axes, devices)
+    for index in range(1, last):
+        gradients = advance(gradients, chunks[1], index)
+    families = [(normals, chunks[0] * left[last]), (gradients, chunks[1] * left[last])]
+    kept, *sent = call_add(axes, groups[last], families)
+    parts = [kept] + swap(sent, groups[last], axes, devices)
     attitude_step = pl.pallas_call(
         functools.partial(sweep_kernel, spread, axes),
         out_shape=jax.ShapeDtypeStruct((4, blocks * KB), jnp.float32),
-        in_specs=in_vmem(2),
+        in_specs=in_vmem(len(parts)),
         out_specs=in_vmem(1)[0],
-        scratch_shapes=[pltpu.VMEM((4, 16, width), jnp.float32)],
+        scratch_shapes=[
+            pltpu.VMEM(kept.shape, jnp.float32),
+            pltpu.VMEM((4, 16, width), jnp.float32),
+        ],
         compiler_params=params(),
+        cost_estimate=work(2),
         name="sweeps",
-    )(band, gradient)
+    )(*parts)
     return (star_step, attitude_step)
 
 

time: 57.6 us -> 53.6 us (0.931)
  waiting for transfers between devices: 7.91 us -> 13.5 us
  starting transfers between devices: 24.6 us -> 19.2 us
  local copies, waits for them, and re-layouts: 5.97 us -> 1.11 us
  Pallas kernels: 15.9 us -> 18.8 us
  other arithmetic: 2.02 us -> 0 us
    ppermute x14 -> x11, waiting for transfers between devices: 7.9 us -> 13.5 us  [swap(): lax.ppermute(array, axes, [(i, i ^ mask) for i in range(devices)])]
    ppermute x14 -> x11, starting transfers between devices: 17.3 us -> 11.9 us  [swap(): lax.ppermute(array, axes, [(i, i ^ mask) for i in range(devices)])]
    pallas_call x2 -> x7, Pallas kernels: 14.2 us -> 17.1 us  [the longest x1 7.99 us: call_stars(): pl.pallas_call(functools.partial(star_kernel, axes), out_shape=[jax.Shape...]
    unnamed x24 -> x14, local copies, waits for them, and re-layouts: 3.54 us -> 1.11 us
    add x7 -> x0, other arithmetic: 2.02 us -> none  [the longest x6 1.29 us: exchange_sum(): added = added + part]
    broadcast_in_dim x1 -> x0, local copies, waits for them, and re-layouts: 1.36 us -> none  [per_device(): jnp.broadcast_to(attitude[None], (devices,) + attitude.shape)]
    dynamic_slice x6 -> x0, local copies, waits for them, and re-layouts: 1.07 us -> none  [exchange_sum(): sent = lax.dynamic_slice_in_dim(parts, (mine ^ other) * rows, rows, 0)]
  transfers between devices with their start and end apart: 15 -> 12, of which waited for: 4 -> 9; matrix products, arithmetic and copies ran while one was open for 5% -> 0% of each run, Pallas kernels for 25% -> 29%
where the time goes in v3:
time: 53.6 us; the launch traced here: 53.4 us
  starting transfers between devices  19.2 us (36%)
  Pallas kernels  18.8 us (35%)
  waiting for transfers between devices  13.5 us (25%)
  local copies, waits for them, and re-layouts  1.11 us (2%)
  between operations  0.75 us (1%)
    ppermute x11, waiting for transfers between devices, swap(): lax.ppermute(array, axes, [(i, i ^ mask) for i in range(devices)])  13.5 us
    ppermute x11, starting transfers between devices, swap(): lax.ppermute(array, axes, [(i, i ^ mask) for i in range(devices)])  11.9 us
    pallas_call x1, Pallas kernels, call_stars(): pl.pallas_call(functools.partial(star_kernel, axes), out_shape=[jax.Shape...  7.99 us
    all_to_all x1, starting transfers between devices, per_device(): whole = lax.all_to_all(wide, axes, split_axis=0, concat_axis=0, tiled=True)  7.3 us
    pallas_call x1, Pallas kernels, call_normals(): pl.pallas_call(functools.partial(normal_kernel, axes), out_shape=[half, h...  6.18 us
    pallas_call x1, Pallas kernels, per_device(): pl.pallas_call(functools.partial(sweep_kernel, spread, axes), out_shape=j...  1.76 us
    pallas_call x1, Pallas kernels, call_facts(): pl.pallas_call(functools.partial(facts_kernel, attitude.shape[1] // KB),...  1.48 us
    pallas_call x1, Pallas kernels, call_factors(): pl.pallas_call(factor_kernel, out_shape=jax.ShapeDtypeStruct((len(ENTRIES...  1.13 us
  transfers between devices with their start and end apart: 12, of which 9 were waited for; matrix products, arithmetic and copies ran while one was open for 0% of the time, Pallas kernels for 29%

profile of v3, /device:TPU:0, one launch (start us, length us, event | category | flops | bytes accessed | tf_op | source)
XLA Modules:
  0.0 53.4 jit_solution(7805171779240211952)
XLA Ops:
  0.6 1.5 %facts.1 = (s32[7,4,64]{2,1,0:T(4,128)}, f32[32,4,256]{2,1,0:T(4,128)}) custom-call(s32[4]{0:T(128)} %counts.1, f32[4,256]{1,0:T(4,128)} %attitude_ref.1, s32[4,64]{1,0:T(4,128)} %bitcast.1, s32[4,64]{1,0:T(4,128)} %slots_ref.1), custom_call_target="tpu_custom_call" | custom-call | bytes 3600000 | tf_op jit(solution)/shard_map/facts/pallas_call | solution.py:529
  2.1 7.3 %all-to-all-start = ((f32[32,4,256]{2,1,0:T(4,128)}), f32[32,4,256]{2,1,0:T(4,128)S(1)}, u32[]{:S(2)}, u32[]{:S(2)}) async-start(f32[32,4,256]{2,1,0:T(4,128)} %get-tuple-element.39), calls=%async_computation | async-start | bytes 262144 | tf_op jit(solution)/shard_map/all_to_all | solution.py:677
  9.4 1.1 %copy-done = f32[5,64,512]{2,1,0:T(8,128)S(1)} copy-done((f32[5,64,512]{2,1,0:T(8,128)S(1)}, f32[5,64,512]{2,1,0:T(8,128)}, u32[]{:S(2)}) %copy-start) | copy-done | bytes 655384
  10.5 1.1 %factors.1.factors_ref = f32[15,8,128]{2,1,0:T(8,128)S(1)} custom-call(s32[7,4,64]{2,1,0:T(4,128)S(1)} %copy-done.6, f32[5,64,512]{2,1,0:T(8,128)S(1)} %copy-done), custom_call_target="tpu_custom_call" | custom-call | bytes 72000000 | tf_op jit(solution)/shard_map/factors/pallas_call | solution.py:583
  11.7 6.2 %normals.1 = (f32[1440,128]{1,0:T(8,128)S(1)}, f32[1440,128]{1,0:T(8,128)S(1)}) custom-call(s32[7,4,64]{2,1,0:T(4,128)S(1)} %copy-done.6, f32[64,512]{1,0:T(8,128)S(1)} %copy-done.3, s32[64,512]{1,0:T(8,128)S(1)} %copy-done.4, f32[4,64,512]{2,1,0:T(8,128)S(1)} %copy-done.2), custom_call_target="tpu_custom_call" | custom-call | bytes 28800000 | tf_op jit(solution)/shard_map/normals/pallas_call | solution.py:547
  18.2 2.0 %collective-permute-done.refs_1_ = f32[1440,128]{1,0:T(8,128)S(1)} collective-permute-done((f32[1440,128]{1,0:T(8,128)S(1)}, f32[1440,128]{1,0:T(8,128)S(1)}, u32[]{:S(2)}, u32[]{:S(2)}) %collective-permute-start) | collective-permute-done | bytes 737312 | tf_op jit(solution)/shard_map/ppermute | solution.py:650
  20.4 1.8 %collective-permute-start.1 = (f32[360,128]{1,0:T(8,128)S(1)}, f32[360,128]{1,0:T(8,128)S(1)}, u32[]{:S(2)}, u32[]{:S(2)}) collective-permute-start(f32[360,128]{1,0:T(8,128)S(1)} %get-tuple-element.49), channel_id=1, source_target_pairs={{0,4},{1,5},{2,6},{3,7},{4,0},{5,1},{6,2},{7,3},{8,12},{9,13},{10,... | collective-permute-start | bytes 552968 | tf_op jit(solution)/shard_map/ppermute | solution.py:650
  22.2 1.5 %collective-permute-start.2 = (f32[360,128]{1,0:T(8,128)S(1)}, f32[360,128]{1,0:T(8,128)S(1)}, u32[]{:S(2)}, u32[]{:S(2)}) collective-permute-start(f32[360,128]{1,0:T(8,128)S(1)} %get-tuple-element.50), channel_id=1, source_target_pairs={{0,2},{1,3},{2,0},{3,1},{4,6},{5,7},{6,4},{7,5},{8,10},{9,11},{10,... | collective-permute-start | bytes 552968 | tf_op jit(solution)/shard_map/ppermute | solution.py:650
  24.0 8.0 %stars.1 = (f32[5,512]{1,0:T(8,128)}, f32[192,128]{1,0:T(8,128)S(1)}, f32[192,128]{1,0:T(8,128)S(1)}) custom-call(s32[7,4,64]{2,1,0:T(4,128)S(1)} %copy-done.6, f32[32,4,256]{2,1,0:T(4,128)S(1)} %all-to-all-done.attitude_ref, f32[15,8,128]{2,1,0:T(8,128)S(1)} %factors.1.factors_ref, f32[64,512]{1,0:T(8,128)S(1)} %copy-done.3, s32[64,512]{1,0:T(8,128)S(1)} %copy-done.4, ...), custom_call_target="tpu_custom_call" | custom-call | bytes 36000000 | tf_op jit(solution)/shard_map/stars/pallas_call | solution.py:612
  32.0 0.4 collective-permute-done.3.refs_3_
  32.4 1.3 %collective-permute-done.4.refs_1_ = f32[192,128]{1,0:T(8,128)S(1)} collective-permute-done((f32[192,128]{1,0:T(8,128)S(1)}, f32[192,128]{1,0:T(8,128)S(1)}, u32[]{:S(2)}, u32[]{:S(2)}) %collective-permute-start.4) | collective-permute-done | bytes 98336 | tf_op jit(solution)/shard_map/ppermute | solution.py:650
  33.7 1.7 %collective-permute-start.5 = (f32[48,128]{1,0:T(8,128)S(1)}, f32[48,128]{1,0:T(8,128)S(1)}, u32[]{:S(2)}, u32[]{:S(2)}) collective-permute-start(f32[48,128]{1,0:T(8,128)S(1)} %get-tuple-element.61), channel_id=1, source_target_pairs={{0,4},{1,5},{2,6},{3,7},{4,0},{5,1},{6,2},{7,3},{8,12},{9,13},{10,... | collective-permute-start | bytes 73736 | tf_op jit(solution)/shard_map/ppermute | solution.py:650
  35.4 1.5 %collective-permute-start.6 = (f32[48,128]{1,0:T(8,128)S(1)}, f32[48,128]{1,0:T(8,128)S(1)}, u32[]{:S(2)}, u32[]{:S(2)}) collective-permute-start(f32[48,128]{1,0:T(8,128)S(1)} %get-tuple-element.62), channel_id=1, source_target_pairs={{0,2},{1,3},{2,0},{3,1},{4,6},{5,7},{6,4},{7,5},{8,10},{9,11},{10,... | collective-permute-start | bytes 73736 | tf_op jit(solution)/shard_map/ppermute | solution.py:650
  36.9 0.4 collective-permute-start.7
  37.3 0.3 collective-permute-done.5.refs_5_
  37.6 1.8 %collective-permute-done.6.refs_6_ = f32[48,128]{1,0:T(8,128)S(1)} collective-permute-done((f32[48,128]{1,0:T(8,128)S(1)}, f32[48,128]{1,0:T(8,128)S(1)}, u32[]{:S(2)}, u32[]{:S(2)}) %collective-permute-start.6) | collective-permute-done | bytes 24608 | tf_op jit(solution)/shard_map/ppermute | solution.py:650
  39.5 2.2 %collective-permute-done.7.refs_7_ = f32[48,128]{1,0:T(8,128)S(1)} collective-permute-done((f32[48,128]{1,0:T(8,128)S(1)}, f32[48,128]{1,0:T(8,128)S(1)}, u32[]{:S(2)}, u32[]{:S(2)}) %collective-permute-start.7) | collective-permute-done | bytes 24608 | tf_op jit(solution)/shard_map/ppermute | solution.py:650
  41.7 2.5 %collective-permute-start.8 = (f32[102,128]{1,0:T(8,128)S(1)}, f32[102,128]{1,0:T(8,128)S(1)}, u32[]{:S(2)}, u32[]{:S(2)}) collective-permute-start(f32[102,128]{1,0:T(8,128)S(1)} %get-tuple-element.65), channel_id=1, source_target_pairs={{0,16},{1,17},{2,18},{3,19},{4,20},{5,21},{6,22},{7,23},{8,24},{9,... | collective-permute-start | bytes 156680 | tf_op jit(solution)/shard_map/ppermute | solution.py:650
  44.2 1.5 %collective-permute-start.9 = (f32[102,128]{1,0:T(8,128)S(1)}, f32[102,128]{1,0:T(8,128)S(1)}, u32[]{:S(2)}, u32[]{:S(2)}) collective-permute-start(f32[102,128]{1,0:T(8,128)S(1)} %get-tuple-element.66), channel_id=1, source_target_pairs={{0,8},{1,9},{2,10},{3,11},{4,12},{5,13},{6,14},{7,15},{8,0},{9,1},... | collective-permute-start | bytes 156680 | tf_op jit(solution)/shard_map/ppermute | solution.py:650
  45.7 0.5 collective-permute-start.10
  46.2 1.1 %collective-permute-done.8.refs_1_ = f32[102,128]{1,0:T(8,128)S(1)} collective-permute-done((f32[102,128]{1,0:T(8,128)S(1)}, f32[102,128]{1,0:T(8,128)S(1)}, u32[]{:S(2)}, u32[]{:S(2)}) %collective-permute-start.8) | collective-permute-done | bytes 52256 | tf_op jit(solution)/shard_map/ppermute | solution.py:650
  47.3 1.4 %collective-permute-done.9.refs_2_ = f32[102,128]{1,0:T(8,128)S(1)} collective-permute-done((f32[102,128]{1,0:T(8,128)S(1)}, f32[102,128]{1,0:T(8,128)S(1)}, u32[]{:S(2)}, u32[]{:S(2)}) %collective-permute-start.9) | collective-permute-done | bytes 52256 | tf_op jit(solution)/shard_map/ppermute | solution.py:650
  48.6 3.0 %collective-permute-done.10.refs_3_ = f32[102,128]{1,0:T(8,128)S(1)} collective-permute-done((f32[102,128]{1,0:T(8,128)S(1)}, f32[102,128]{1,0:T(8,128)S(1)}, u32[]{:S(2)}, u32[]{:S(2)}) %collective-permute-start.10) | collective-permute-done | bytes 52256 | tf_op jit(solution)/shard_map/ppermute | solution.py:650
  51.6 1.8 %sweeps.1 = f32[4,256]{1,0:T(4,128)} custom-call(f32[102,128]{1,0:T(8,128)S(1)} %get-tuple-element.64.refs_0_, f32[102,128]{1,0:T(8,128)S(1)} %collective-permute-done.8.refs_1_, f32[102,128]{1,0:T(8,128)S(1)} %collective-permute-done.9.refs_2_, f32[102,128]{1,0:T(8,128)S(1)} %collective-permute-done.10.refs_3_), custom_call_target="tpu_custom_call" | custom-call | bytes 7200000 | tf_op jit(solution)/shard_map/sweeps/pallas_call | solution.py:719
  (22 shorter events, 0.9 us)
Async XLA Ops:
  2.1 7.3 %copy-start.6 = (s32[7,4,64]{2,1,0:T(4,128)S(1)}, s32[7,4,64]{2,1,0:T(4,128)}, u32[]{:S(2)}) copy-start(s32[7,4,64]{2,1,0:T(4,128)} %get-tuple-element.36.facts) | copy-start | bytes 21508
  2.1 9.5 %copy-start.4 = (s32[64,512]{1,0:T(8,128)S(1)}, s32[64,512]{1,0:T(8,128)}, u32[]{:S(2)}) copy-start(s32[64,512]{1,0:T(8,128)} %offset_ref.3) | copy-start | bytes 393220
  2.1 15.8 %all-to-all-start = ((f32[32,4,256]{2,1,0:T(4,128)}), f32[32,4,256]{2,1,0:T(4,128)S(1)}, u32[]{:S(2)}, u32[]{:S(2)}) async-start(f32[32,4,256]{2,1,0:T(4,128)} %get-tuple-element.39), calls=%async_computation | async-start | bytes 262144 | tf_op jit(solution)/shard_map/all_to_all | solution.py:677
  9.4 1.1 %copy-start = (f32[5,64,512]{2,1,0:T(8,128)S(1)}, f32[5,64,512]{2,1,0:T(8,128)}, u32[]{:S(2)}) copy-start(f32[5,64,512]{2,1,0:T(8,128)} %star_ref.3) | copy-start | bytes 1966084
  10.5 1.2 %copy-start.2 = (f32[4,64,512]{2,1,0:T(8,128)S(1)}, f32[4,64,512]{2,1,0:T(8,128)}, u32[]{:S(2)}) copy-start(f32[4,64,512]{2,1,0:T(8,128)} %axis_ref.3) | copy-start | bytes 1572868
  10.5 1.2 %copy-start.3 = (f32[64,512]{1,0:T(8,128)S(1)}, f32[64,512]{1,0:T(8,128)}, u32[]{:S(2)}) copy-start(f32[64,512]{1,0:T(8,128)} %phase_ref.3) | copy-start | bytes 393220
  17.9 6.1 %copy-start.1 = (f32[5,64,512]{2,1,0:T(8,128)S(1)}, f32[5,64,512]{2,1,0:T(8,128)}, u32[]{:S(2)}) copy-start(f32[5,64,512]{2,1,0:T(8,128)} %star_ref.3) | copy-start | bytes 1966084
  17.9 6.1 %copy-start.5 = (f32[64,512]{1,0:T(8,128)S(1)}, f32[64,512]{1,0:T(8,128)}, u32[]{:S(2)}) copy-start(f32[64,512]{1,0:T(8,128)} %observed_ref.1) | copy-start | bytes 393220
  17.9 2.3 %collective-permute-start = (f32[1440,128]{1,0:T(8,128)S(1)}, f32[1440,128]{1,0:T(8,128)S(1)}, u32[]{:S(2)}, u32[]{:S(2)}) collective-permute-start(f32[1440,128]{1,0:T(8,128)S(1)} %get-tuple-element.41), channel_id=1, source_target_pairs={{0,1},{1,0},{2,3},{3,2},{4,5},{5,4},{6,7},{7,6},{8,9},{9,8},{10,11... | collective-permute-start | bytes 2211848 | tf_op jit(solution)/shard_map/ppermute | solution.py:650
  20.4 11.6 %collective-permute-start.1 = (f32[360,128]{1,0:T(8,128)S(1)}, f32[360,128]{1,0:T(8,128)S(1)}, u32[]{:S(2)}, u32[]{:S(2)}) collective-permute-start(f32[360,128]{1,0:T(8,128)S(1)} %get-tuple-element.49), channel_id=1, source_target_pairs={{0,4},{1,5},{2,6},{3,7},{4,0},{5,1},{6,2},{7,3},{8,12},{9,13},{10,... | collective-permute-start | bytes 552968 | tf_op jit(solution)/shard_map/ppermute | solution.py:650
  22.2 9.7 %collective-permute-start.2 = (f32[360,128]{1,0:T(8,128)S(1)}, f32[360,128]{1,0:T(8,128)S(1)}, u32[]{:S(2)}, u32[]{:S(2)}) collective-permute-start(f32[360,128]{1,0:T(8,128)S(1)} %get-tuple-element.50), channel_id=1, source_target_pairs={{0,2},{1,3},{2,0},{3,1},{4,6},{5,7},{6,4},{7,5},{8,10},{9,11},{10,... | collective-permute-start | bytes 552968 | tf_op jit(solution)/shard_map/ppermute | solution.py:650
  23.7 8.7 %collective-permute-start.3 = (f32[360,128]{1,0:T(8,128)S(1)}, f32[360,128]{1,0:T(8,128)S(1)}, u32[]{:S(2)}, u32[]{:S(2)}) collective-permute-start(f32[360,128]{1,0:T(8,128)S(1)} %get-tuple-element.51), channel_id=1, source_target_pairs={{0,6},{1,7},{2,4},{3,5},{4,2},{5,3},{6,0},{7,1},{8,14},{9,15},{10,... | collective-permute-start | bytes 552968 | tf_op jit(solution)/shard_map/ppermute | solution.py:650
  32.4 1.3 %collective-permute-start.4 = (f32[192,128]{1,0:T(8,128)S(1)}, f32[192,128]{1,0:T(8,128)S(1)}, u32[]{:S(2)}, u32[]{:S(2)}) collective-permute-start(f32[192,128]{1,0:T(8,128)S(1)} %get-tuple-element.59), channel_id=1, source_target_pairs={{0,1},{1,0},{2,3},{3,2},{4,5},{5,4},{6,7},{7,6},{8,9},{9,8},{10,11... | collective-permute-start | bytes 294920 | tf_op jit(solution)/shard_map/ppermute | solution.py:650
  33.7 3.9 %collective-permute-start.5 = (f32[48,128]{1,0:T(8,128)S(1)}, f32[48,128]{1,0:T(8,128)S(1)}, u32[]{:S(2)}, u32[]{:S(2)}) collective-permute-start(f32[48,128]{1,0:T(8,128)S(1)} %get-tuple-element.61), channel_id=1, source_target_pairs={{0,4},{1,5},{2,6},{3,7},{4,0},{5,1},{6,2},{7,3},{8,12},{9,13},{10,... | collective-permute-start | bytes 73736 | tf_op jit(solution)/shard_map/ppermute | solution.py:650
  35.4 4.0 %collective-permute-start.6 = (f32[48,128]{1,0:T(8,128)S(1)}, f32[48,128]{1,0:T(8,128)S(1)}, u32[]{:S(2)}, u32[]{:S(2)}) collective-permute-start(f32[48,128]{1,0:T(8,128)S(1)} %get-tuple-element.62), channel_id=1, source_target_pairs={{0,2},{1,3},{2,0},{3,1},{4,6},{5,7},{6,4},{7,5},{8,10},{9,11},{10,... | collective-permute-start | bytes 73736 | tf_op jit(solution)/shard_map/ppermute | solution.py:650
  36.9 4.7 %collective-permute-start.7 = (f32[48,128]{1,0:T(8,128)S(1)}, f32[48,128]{1,0:T(8,128)S(1)}, u32[]{:S(2)}, u32[]{:S(2)}) collective-permute-start(f32[48,128]{1,0:T(8,128)S(1)} %get-tuple-element.63), channel_id=1, source_target_pairs={{0,6},{1,7},{2,4},{3,5},{4,2},{5,3},{6,0},{7,1},{8,14},{9,15},{10,... | collective-permute-start | bytes 73736 | tf_op jit(solution)/shard_map/ppermute | solution.py:650
  41.7 5.5 %collective-permute-start.8 = (f32[102,128]{1,0:T(8,128)S(1)}, f32[102,128]{1,0:T(8,128)S(1)}, u32[]{:S(2)}, u32[]{:S(2)}) collective-permute-start(f32[102,128]{1,0:T(8,128)S(1)} %get-tuple-element.65), channel_id=1, source_target_pairs={{0,16},{1,17},{2,18},{3,19},{4,20},{5,21},{6,22},{7,23},{8,24},{9,... | collective-permute-start | bytes 156680 | tf_op jit(solution)/shard_map/ppermute | solution.py:650
  44.2 4.5 %collective-permute-start.9 = (f32[102,128]{1,0:T(8,128)S(1)}, f32[102,128]{1,0:T(8,128)S(1)}, u32[]{:S(2)}, u32[]{:S(2)}) collective-permute-start(f32[102,128]{1,0:T(8,128)S(1)} %get-tuple-element.66), channel_id=1, source_target_pairs={{0,8},{1,9},{2,10},{3,11},{4,12},{5,13},{6,14},{7,15},{8,0},{9,1},... | collective-permute-start | bytes 156680 | tf_op jit(solution)/shard_map/ppermute | solution.py:650
  45.7 5.9 %collective-permute-start.10 = (f32[102,128]{1,0:T(8,128)S(1)}, f32[102,128]{1,0:T(8,128)S(1)}, u32[]{:S(2)}, u32[]{:S(2)}) collective-permute-start(f32[102,128]{1,0:T(8,128)S(1)} %get-tuple-element.67), channel_id=1, source_target_pairs={{0,24},{1,25},{2,26},{3,27},{4,28},{5,29},{6,30},{7,31},{8,16},{9,... | collective-permute-start | bytes 156680 | tf_op jit(solution)/shard_map/ppermute | solution.py:650

commit v4 on v3

--- a/solution.py
+++ b/solution.py
@@ -14,7 +14,7 @@
 PAIRS = tuple((m, n) for m in range(4) for n in range(m, 4))
 HOME, HALO, HOME_LANES, HALO_LANES, OWNER, SLOT, COUNT = range(7)
 ROWS = 5
-UNROLL = 4
+UNROLL = 8
 
 smoothing = 16.0
 damping = 2.0
@@ -676,14 +676,20 @@
     facts, wide = call_facts(cell_counts, attitude, owners, block_slot, devices)
     whole = lax.all_to_all(wide, axes, split_axis=0, concat_axis=0, tiled=True)
     bits = list(range(devices.bit_length() - 1))
-    groups = [bits[:1]] + [bits[start : start + 2] for start in range(1, len(bits), 2)]
-    last = len(groups) - 1
-    left = [devices >> (group[-1] + 1) for group in groups]
+    pairs = [bits[start : start + 2] for start in range(3, len(bits), 2)]
+    groups = [bits[:1], bits[1:3]] + pairs
+    band_groups = [bits[:1], bits[1:2], bits[2:3]] + pairs
     chunks = (spread * ROWS, tiles * 4)
 
-    def advance(arrays, chunk, index):
-        kept, *sent = call_add(axes, groups[index], [(arrays, chunk * left[index])])
-        return [kept] + swap(sent, groups[index], axes, devices)
+    def rows(kind, group):
+        return chunks[kind] * (devices >> (group[-1] + 1))
+
+    def share(arrays, kind, group):
+        return call_add(axes, group, [(arrays, rows(kind, group))])
+
+    def advance(arrays, kind, group):
+        kept, *sent = share(arrays, kind, group)
+        return [kept] + swap(sent, group, axes, devices)
 
     factors = call_factors(facts, star_partials)
     facts, factors = lax.optimization_barrier((facts, factors))
@@ -691,8 +697,10 @@
         axes, facts, phase, knot_offset, attitude_partials, devices, spread
     )
     kept, sent, whole = lax.optimization_barrier((kept, sent, whole))
-    normals = [kept] + swap([sent], groups[0], axes, devices)
-    *normals, whole = lax.optimization_barrier((*normals, whole))
+    normals = [kept] + swap([sent], band_groups[0], axes, devices)
+    kept, *sent = share(normals, 0, band_groups[1])
+    facts, whole, kept, *sent = lax.optimization_barrier((facts, whole, kept, *sent))
+    normals = [kept] + swap(sent, band_groups[1], axes, devices)
     star_step, kept, sent = call_stars(
         axes,
         facts,
@@ -706,16 +714,18 @@
         devices,
         spread,
     )
-    normals = advance(normals, chunks[0], 1)
-    *normals, kept, sent = lax.optimization_barrier((*normals, kept, sent))
-    for index in range(2, last):
-        normals = advance(normals, chunks[0], index)
     gradients = [kept] + swap([sent], groups[0], axes, devices)
-    for index in range(1, last):
-        gradients = advance(gradients, chunks[1], index)
-    families = [(normals, chunks[0] * left[last]), (gradients, chunks[1] * left[last])]
-    kept, *sent = call_add(axes, groups[last], families)
-    parts = [kept] + swap(sent, groups[last], axes, devices)
+    count = len(normals)
+    both = lax.optimization_barrier((*normals, *gradients))
+    normals, gradients = both[:count], both[count:]
+    for group in band_groups[2:-1]:
+        normals = advance(normals, 0, group)
+    for group in groups[1:-1]:
+        gradients = advance(gradients, 1, group)
+    final = groups[-1]
+    families = [(normals, rows(0, final)), (gradients, rows(1, final))]
+    kept, *sent = call_add(axes, final, families)
+    parts = [kept] + swap(sent, final, axes, devices)
     attitude_step = pl.pallas_call(
         functools.partial(sweep_kernel, spread, axes),
         out_shape=jax.ShapeDtypeStruct((4, blocks * KB), jnp.float32),

time: 53.6 us -> 51.1 us (0.953)
  Pallas kernels: 18.8 us -> 17.6 us
  starting transfers between devices: 19.2 us -> 18.3 us
    ppermute x11 -> x10, waiting for transfers between devices: 13.5 us -> 12.6 us  [swap(): lax.ppermute(array, axes, [(i, i ^ mask) for i in range(devices)])]
    ppermute x11 -> x10, starting transfers between devices: 11.9 us -> 11 us  [swap(): lax.ppermute(array, axes, [(i, i ^ mask) for i in range(devices)])]
    pallas_call x1, Pallas kernels: 6.18 us -> 5.45 us  [call_normals(): pl.pallas_call(functools.partial(normal_kernel, axes), out_shape=[half, h...]
    pallas_call x1, Pallas kernels: 7.99 us -> 7.41 us  [call_stars(): pl.pallas_call(functools.partial(star_kernel, axes), out_shape=[jax.Shape...]
  transfers between devices with their start and end apart: 12 -> 11, of which waited for: 9 -> 9; matrix products, arithmetic and copies ran while one was open for 0% -> 0% of each run, Pallas kernels for 29% -> 28%
where the time goes in v4:
time: 51.1 us; the launch traced here: 50.8 us
  starting transfers between devices  18.3 us (36%)
  Pallas kernels  17.6 us (34%)
  waiting for transfers between devices  13.1 us (26%)
  local copies, waits for them, and re-layouts  1.1 us (2%)
  between operations  0.73 us (1%)
    ppermute x10, waiting for transfers between devices, swap(): lax.ppermute(array, axes, [(i, i ^ mask) for i in range(devices)])  12.6 us
    ppermute x10, starting transfers between devices, swap(): lax.ppermute(array, axes, [(i, i ^ mask) for i in range(devices)])  11 us
    pallas_call x1, Pallas kernels, call_stars(): pl.pallas_call(functools.partial(star_kernel, axes), out_shape=[jax.Shape...  7.41 us
    all_to_all x1, starting transfers between devices, per_device(): whole = lax.all_to_all(wide, axes, split_axis=0, concat_axis=0, tiled=True)  7.3 us
    pallas_call x1, Pallas kernels, call_normals(): pl.pallas_call(functools.partial(normal_kernel, axes), out_shape=[half, h...  5.45 us
    pallas_call x1, Pallas kernels, per_device(): pl.pallas_call(functools.partial(sweep_kernel, spread, axes), out_shape=j...  1.76 us
    pallas_call x1, Pallas kernels, call_facts(): pl.pallas_call(functools.partial(facts_kernel, attitude.shape[1] // KB),...  1.48 us
    pallas_call x1, Pallas kernels, call_factors(): pl.pallas_call(factor_kernel, out_shape=jax.ShapeDtypeStruct((len(ENTRIES...  1.13 us
  transfers between devices with their start and end apart: 11, of which 9 were waited for; matrix products, arithmetic and copies ran while one was open for 0% of the time, Pallas kernels for 28%

profile of v4, /device:TPU:0, one launch (start us, length us, event | category | flops | bytes accessed | tf_op | source)
XLA Modules:
  0.0 50.8 jit_solution(18327531803431854472)
XLA Ops:
  0.6 1.5 %facts.1 = (s32[7,4,64]{2,1,0:T(4,128)}, f32[32,4,256]{2,1,0:T(4,128)}) custom-call(s32[4]{0:T(128)} %counts.1, f32[4,256]{1,0:T(4,128)} %attitude_ref.1, s32[4,64]{1,0:T(4,128)} %bitcast.1, s32[4,64]{1,0:T(4,128)} %slots_ref.1), custom_call_target="tpu_custom_call" | custom-call | bytes 3600000 | tf_op jit(solution)/shard_map/facts/pallas_call | solution.py:529
  2.1 7.3 %all-to-all-start = ((f32[32,4,256]{2,1,0:T(4,128)}), f32[32,4,256]{2,1,0:T(4,128)S(1)}, u32[]{:S(2)}, u32[]{:S(2)}) async-start(f32[32,4,256]{2,1,0:T(4,128)} %get-tuple-element.38), calls=%async_computation | async-start | bytes 262144 | tf_op jit(solution)/shard_map/all_to_all | solution.py:677
  9.4 1.1 %copy-done = f32[5,64,512]{2,1,0:T(8,128)S(1)} copy-done((f32[5,64,512]{2,1,0:T(8,128)S(1)}, f32[5,64,512]{2,1,0:T(8,128)}, u32[]{:S(2)}) %copy-start) | copy-done | bytes 655384
  10.5 1.1 %factors.1.factors_ref = f32[15,8,128]{2,1,0:T(8,128)S(1)} custom-call(s32[7,4,64]{2,1,0:T(4,128)S(1)} %copy-done.6, f32[5,64,512]{2,1,0:T(8,128)S(1)} %copy-done), custom_call_target="tpu_custom_call" | custom-call | bytes 72000000 | tf_op jit(solution)/shard_map/factors/pallas_call | solution.py:583
  11.7 5.5 %normals.1 = (f32[1440,128]{1,0:T(8,128)S(1)}, f32[1440,128]{1,0:T(8,128)S(1)}) custom-call(s32[7,4,64]{2,1,0:T(4,128)S(1)} %copy-done.6, f32[64,512]{1,0:T(8,128)S(1)} %copy-done.3, s32[64,512]{1,0:T(8,128)S(1)} %copy-done.4, f32[4,64,512]{2,1,0:T(8,128)S(1)} %copy-done.2), custom_call_target="tpu_custom_call" | custom-call | bytes 28800000 | tf_op jit(solution)/shard_map/normals/pallas_call | solution.py:547
  17.1 0.5 all-to-all-done.attitude_ref
  17.9 2.0 %collective-permute-done.refs_1_ = f32[1440,128]{1,0:T(8,128)S(1)} collective-permute-done((f32[1440,128]{1,0:T(8,128)S(1)}, f32[1440,128]{1,0:T(8,128)S(1)}, u32[]{:S(2)}, u32[]{:S(2)}) %collective-permute-start) | collective-permute-done | bytes 737312 | tf_op jit(solution)/shard_map/ppermute | solution.py:650
  20.1 1.4 %collective-permute-start.1 = (f32[720,128]{1,0:T(8,128)S(1)}, f32[720,128]{1,0:T(8,128)S(1)}, u32[]{:S(2)}, u32[]{:S(2)}) collective-permute-start(f32[720,128]{1,0:T(8,128)S(1)} %get-tuple-element.49), channel_id=1, source_target_pairs={{0,2},{1,3},{2,0},{3,1},{4,6},{5,7},{6,4},{7,5},{8,10},{9,11},{10,... | collective-permute-start | bytes 1105928 | tf_op jit(solution)/shard_map/ppermute | solution.py:650
  21.5 7.4 %stars.1 = (f32[5,512]{1,0:T(8,128)}, f32[192,128]{1,0:T(8,128)S(1)}, f32[192,128]{1,0:T(8,128)S(1)}) custom-call(s32[7,4,64]{2,1,0:T(4,128)S(1)} %copy-done.6, f32[32,4,256]{2,1,0:T(4,128)S(1)} %all-to-all-done.attitude_ref, f32[15,8,128]{2,1,0:T(8,128)S(1)} %factors.1.factors_ref, f32[64,512]{1,0:T(8,128)S(1)} %copy-done.3, s32[64,512]{1,0:T(8,128)S(1)} %copy-done.4, ...), custom_call_target="tpu_custom_call" | custom-call | bytes 36000000 | tf_op jit(solution)/shard_map/stars/pallas_call | solution.py:612
  28.9 1.3 %collective-permute-done.2.refs_1_ = f32[192,128]{1,0:T(8,128)S(1)} collective-permute-done((f32[192,128]{1,0:T(8,128)S(1)}, f32[192,128]{1,0:T(8,128)S(1)}, u32[]{:S(2)}, u32[]{:S(2)}) %collective-permute-start.2) | collective-permute-done | bytes 98336 | tf_op jit(solution)/shard_map/ppermute | solution.py:650
  30.2 0.6 %collective-permute-done.1.refs_1_ = f32[720,128]{1,0:T(8,128)S(1)} collective-permute-done((f32[720,128]{1,0:T(8,128)S(1)}, f32[720,128]{1,0:T(8,128)S(1)}, u32[]{:S(2)}, u32[]{:S(2)}) %collective-permute-start.1) | collective-permute-done | bytes 368672 | tf_op jit(solution)/shard_map/ppermute | solution.py:650
  31.0 1.4 %collective-permute-start.3 = (f32[360,128]{1,0:T(8,128)S(1)}, f32[360,128]{1,0:T(8,128)S(1)}, u32[]{:S(2)}, u32[]{:S(2)}) collective-permute-start(f32[360,128]{1,0:T(8,128)S(1)} %get-tuple-element.55), channel_id=1, source_target_pairs={{0,4},{1,5},{2,6},{3,7},{4,0},{5,1},{6,2},{7,3},{8,12},{9,13},{10,... | collective-permute-start | bytes 552968 | tf_op jit(solution)/shard_map/ppermute | solution.py:650
  32.3 0.8 %collective-permute-start.4 = (f32[48,128]{1,0:T(8,128)S(1)}, f32[48,128]{1,0:T(8,128)S(1)}, u32[]{:S(2)}, u32[]{:S(2)}) collective-permute-start(f32[48,128]{1,0:T(8,128)S(1)} %get-tuple-element.59), channel_id=1, source_target_pairs={{0,4},{1,5},{2,6},{3,7},{4,0},{5,1},{6,2},{7,3},{8,12},{9,13},{10,... | collective-permute-start | bytes 73736 | tf_op jit(solution)/shard_map/ppermute | solution.py:650
  33.1 1.3 %collective-permute-start.5 = (f32[48,128]{1,0:T(8,128)S(1)}, f32[48,128]{1,0:T(8,128)S(1)}, u32[]{:S(2)}, u32[]{:S(2)}) collective-permute-start(f32[48,128]{1,0:T(8,128)S(1)} %get-tuple-element.60), channel_id=1, source_target_pairs={{0,2},{1,3},{2,0},{3,1},{4,6},{5,7},{6,4},{7,5},{8,10},{9,11},{10,... | collective-permute-start | bytes 73736 | tf_op jit(solution)/shard_map/ppermute | solution.py:650
  34.4 1.5 %collective-permute-start.6 = (f32[48,128]{1,0:T(8,128)S(1)}, f32[48,128]{1,0:T(8,128)S(1)}, u32[]{:S(2)}, u32[]{:S(2)}) collective-permute-start(f32[48,128]{1,0:T(8,128)S(1)} %get-tuple-element.61), channel_id=1, source_target_pairs={{0,6},{1,7},{2,4},{3,5},{4,2},{5,3},{6,0},{7,1},{8,14},{9,15},{10,... | collective-permute-start | bytes 73736 | tf_op jit(solution)/shard_map/ppermute | solution.py:650
  35.9 2.0 %collective-permute-done.4.refs_3_ = f32[48,128]{1,0:T(8,128)S(1)} collective-permute-done((f32[48,128]{1,0:T(8,128)S(1)}, f32[48,128]{1,0:T(8,128)S(1)}, u32[]{:S(2)}, u32[]{:S(2)}) %collective-permute-start.4) | collective-permute-done | bytes 24608 | tf_op jit(solution)/shard_map/ppermute | solution.py:650
  37.9 1.3 %collective-permute-done.6.refs_5_ = f32[48,128]{1,0:T(8,128)S(1)} collective-permute-done((f32[48,128]{1,0:T(8,128)S(1)}, f32[48,128]{1,0:T(8,128)S(1)}, u32[]{:S(2)}, u32[]{:S(2)}) %collective-permute-start.6) | collective-permute-done | bytes 24608 | tf_op jit(solution)/shard_map/ppermute | solution.py:650
  39.2 2.4 %collective-permute-start.7 = (f32[102,128]{1,0:T(8,128)S(1)}, f32[102,128]{1,0:T(8,128)S(1)}, u32[]{:S(2)}, u32[]{:S(2)}) collective-permute-start(f32[102,128]{1,0:T(8,128)S(1)} %get-tuple-element.63), channel_id=1, source_target_pairs={{0,16},{1,17},{2,18},{3,19},{4,20},{5,21},{6,22},{7,23},{8,24},{9,... | collective-permute-start | bytes 156680 | tf_op jit(solution)/shard_map/ppermute | solution.py:650
  41.6 1.5 %collective-permute-start.8 = (f32[102,128]{1,0:T(8,128)S(1)}, f32[102,128]{1,0:T(8,128)S(1)}, u32[]{:S(2)}, u32[]{:S(2)}) collective-permute-start(f32[102,128]{1,0:T(8,128)S(1)} %get-tuple-element.64), channel_id=1, source_target_pairs={{0,8},{1,9},{2,10},{3,11},{4,12},{5,13},{6,14},{7,15},{8,0},{9,1},... | collective-permute-start | bytes 156680 | tf_op jit(solution)/shard_map/ppermute | solution.py:650
  43.2 0.5 collective-permute-start.9
  43.7 0.6 %collective-permute-done.7.refs_1_ = f32[102,128]{1,0:T(8,128)S(1)} collective-permute-done((f32[102,128]{1,0:T(8,128)S(1)}, f32[102,128]{1,0:T(8,128)S(1)}, u32[]{:S(2)}, u32[]{:S(2)}) %collective-permute-start.7) | collective-permute-done | bytes 52256 | tf_op jit(solution)/shard_map/ppermute | solution.py:650
  44.3 1.6 %collective-permute-done.8.refs_2_ = f32[102,128]{1,0:T(8,128)S(1)} collective-permute-done((f32[102,128]{1,0:T(8,128)S(1)}, f32[102,128]{1,0:T(8,128)S(1)}, u32[]{:S(2)}, u32[]{:S(2)}) %collective-permute-start.8) | collective-permute-done | bytes 52256 | tf_op jit(solution)/shard_map/ppermute | solution.py:650
  45.9 3.2 %collective-permute-done.9.refs_3_ = f32[102,128]{1,0:T(8,128)S(1)} collective-permute-done((f32[102,128]{1,0:T(8,128)S(1)}, f32[102,128]{1,0:T(8,128)S(1)}, u32[]{:S(2)}, u32[]{:S(2)}) %collective-permute-start.9) | collective-permute-done | bytes 52256 | tf_op jit(solution)/shard_map/ppermute | solution.py:650
  49.1 1.8 %sweeps.1 = f32[4,256]{1,0:T(4,128)} custom-call(f32[102,128]{1,0:T(8,128)S(1)} %get-tuple-element.62.refs_0_, f32[102,128]{1,0:T(8,128)S(1)} %collective-permute-done.7.refs_1_, f32[102,128]{1,0:T(8,128)S(1)} %collective-permute-done.8.refs_2_, f32[102,128]{1,0:T(8,128)S(1)} %collective-permute-done.9.refs_3_), custom_call_target="tpu_custom_call" | custom-call | bytes 7200000 | tf_op jit(solution)/shard_map/sweeps/pallas_call | solution.py:729
  (21 shorter events, 0.6 us)
Async XLA Ops:
  2.1 7.3 %copy-start.6 = (s32[7,4,64]{2,1,0:T(4,128)S(1)}, s32[7,4,64]{2,1,0:T(4,128)}, u32[]{:S(2)}) copy-start(s32[7,4,64]{2,1,0:T(4,128)} %get-tuple-element.44.facts) | copy-start | bytes 21508
  2.1 9.5 %copy-start.4 = (s32[64,512]{1,0:T(8,128)S(1)}, s32[64,512]{1,0:T(8,128)}, u32[]{:S(2)}) copy-start(s32[64,512]{1,0:T(8,128)} %offset_ref.3) | copy-start | bytes 393220
  2.1 15.5 %all-to-all-start = ((f32[32,4,256]{2,1,0:T(4,128)}), f32[32,4,256]{2,1,0:T(4,128)S(1)}, u32[]{:S(2)}, u32[]{:S(2)}) async-start(f32[32,4,256]{2,1,0:T(4,128)} %get-tuple-element.38), calls=%async_computation | async-start | bytes 262144 | tf_op jit(solution)/shard_map/all_to_all | solution.py:677
  9.4 1.1 %copy-start = (f32[5,64,512]{2,1,0:T(8,128)S(1)}, f32[5,64,512]{2,1,0:T(8,128)}, u32[]{:S(2)}) copy-start(f32[5,64,512]{2,1,0:T(8,128)} %star_ref.3) | copy-start | bytes 1966084
  10.5 1.2 %copy-start.2 = (f32[4,64,512]{2,1,0:T(8,128)S(1)}, f32[4,64,512]{2,1,0:T(8,128)}, u32[]{:S(2)}) copy-start(f32[4,64,512]{2,1,0:T(8,128)} %axis_ref.3) | copy-start | bytes 1572868
  10.5 1.2 %copy-start.3 = (f32[64,512]{1,0:T(8,128)S(1)}, f32[64,512]{1,0:T(8,128)}, u32[]{:S(2)}) copy-start(f32[64,512]{1,0:T(8,128)} %phase_ref.3) | copy-start | bytes 393220
  17.6 3.9 %copy-start.1 = (f32[5,64,512]{2,1,0:T(8,128)S(1)}, f32[5,64,512]{2,1,0:T(8,128)}, u32[]{:S(2)}) copy-start(f32[5,64,512]{2,1,0:T(8,128)} %star_ref.3) | copy-start | bytes 1966084
  17.7 3.9 %copy-start.5 = (f32[64,512]{1,0:T(8,128)S(1)}, f32[64,512]{1,0:T(8,128)}, u32[]{:S(2)}) copy-start(f32[64,512]{1,0:T(8,128)} %observed_ref.1) | copy-start | bytes 393220
  17.7 2.2 %collective-permute-start = (f32[1440,128]{1,0:T(8,128)S(1)}, f32[1440,128]{1,0:T(8,128)S(1)}, u32[]{:S(2)}, u32[]{:S(2)}) collective-permute-start(f32[1440,128]{1,0:T(8,128)S(1)} %get-tuple-element.41), channel_id=1, source_target_pairs={{0,1},{1,0},{2,3},{3,2},{4,5},{5,4},{6,7},{7,6},{8,9},{9,8},{10,11... | collective-permute-start | bytes 2211848 | tf_op jit(solution)/shard_map/ppermute | solution.py:650
  20.1 10.8 %collective-permute-start.1 = (f32[720,128]{1,0:T(8,128)S(1)}, f32[720,128]{1,0:T(8,128)S(1)}, u32[]{:S(2)}, u32[]{:S(2)}) collective-permute-start(f32[720,128]{1,0:T(8,128)S(1)} %get-tuple-element.49), channel_id=1, source_target_pairs={{0,2},{1,3},{2,0},{3,1},{4,6},{5,7},{6,4},{7,5},{8,10},{9,11},{10,... | collective-permute-start | bytes 1105928 | tf_op jit(solution)/shard_map/ppermute | solution.py:650
  28.9 1.3 %collective-permute-start.2 = (f32[192,128]{1,0:T(8,128)S(1)}, f32[192,128]{1,0:T(8,128)S(1)}, u32[]{:S(2)}, u32[]{:S(2)}) collective-permute-start(f32[192,128]{1,0:T(8,128)S(1)} %get-tuple-element.51), channel_id=1, source_target_pairs={{0,1},{1,0},{2,3},{3,2},{4,5},{5,4},{6,7},{7,6},{8,9},{9,8},{10,11... | collective-permute-start | bytes 294920 | tf_op jit(solution)/shard_map/ppermute | solution.py:650
  31.0 8.2 %collective-permute-start.3 = (f32[360,128]{1,0:T(8,128)S(1)}, f32[360,128]{1,0:T(8,128)S(1)}, u32[]{:S(2)}, u32[]{:S(2)}) collective-permute-start(f32[360,128]{1,0:T(8,128)S(1)} %get-tuple-element.55), channel_id=1, source_target_pairs={{0,4},{1,5},{2,6},{3,7},{4,0},{5,1},{6,2},{7,3},{8,12},{9,13},{10,... | collective-permute-start | bytes 552968 | tf_op jit(solution)/shard_map/ppermute | solution.py:650
  32.3 5.5 %collective-permute-start.4 = (f32[48,128]{1,0:T(8,128)S(1)}, f32[48,128]{1,0:T(8,128)S(1)}, u32[]{:S(2)}, u32[]{:S(2)}) collective-permute-start(f32[48,128]{1,0:T(8,128)S(1)} %get-tuple-element.59), channel_id=1, source_target_pairs={{0,4},{1,5},{2,6},{3,7},{4,0},{5,1},{6,2},{7,3},{8,12},{9,13},{10,... | collective-permute-start | bytes 73736 | tf_op jit(solution)/shard_map/ppermute | solution.py:650
  33.1 4.8 %collective-permute-start.5 = (f32[48,128]{1,0:T(8,128)S(1)}, f32[48,128]{1,0:T(8,128)S(1)}, u32[]{:S(2)}, u32[]{:S(2)}) collective-permute-start(f32[48,128]{1,0:T(8,128)S(1)} %get-tuple-element.60), channel_id=1, source_target_pairs={{0,2},{1,3},{2,0},{3,1},{4,6},{5,7},{6,4},{7,5},{8,10},{9,11},{10,... | collective-permute-start | bytes 73736 | tf_op jit(solution)/shard_map/ppermute | solution.py:650
  34.4 4.7 %collective-permute-start.6 = (f32[48,128]{1,0:T(8,128)S(1)}, f32[48,128]{1,0:T(8,128)S(1)}, u32[]{:S(2)}, u32[]{:S(2)}) collective-permute-start(f32[48,128]{1,0:T(8,128)S(1)} %get-tuple-element.61), channel_id=1, source_target_pairs={{0,6},{1,7},{2,4},{3,5},{4,2},{5,3},{6,0},{7,1},{8,14},{9,15},{10,... | collective-permute-start | bytes 73736 | tf_op jit(solution)/shard_map/ppermute | solution.py:650
  39.2 5.1 %collective-permute-start.7 = (f32[102,128]{1,0:T(8,128)S(1)}, f32[102,128]{1,0:T(8,128)S(1)}, u32[]{:S(2)}, u32[]{:S(2)}) collective-permute-start(f32[102,128]{1,0:T(8,128)S(1)} %get-tuple-element.63), channel_id=1, source_target_pairs={{0,16},{1,17},{2,18},{3,19},{4,20},{5,21},{6,22},{7,23},{8,24},{9,... | collective-permute-start | bytes 156680 | tf_op jit(solution)/shard_map/ppermute | solution.py:650
  41.6 4.2 %collective-permute-start.8 = (f32[102,128]{1,0:T(8,128)S(1)}, f32[102,128]{1,0:T(8,128)S(1)}, u32[]{:S(2)}, u32[]{:S(2)}) collective-permute-start(f32[102,128]{1,0:T(8,128)S(1)} %get-tuple-element.64), channel_id=1, source_target_pairs={{0,8},{1,9},{2,10},{3,11},{4,12},{5,13},{6,14},{7,15},{8,0},{9,1},... | collective-permute-start | bytes 156680 | tf_op jit(solution)/shard_map/ppermute | solution.py:650
  43.2 5.9 %collective-permute-start.9 = (f32[102,128]{1,0:T(8,128)S(1)}, f32[102,128]{1,0:T(8,128)S(1)}, u32[]{:S(2)}, u32[]{:S(2)}) collective-permute-start(f32[102,128]{1,0:T(8,128)S(1)} %get-tuple-element.65), channel_id=1, source_target_pairs={{0,24},{1,25},{2,26},{3,27},{4,28},{5,29},{6,30},{7,31},{8,16},{9,... | collective-permute-start | bytes 156680 | tf_op jit(solution)/shard_map/ppermute | solution.py:650

commit v5 on v4

--- a/solution.py
+++ b/solution.py
@@ -72,13 +72,14 @@
     return high, low
 
 
-def over_groups(cells, groups, body, unroll):
+def over_groups(cells, groups, body):
     def cell_body(cell, carry):
-        def group_body(index, inner):
-            body(cell, index)
+        def some(index, inner):
+            for slot in range(UNROLL):
+                body(cell, index * UNROLL + slot, slot)
             return inner
 
-        return lax.fori_loop(0, groups, group_body, carry, unroll=unroll)
+        return lax.fori_loop(0, groups // UNROLL, some, carry)
 
     lax.fori_loop(0, cells, cell_body, 0)
 
@@ -111,16 +112,28 @@
             reversed_bits = reversed_bits | (((owner >> bit) & 1) << (levels - 1 - bit))
         return reversed_bits
 
+    def reverse_band(owner):
+        bits = [(owner >> bit) & 1 for bit in range(levels)]
+        swapped = bits[0] != bits[3]
+        order = [bits[0], bits[3], jnp.where(swapped, bits[2], bits[1])]
+        order += [jnp.where(swapped, bits[1], bits[2])] + bits[4:]
+        place = jnp.zeros_like(owner)
+        for bit in order:
+            place = place * 2 + bit
+        return place
+
     first = slots == 0
     final = slots == blocks - 1
     neighbour = owners + jnp.where(first, -1, jnp.where(final, 1, 0))
     nowhere = (neighbour == owners) | (neighbour < 0) | (neighbour >= devices)
     home_owner = reverse(owners)
     halo_owner = jnp.where(nowhere, devices, reverse(neighbour))
+    home_band = reverse_band(owners)
+    halo_band = jnp.where(nowhere, devices, reverse_band(neighbour))
     home_place = slots + 1
     halo_place = jnp.where(first & ~nowhere, spread - 1, 0)
-    facts_ref[HOME] = home_owner * spread + home_place
-    facts_ref[HALO] = halo_owner * spread + halo_place
+    facts_ref[HOME] = home_band * spread + home_place
+    facts_ref[HALO] = halo_band * spread + halo_place
     facts_ref[HOME_LANES] = home_owner * lanes + home_place
     facts_ref[HALO_LANES] = halo_owner * lanes + halo_place
     facts_ref[OWNER] = owners
@@ -136,27 +149,46 @@
     lax.fori_loop(0, devices, copy, 0, unroll=8)
 
 
+def clear_kernel(out_ref):
+    out_ref[...] = jnp.zeros_like(out_ref)
+
+
 def normal_kernel(
     axes,
-    facts,
+    facts_ref,
+    factors_ref,
     phase_ref,
     offset_ref,
     axis_ref,
+    clear_ref,
     kept_ref,
     sent_ref,
+    facts_out,
+    phase_out,
+    offset_out,
+    axis_out,
     total,
     weights,
     basis,
     offsets,
+    facts,
+    semaphore,
 ):
+    scalars = pltpu.make_async_copy(facts_ref, facts, semaphore)
+    scalars.start()
+    facts_out[...] = facts_ref[...]
+    phase_out[...] = phase_ref[...]
+    offset_out[...] = offset_ref[...]
+    axis_out[...] = axis_ref[...]
     transits, stars = phase_ref.shape
     cells = stars // LANES
     knots = lax.broadcasted_iota(jnp.int32, (KB, LANES), 0)
     total[...] = jnp.zeros_like(total)
-    weights[...] = jnp.zeros_like(weights)
+    weights[...] = clear_ref[...]
+    scalars.wait()
     groups = transits // 8
 
-    def group(cell, index):
+    def group(cell, index, slot):
         first = pl.multiple_of(index * 8, 8)
         rows = pl.ds(first, 8)
         columns = pl.ds(pl.multiple_of(cell * LANES, LANES), LANES)
@@ -165,26 +197,26 @@
         values = spline_basis(phase_ref[rows, columns])
         for shift in range(4):
             for order in range(4 - shift):
-                basis[shift * 4 + order] = values[order] * values[order + shift]
-        offsets[...] = offset_ref[rows, columns]
+                basis[slot, shift * 4 + order] = values[order] * values[order + shift]
+        offsets[slot] = offset_ref[rows, columns]
         parts = [axis_ref[m, rows, columns] for m in range(4)]
         lively = [part * live for part in parts]
         for place, (m, n) in enumerate(PAIRS):
             row = place if place < ROWS else place + 3
-            weights[pl.ds(row, 8, stride=16), :] = lively[m] * parts[n]
+            weights[slot, pl.ds(row, 8, stride=16), :] = lively[m] * parts[n]
         for j in range(8):
-            relative = knots - pair_rows(offsets[pl.ds(j, 1), :])
+            relative = knots - pair_rows(offsets[slot, pl.ds(j, 1), :])
             hits = [relative == order for order in range(4)]
             highs, lows = [], []
             for shift in range(4):
                 piece = jnp.zeros((KB, LANES), jnp.float32)
                 for order in range(4 - shift):
-                    value = pair_rows(basis[shift * 4 + order, pl.ds(j, 1), :])
+                    value = pair_rows(basis[slot, shift * 4 + order, pl.ds(j, 1), :])
                     piece = jnp.where(hits[order], value, piece)
                 high, low = split(piece)
                 highs.append(high)
                 lows.append(low)
-            weight_high, weight_low = split(weights[pl.ds(j * 16, 16), :])
+            weight_high, weight_low = split(weights[slot, pl.ds(j * 16, 16), :])
             left = jnp.concatenate([weight_high, weight_low], axis=0)
             right = jnp.concatenate([weight_high, jnp.zeros_like(weight_low)], axis=0)
             result = product(
@@ -199,7 +231,7 @@
                 block = pl.ds(pl.multiple_of(place * 8, 8), 8)
                 total[block, :] = total[block, :] + band
 
-    over_groups(cells, groups, group, UNROLL)
+    over_groups(cells, groups, group)
 
     mine = lax.axis_index(axes) & 1
     half = kept_ref.shape[0] // ROWS * 8
@@ -218,17 +250,20 @@
 ENTRIES = tuple((row, column) for row in range(5) for column in range(row + 1))
 
 
-def factor_kernel(facts, star_ref, factors_ref, sums):
+def factor_kernel(facts_ref, star_ref, factors_ref, sums):
     transits, stars = star_ref.shape[1:]
     sums[...] = jnp.zeros_like(sums)
 
-    def cell_body(cell, carry):
-        columns = pl.ds(pl.multiple_of(cell * LANES, LANES), LANES)
-
-        def add(index, accumulated):
+    for cell in range(stars // LANES):
+        columns = pl.ds(cell * LANES, LANES)
+        count = facts_ref[COUNT, cell : cell + 1, :]
+        count = jnp.concatenate([count] * (LANES // transits), axis=1)
+        count = jnp.broadcast_to(count, (8, LANES))
+
+        def add(index, accumulated, columns=columns, count=count):
             first = pl.multiple_of(index * 8, 8)
             number = first + lax.broadcasted_iota(jnp.int32, (8, LANES), 0)
-            live = jnp.where(number < facts[COUNT, cell, 0], 1.0, 0.0)
+            live = jnp.where(number < count, 1.0, 0.0)
             parts = [star_ref[row, pl.ds(first, 8), columns] for row in range(5)]
             lively = [part * live for part in parts]
             return tuple(
@@ -239,9 +274,6 @@
         accumulated = lax.fori_loop(0, transits // 8, add, start, unroll=4)
         for entry in range(len(ENTRIES)):
             sums[entry, pl.ds(cell, 1), :] = jnp.sum(accumulated[entry], axis=0, keepdims=True)
-        return carry
-
-    lax.fori_loop(0, stars // LANES, cell_body, 0)
     normal = [[None for column in range(5)] for row in range(5)]
     for entry, (row, column) in enumerate(ENTRIES):
         normal[row][column] = sums[entry] + (star_prior if row == column else 0.0)
@@ -251,7 +283,6 @@
 
 
 def star_kernel(
-    axes,
     facts,
     attitude_ref,
     factors_ref,
@@ -261,24 +292,13 @@
     star_ref,
     observed_ref,
     step_ref,
-    kept_ref,
-    sent_ref,
-    total,
+    second_ref,
     table,
-    first_order,
     sums,
-    steps,
-    weights,
-    basis,
-    offsets,
 ):
     transits, stars = phase_ref.shape
     cells = stars // LANES
     groups = transits // 8
-    knots = lax.broadcasted_iota(jnp.int32, (KB, LANES), 0)
-    lanes_block = lax.broadcasted_iota(jnp.int32, (8, LANES), 1) // KB
-    total[...] = jnp.zeros_like(total)
-    weights[...] = jnp.zeros_like(weights)
     sums[...] = jnp.zeros_like(sums)
     sublane = lax.broadcasted_iota(jnp.int32, (8, LANES), 0)
 
@@ -309,7 +329,7 @@
                     spline = spline + found * values[order]
                 predicted = predicted + spline * axis_ref[m, rows, columns]
             first_value = live * (observed_ref[rows, columns] - predicted)
-            first_order[rows, columns] = first_value
+            second_ref[rows, columns] = first_value
             parts = [star_ref[row, rows, columns] for row in range(5)]
             return tuple(old + part * first_value for old, part in zip(accumulated, parts))
 
@@ -327,40 +347,72 @@
     inverse = [lower[row][row] for row in range(5)]
     answer = cholesky_solve(lower, inverse, [sums[row] for row in range(5)], 5)
     for row in range(5):
-        steps[row] = answer[row]
+        sums[row] = answer[row]
         for cell in range(cells):
             step_ref[row : row + 1, cell * LANES : (cell + 1) * LANES] = answer[row][
                 cell : cell + 1
             ]
 
-    def group(cell, index):
+    def correct(cell, carry):
+        columns = pl.ds(pl.multiple_of(cell * LANES, LANES), LANES)
+        own = [jnp.broadcast_to(sums[row, pl.ds(cell, 1), :], (8, LANES)) for row in range(5)]
+        for index in range(groups):
+            rows = pl.ds(index * 8, 8)
+            number = index * 8 + sublane
+            live = jnp.where(number < facts[COUNT, cell, 0], 1.0, 0.0)
+            fitted = star_ref[0, rows, columns] * own[0]
+            for row in range(1, 5):
+                fitted = fitted + star_ref[row, rows, columns] * own[row]
+            second_ref[rows, columns] = second_ref[rows, columns] - live * fitted
+        return carry
+
+    lax.fori_loop(0, cells, correct, 0)
+
+
+def gradient_kernel(
+    axes,
+    facts,
+    phase_ref,
+    offset_ref,
+    axis_ref,
+    second_ref,
+    kept_ref,
+    sent_ref,
+    total,
+    weights,
+    basis,
+    offsets,
+):
+    transits, stars = phase_ref.shape
+    cells = stars // LANES
+    groups = transits // 8
+    knots = lax.broadcasted_iota(jnp.int32, (KB, LANES), 0)
+    lanes_block = lax.broadcasted_iota(jnp.int32, (8, LANES), 1) // KB
+    total[...] = jnp.zeros_like(total)
+    weights[...] = jnp.zeros_like(weights)
+
+    def group(cell, index, slot):
         first = pl.multiple_of(index * 8, 8)
         rows = pl.ds(first, 8)
         columns = pl.ds(pl.multiple_of(cell * LANES, LANES), LANES)
-        number = first + lax.broadcasted_iota(jnp.int32, (8, LANES), 0)
-        live = jnp.where(number < facts[COUNT, cell, 0], 1.0, 0.0)
-        fitted = jnp.zeros((8, LANES), jnp.float32)
-        for row in range(5):
-            step = jnp.broadcast_to(steps[row, pl.ds(cell, 1), :], (8, LANES))
-            fitted = fitted + star_ref[row, rows, columns] * step
-        second = first_order[rows, columns] - live * fitted
+        second = second_ref[rows, columns]
         for m in range(4):
             value = axis_ref[m, rows, columns] * second
             high = value.astype(jnp.bfloat16).astype(jnp.float32)
-            weights[pl.ds(m, 8, stride=16), :] = high
-            weights[pl.ds(4 + m, 8, stride=16), :] = value - high
+            weights[slot, pl.ds(m, 8, stride=16), :] = high
+            weights[slot, pl.ds(4 + m, 8, stride=16), :] = value - high
         values = spline_basis(phase_ref[rows, columns])
         for order in range(4):
-            basis[order] = values[order]
-        offsets[...] = offset_ref[rows, columns]
+            basis[slot, order] = values[order]
+        offsets[slot] = offset_ref[rows, columns]
         for j in range(8):
-            relative = knots - pair_rows(offsets[pl.ds(j, 1), :])
+            relative = knots - pair_rows(offsets[slot, pl.ds(j, 1), :])
             piece = jnp.zeros((KB, LANES), jnp.float32)
             for order in range(4):
-                value = pair_rows(basis[order, pl.ds(j, 1), :])
+                value = pair_rows(basis[slot, order, pl.ds(j, 1), :])
                 piece = jnp.where(relative == order, value, piece)
             high, low = split(piece)
-            weight = weights[pl.ds(j * 16, 16), :]
+            weight = weights[slot, pl.ds(j * 16, 16), :]
             right = jnp.where(knots < 4, weight, 0.0)
             result = product(
                 jnp.concatenate([weight, right], axis=1).astype(jnp.bfloat16),
@@ -373,7 +425,7 @@
                 block = pl.ds(pl.multiple_of((place >> 3) * 8, 8), 8)
                 total[block, :] = total[block, :] + chosen
 
-    over_groups(cells, groups, group, UNROLL)
+    over_groups(cells, groups, group)
 
     mine = lax.axis_index(axes) & 1
     half = kept_ref.shape[0] * 2
@@ -398,32 +450,64 @@
     return mine
 
 
+def add_rows(out_ref, base, inputs, start, rows):
+    step = 40 if rows % 40 == 0 else rows
+
+    def add(index, carry):
+        source = pl.ds(start + index * step, step)
+        added = inputs[0][source, :]
+        for ref in inputs[1:]:
+            added = added + ref[source, :]
+        out_ref[pl.ds(base + index * step, step), :] = added
+        return carry
+
+    if step == rows:
+        add(0, 0)
+    else:
+        lax.fori_loop(0, rows // step, add, 0)
+
+
+def order_of(members):
+    return {2: ((1,), (1,)), 4: ((1, 3, 2), (2, 1, 3))}[members]
+
+
 def add_kernel(axes, group, families, *refs):
     mine = share_of(axes, group)
     members = 1 << len(group)
+    odd = lax.axis_index(axes) & 1
+    others = [0] + [jnp.where(odd == 1, second, first) for first, second in zip(*order_of(members))]
     outputs = refs[-members:]
     first = 0
     base = 0
-    for count, rows in families:
-        inputs = refs[first : first + count]
-        first += count
-        step = 40 if rows % 40 == 0 else rows
-        for other, out_ref in enumerate(outputs):
-            start = (mine ^ other) * rows
-
-            def add(index, carry, out_ref=out_ref, inputs=inputs, start=start, step=step, base=base):
-                source = pl.ds(start + index * step, step)
-                added = inputs[0][source, :]
-                for ref in inputs[1:]:
-                    added = added + ref[source, :]
-                out_ref[pl.ds(base + index * step, step), :] = added
-                return carry
-
-            if step == rows:
-                add(0, 0)
-            else:
-                lax.fori_loop(0, rows // step, add, 0)
+    for counts, rows in families:
+        segments = []
+        for count in counts:
+            segments.append(refs[first : first + count])
+            first += count
+        within = members // len(segments)
+        for other, out_ref in zip(others, outputs):
+            which = mine ^ other
+            for number, inputs in enumerate(segments):
+                if len(segments) == 1:
+                    add_rows(out_ref, base, inputs, which * rows, rows)
+                else:
+
+                    @pl.when(which // within == number)
+                    def _(out_ref=out_ref, inputs=inputs, which=which, base=base, rows=rows):
+                        add_rows(out_ref, base, inputs, (which % within) * rows, rows)
+
         base += rows
+
+
+def cut_kernel(axes, cuts, count, *refs):
+    me = lax.axis_index(axes)
+    odd = me & 1
+    outputs = refs[count:]
+    for place, (inputs, base, rows, bit) in enumerate(cuts):
+        mine = (me >> jnp.where(odd == 1, 3 - bit, bit)) & 1
+        arrays = [refs[index] for index in inputs]
+        add_rows(outputs[2 * place], 0, arrays, base + mine * rows, rows)
+        add_rows(outputs[2 * place + 1], 0, arrays, base + (1 - mine) * rows, rows)
 
 
 def sweep_kernel(spread, axes, *refs):
@@ -521,7 +605,7 @@
 
 
 def params(rows=0):
-    return pltpu.CompilerParams(vmem_limit_bytes=min(56 << 20, (16 << 20) + 2 * rows * LANES * 4))
+    return pltpu.CompilerParams(vmem_limit_bytes=min(56 << 20, (8 << 20) + 2 * rows * LANES * 4))
 
 
 def call_facts(counts, attitude, owners, slots, devices):
@@ -540,36 +624,49 @@
     )(counts, attitude, owners, slots)
 
 
-def call_normals(axes, facts, phase, knot_offset, partials, devices, spread):
+def call_clear():
+    return pl.pallas_call(
+        clear_kernel,
+        out_shape=jax.ShapeDtypeStruct((UNROLL, 8 * 16, LANES), jnp.float32),
+        out_specs=in_vmem(1)[0],
+        compiler_params=params(),
+        cost_estimate=work(200),
+        name="clear",
+    )()
+
+
+def call_normals(axes, facts, factors, phase, knot_offset, partials, clear, devices, spread):
     f32 = jnp.float32
     half = jax.ShapeDtypeStruct((devices // 2 * spread * ROWS, LANES), f32)
     blocks = devices * spread
     return pl.pallas_call(
         functools.partial(normal_kernel, axes),
-        out_shape=[half, half],
-        in_specs=in_smem(1) + in_vmem(3),
-        out_specs=in_vmem(2),
+        out_shape=[half, half]
+        + [jax.ShapeDtypeStruct(x.shape, x.dtype) for x in (facts, phase, knot_offset, partials)],
+        in_specs=in_vmem(6),
+        out_specs=in_vmem(6),
         scratch_shapes=[
             pltpu.VMEM(((blocks + 1) * 8, LANES), f32),
-            pltpu.VMEM((8 * 16, LANES), f32),
-            pltpu.VMEM((16, 8, LANES), f32),
-            pltpu.VMEM((8, LANES), jnp.int32),
+            pltpu.VMEM((UNROLL, 8 * 16, LANES), f32),
+            pltpu.VMEM((UNROLL, 16, 8, LANES), f32),
+            pltpu.VMEM((UNROLL, 8, LANES), jnp.int32),
+            pltpu.SMEM(facts.shape, jnp.int32),
+            pltpu.SemaphoreType.DMA,
         ],
         compiler_params=params(blocks * 13),
-        cost_estimate=work(8),
+        cost_estimate=work(100),
         name="normals",
-    )(facts, phase, knot_offset, partials)
+    )(facts, factors, phase, knot_offset, partials, clear)
 
 
 def call_add(axes, group, families):
     members = 1 << len(group)
-    rows = sum(count for arrays, count in families)
+    rows = sum(count for segments, count in families)
     out = jax.ShapeDtypeStruct((rows, LANES), jnp.float32)
-    arrays = [array for family, count in families for array in family]
+    arrays = [array for segments, count in families for segment in segments for array in segment]
+    shapes = [([len(segment) for segment in segments], count) for segments, count in families]
     return pl.pallas_call(
-        functools.partial(
-            add_kernel, axes, group, [(len(family), count) for family, count in families]
-        ),
+        functools.partial(add_kernel, axes, group, shapes),
         out_shape=[out] * members,
         in_specs=in_vmem(len(arrays)),
         out_specs=in_vmem(members),
@@ -579,76 +676,91 @@
     )(*arrays)
 
 
+def call_cut(axes, arrays, cuts):
+    outs = [
+        jax.ShapeDtypeStruct((rows, LANES), jnp.float32) for inputs, base, rows, bit in cuts for half in range(2)
+    ]
+    return pl.pallas_call(
+        functools.partial(cut_kernel, axes, cuts, len(arrays)),
+        out_shape=outs,
+        in_specs=in_vmem(len(arrays)),
+        out_specs=in_vmem(len(outs)),
+        compiler_params=params(sum(out.shape[0] for out in outs) * 3),
+        cost_estimate=work(0),
+        name="halves",
+    )(*arrays)
+
+
 def call_factors(facts, star_partials):
     return pl.pallas_call(
         factor_kernel,
         out_shape=jax.ShapeDtypeStruct((len(ENTRIES), 8, LANES), jnp.float32),
-        in_specs=in_smem(1) + in_vmem(1),
+        in_specs=in_vmem(2),
         out_specs=in_vmem(1)[0],
         scratch_shapes=[pltpu.VMEM((len(ENTRIES), 8, LANES), jnp.float32)],
         compiler_params=params(),
-        cost_estimate=work(20),
+        cost_estimate=work(200),
         name="factors",
     )(facts, star_partials)
 
 
-def call_stars(
-    axes,
-    facts,
-    attitude,
-    factors,
-    phase,
-    knot_offset,
-    partials,
-    star_partials,
-    observed,
-    devices,
-    spread,
-):
+def call_stars(facts, attitude, factors, phase, knot_offset, partials, star_partials, observed):
+    f32 = jnp.float32
+    transits, stars = phase.shape
+    return pl.pallas_call(
+        star_kernel,
+        out_shape=[
+            jax.ShapeDtypeStruct((5, stars), f32),
+            jax.ShapeDtypeStruct((transits, stars), f32),
+        ],
+        in_specs=in_smem(1) + in_vmem(7),
+        out_specs=in_vmem(2),
+        scratch_shapes=[
+            pltpu.VMEM((transits // 8, 32, LANES), f32),
+            pltpu.VMEM((5, 8, LANES), f32),
+        ],
+        compiler_params=params(),
+        cost_estimate=work(5),
+        name="stars",
+    )(facts, attitude, factors, phase, knot_offset, partials, star_partials, observed)
+
+
+def call_gradients(axes, facts, phase, knot_offset, partials, second, devices, spread):
     f32 = jnp.float32
     tiles = (spread + 7) // 8
-    transits, stars = phase.shape
     half = jax.ShapeDtypeStruct((devices // 2 * tiles * 4, LANES), f32)
     return pl.pallas_call(
-        functools.partial(star_kernel, axes),
-        out_shape=[
-            jax.ShapeDtypeStruct((5, stars), f32),
-            half,
-            half,
-        ],
-        in_specs=in_smem(1) + in_vmem(7),
-        out_specs=in_vmem(3),
+        functools.partial(gradient_kernel, axes),
+        out_shape=[half, half],
+        in_specs=in_smem(1) + in_vmem(4),
+        out_specs=in_vmem(2),
         scratch_shapes=[
             pltpu.VMEM(((devices + 1) * tiles * 8, LANES), f32),
-            pltpu.VMEM((transits // 8, 32, LANES), f32),
-            pltpu.VMEM((transits, stars), f32),
-            pltpu.VMEM((5, 8, LANES), f32),
-            pltpu.VMEM((5, 8, LANES), f32),
-            pltpu.VMEM((8 * 16, LANES), f32),
-            pltpu.VMEM((4, 8, LANES), f32),
-            pltpu.VMEM((8, LANES), jnp.int32),
+            pltpu.VMEM((UNROLL, 8 * 16, LANES), f32),
+            pltpu.VMEM((UNROLL, 4, 8, LANES), f32),
+            pltpu.VMEM((UNROLL, 8, LANES), jnp.int32),
         ],
         compiler_params=params((devices + 1) * tiles * 12),
-        cost_estimate=work(10),
-        name="stars",
-    )(
-        facts,
-        attitude,
-        factors,
-        phase,
-        knot_offset,
-        partials,
-        star_partials,
-        observed,
-    )
+        cost_estimate=work(5),
+        name="gradients",
+    )(facts, phase, knot_offset, partials, second)
 
 
 def swap(arrays, group, axes, devices):
+    def mask(other):
+        return sum(1 << bit for place, bit in enumerate(reversed(group)) if (other >> place) & 1)
+
+    even, odd = order_of(len(arrays) + 1)
     arrived = []
-    for other, array in enumerate(arrays, start=1):
-        mask = sum(1 << bit for place, bit in enumerate(reversed(group)) if (other >> place) & 1)
-        arrived.append(lax.ppermute(array, axes, [(i, i ^ mask) for i in range(devices)]))
+    for array, first, second in zip(arrays, even, odd):
+        pairs = [(i, i ^ mask(second if i & 1 else first)) for i in range(devices)]
+        arrived.append(lax.ppermute(array, axes, pairs))
     return arrived
+
+
+def hop(array, bit, axes, devices):
+    pairs = [(i, i ^ (1 << (3 - bit if bit and i & 1 else bit))) for i in range(devices)]
+    return lax.ppermute(array, axes, pairs)
 
 
 def per_device(
@@ -676,53 +788,52 @@
     facts, wide = call_facts(cell_counts, attitude, owners, block_slot, devices)
     whole = lax.all_to_all(wide, axes, split_axis=0, concat_axis=0, tiled=True)
     bits = list(range(devices.bit_length() - 1))
-    pairs = [bits[start : start + 2] for start in range(3, len(bits), 2)]
-    groups = [bits[:1], bits[1:3]] + pairs
-    band_groups = [bits[:1], bits[1:2], bits[2:3]] + pairs
+    later = [bits[start : start + 2] for start in range(3, len(bits), 2)]
+    groups = [bits[:1], bits[1:3]] + later
+    final = later[-1]
     chunks = (spread * ROWS, tiles * 4)
 
     def rows(kind, group):
         return chunks[kind] * (devices >> (group[-1] + 1))
 
-    def share(arrays, kind, group):
-        return call_add(axes, group, [(arrays, rows(kind, group))])
-
-    def advance(arrays, kind, group):
-        kept, *sent = share(arrays, kind, group)
-        return [kept] + swap(sent, group, axes, devices)
-
+    def advance(segments, kind, group):
+        kept, *sent = call_add(axes, group, [(segments, rows(kind, group))])
+        return [[kept] + swap(sent, group, axes, devices)]
+
+    def turn(array, bit):
+        return hop(array, bit, axes, devices)
+
+    clear = call_clear()
+    clear, facts = lax.optimization_barrier((clear, facts))
     factors = call_factors(facts, star_partials)
-    facts, factors = lax.optimization_barrier((facts, factors))
-    kept, sent = call_normals(
-        axes, facts, phase, knot_offset, attitude_partials, devices, spread
+    kept, sent, facts, phase, knot_offset, attitude_partials = call_normals(
+        axes, facts, factors, phase, knot_offset, attitude_partials, clear, devices, spread
     )
     kept, sent, whole = lax.optimization_barrier((kept, sent, whole))
-    normals = [kept] + swap([sent], band_groups[0], axes, devices)
-    kept, *sent = share(normals, 0, band_groups[1])
-    facts, whole, kept, *sent = lax.optimization_barrier((facts, whole, kept, *sent))
-    normals = [kept] + swap(sent, band_groups[1], axes, devices)
-    star_step, kept, sent = call_stars(
-        axes,
-        facts,
-        whole,
-        factors,
-        phase,
-        knot_offset,
-        attitude_partials,
-        star_partials,
-        observed,
-        devices,
-        spread,
+    arrived = turn(sent, 0)
+    star_step, second = call_stars(
+        facts, whole, factors, phase, knot_offset, attitude_partials, star_partials, observed
     )
-    gradients = [kept] + swap([sent], groups[0], axes, devices)
-    count = len(normals)
-    both = lax.optimization_barrier((*normals, *gradients))
-    normals, gradients = both[:count], both[count:]
-    for group in band_groups[2:-1]:
-        normals = advance(normals, 0, group)
+    kept, arrived, second = lax.optimization_barrier((kept, arrived, second))
+    size = kept.shape[0] // 4
+    halves = call_cut(
+        axes, [kept, arrived], [([0, 1], 0, size, 1), ([0, 1], 2 * size, size, 2)]
+    )
+    second, *halves = lax.optimization_barrier((second, *halves))
+    low = [halves[0], turn(halves[1], 1)]
+    high = [halves[2], turn(halves[3], 2)]
+    kept, sent = call_gradients(
+        axes, facts, phase, knot_offset, attitude_partials, second, devices, spread
+    )
+    gradients = [kept, turn(sent, 0)]
+    both = lax.optimization_barrier((*low, *high, *gradients))
+    halves = call_cut(axes, both[:4], [([0, 1], 0, size // 2, 2), ([2, 3], 0, size // 2, 1)])
+    normals = [[halves[0], turn(halves[1], 2)], [halves[2], turn(halves[3], 1)]]
+    gradients = [both[4:]]
     for group in groups[1:-1]:
         gradients = advance(gradients, 1, group)
-    final = groups[-1]
+    for group in later[:-1]:
+        normals = advance(normals, 0, group)
     families = [(normals, rows(0, final)), (gradients, rows(1, final))]
     kept, *sent = call_add(axes, final, families)
     parts = [kept] + swap(sent, final, axes, devices)

time: 51.1 us -> 47.8 us (0.935)
  waiting for transfers between devices: 13.1 us -> 9.93 us
  local copies, waits for them, and re-layouts: 1.1 us -> 0.5 us
  starting transfers between devices: 18.3 us -> 18.9 us
    ppermute x10 -> x12, waiting for transfers between devices: 12.6 us -> 8.09 us  [the longest x6 6.79 us: swap(): arrived.append(lax.ppermute(array, axes, pairs))]
    all_to_all x1, waiting for transfers between devices: 0.5 us -> 1.83 us  [per_device(): whole = lax.all_to_all(wide, axes, split_axis=0, concat_axis=0, tiled=True)]
    pallas_call x5 -> x7, Pallas kernels: 7.76 us -> 8.39 us  [the longest x1 4.57 us: call_gradients(): pl.pallas_call(functools.partial(gradient_kernel, axes), out_shape=[half,...]
    unnamed x14 -> x12, local copies, waits for them, and re-layouts: 1.1 us -> 0.5 us
    pallas_call x1, Pallas kernels: 1.13 us -> 0.53 us  [call_factors(): pl.pallas_call(factor_kernel, out_shape=jax.ShapeDtypeStruct((len(ENTRIES...]
    ppermute x10 -> x12, starting transfers between devices: 11 us -> 11.6 us  [the longest x6 7.12 us: swap(): arrived.append(lax.ppermute(array, axes, pairs))]
  transfers between devices with their start and end apart: 11 -> 13, of which waited for: 9 -> 8; matrix products, arithmetic and copies ran while one was open for 0% -> 0% of each run, Pallas kernels for 28% -> 29%
where the time goes in v5:
time: 47.8 us; the launch traced here: 47.5 us
  starting transfers between devices  18.9 us (40%)
  Pallas kernels  17.4 us (36%)
  waiting for transfers between devices  9.93 us (21%)
  between operations  0.76 us (2%)
  local copies, waits for them, and re-layouts  0.5 us (1%)
    all_to_all x1, starting transfers between devices, per_device(): whole = lax.all_to_all(wide, axes, split_axis=0, concat_axis=0, tiled=True)  7.3 us
    ppermute x6, starting transfers between devices, swap(): arrived.append(lax.ppermute(array, axes, pairs))  7.12 us
    ppermute x6, waiting for transfers between devices, swap(): arrived.append(lax.ppermute(array, axes, pairs))  6.79 us
    pallas_call x1, Pallas kernels, call_normals(): pl.pallas_call(functools.partial(normal_kernel, axes), out_shape=[half, h...  5.26 us
    pallas_call x1, Pallas kernels, call_gradients(): pl.pallas_call(functools.partial(gradient_kernel, axes), out_shape=[half,...  4.57 us
    ppermute x6, starting transfers between devices, hop(): return lax.ppermute(array, axes, pairs)  4.47 us
    pallas_call x1, Pallas kernels, call_stars(): pl.pallas_call(star_kernel, out_shape=[jax.ShapeDtypeStruct((5, stars), f...  3.43 us
    all_to_all x1, waiting for transfers between devices, per_device(): whole = lax.all_to_all(wide, axes, split_axis=0, concat_axis=0, tiled=True)  1.83 us
  transfers between devices with their start and end apart: 13, of which 8 were waited for; matrix products, arithmetic and copies ran while one was open for 0% of the time, Pallas kernels for 29%

profile of v5, /device:TPU:0, one launch (start us, length us, event | category | flops | bytes accessed | tf_op | source)
XLA Modules:
  0.0 47.5 jit_solution(17754586757619636096)
XLA Ops:
  0.6 1.5 %facts.1 = (s32[7,4,64]{2,1,0:T(4,128)}, f32[32,4,256]{2,1,0:T(4,128)}) custom-call(s32[4]{0:T(128)} %counts.1, f32[4,256]{1,0:T(4,128)} %attitude_ref.1, s32[4,64]{1,0:T(4,128)} %bitcast.1, s32[4,64]{1,0:T(4,128)} %slots_ref.1), custom_call_target="tpu_custom_call" | custom-call | bytes 3600000 | tf_op jit(solution)/shard_map/facts/pallas_call | solution.py:613
  2.1 7.3 %all-to-all-start = ((f32[32,4,256]{2,1,0:T(4,128)}), f32[32,4,256]{2,1,0:T(4,128)S(1)}, u32[]{:S(2)}, u32[]{:S(2)}) async-start(f32[32,4,256]{2,1,0:T(4,128)} %get-tuple-element.55), calls=%async_computation | async-start | bytes 262144 | tf_op jit(solution)/shard_map/all_to_all | solution.py:789
  9.5 0.5 %factors.1.factors_ref = f32[15,8,128]{2,1,0:T(8,128)S(1)} custom-call(s32[7,4,64]{2,1,0:T(4,128)S(1)} %copy-done.5, f32[5,64,512]{2,1,0:T(8,128)S(1)} %copy-done), custom_call_target="tpu_custom_call" | custom-call | bytes 720000000 | tf_op jit(solution)/shard_map/factors/pallas_call | solution.py:695
  10.1 0.4 copy-done.1
  10.6 5.3 %normals.1 = (f32[1440,128]{1,0:T(8,128)S(1)}, f32[1440,128]{1,0:T(8,128)S(1)}, s32[7,4,64]{2,1,0:T(4,128)S(1)}, f32[64,512]{1,0:T(8,128)S(1)}, s32[64,512]{1,0:T(8,128)S(1)}, /*index=5*/f32[4,64,512]{2,1,0:T(8,128)S(1)}) custom-call(s32[7,4,64]{2,1,0:T(4,128)S(1)} %copy-done.5, f32[15,8,128]{2,1,0:T(8,128)S(1)} %factors.1.factors_ref, ...), custom_call_target="tpu_custom_call" | custom-call | bytes 360000000 | tf_op jit(solution)/shard_map/normals/pallas_call | solution.py:642
  15.8 1.8 %all-to-all-done.attitude_ref = f32[32,4,256]{2,1,0:T(4,128)S(1)} async-done(((f32[32,4,256]{2,1,0:T(4,128)}), f32[32,4,256]{2,1,0:T(4,128)S(1)}, u32[]{:S(2)}, u32[]{:S(2)}) %all-to-all-start) | async-done | bytes 131104 | tf_op jit(solution)/shard_map/all_to_all | solution.py:789
  17.9 3.4 %stars.1 = (f32[5,512]{1,0:T(8,128)}, f32[64,512]{1,0:T(8,128)S(1)}) custom-call(s32[7,4,64]{2,1,0:T(4,128)S(1)} %get-tuple-element.52.facts, f32[32,4,256]{2,1,0:T(4,128)S(1)} %all-to-all-done.attitude_ref, f32[15,8,128]{2,1,0:T(8,128)S(1)} %factors.1.factors_ref, f32[64,512]{1,0:T(8,128)S(1)} %get-tuple-element.57.phase_ref, ...), custom_call_target="tpu_custom_call" | custom-call | bytes 18000000 | tf_op jit(solution)/shard_map/stars/pallas_call | solution.py:710
  21.5 0.4 collective-permute-start.1
  21.9 1.1 %collective-permute-start.2 = (f32[360,128]{1,0:T(8,128)S(1)}, f32[360,128]{1,0:T(8,128)S(1)}, u32[]{:S(2)}, u32[]{:S(2)}) collective-permute-start(f32[360,128]{1,0:T(8,128)S(1)} %get-tuple-element.74), channel_id=1, source_target_pairs={{0,4},{1,3},{2,6},{3,1},{4,0},{5,7},{6,2},{7,5},{8,12},{9,11},{10,... | collective-permute-start | bytes 552968 | tf_op jit(solution)/shard_map/ppermute | solution.py:763
  23.0 4.6 %gradients.1 = (f32[192,128]{1,0:T(8,128)S(1)}, f32[192,128]{1,0:T(8,128)S(1)}) custom-call(s32[7,4,64]{2,1,0:T(4,128)S(1)} %get-tuple-element.52.facts, f32[64,512]{1,0:T(8,128)S(1)} %get-tuple-element.57.phase_ref, s32[64,512]{1,0:T(8,128)S(1)} %get-tuple-element.58.offset_ref, f32[4,64,512]{2,1,0:T(8,128)S(1)} %get-tuple-element.59.axis_ref, ...), custom_call_target="tpu_custom_call" | custom-call | bytes 18000000 | tf_op jit(solution)/shard_map/gradients/pallas_call | solution.py:732
  27.7 1.3 %collective-permute-done.3.refs_1_ = f32[192,128]{1,0:T(8,128)S(1)} collective-permute-done((f32[192,128]{1,0:T(8,128)S(1)}, f32[192,128]{1,0:T(8,128)S(1)}, u32[]{:S(2)}, u32[]{:S(2)}) %collective-permute-start.3) | collective-permute-done | bytes 98336 | tf_op jit(solution)/shard_map/ppermute | solution.py:763
  29.0 1.0 %collective-permute-start.4 = (f32[180,128]{1,0:T(8,128)S(1)}, f32[180,128]{1,0:T(8,128)S(1)}, u32[]{:S(2)}, u32[]{:S(2)}) collective-permute-start(f32[180,128]{1,0:T(8,128)S(1)} %get-tuple-element.83), channel_id=1, source_target_pairs={{0,4},{1,3},{2,6},{3,1},{4,0},{5,7},{6,2},{7,5},{8,12},{9,11},{10,... | collective-permute-start | bytes 276488 | tf_op jit(solution)/shard_map/ppermute | solution.py:763
  30.0 1.7 %collective-permute-start.5 = (f32[180,128]{1,0:T(8,128)S(1)}, f32[180,128]{1,0:T(8,128)S(1)}, u32[]{:S(2)}, u32[]{:S(2)}) collective-permute-start(f32[180,128]{1,0:T(8,128)S(1)} %get-tuple-element.85), channel_id=1, source_target_pairs={{0,2},{1,5},{2,0},{3,7},{4,6},{5,1},{6,4},{7,3},{8,10},{9,13},{10,... | collective-permute-start | bytes 276488 | tf_op jit(solution)/shard_map/ppermute | solution.py:763
  31.7 0.5 %collective-permute-start.6 = (f32[48,128]{1,0:T(8,128)S(1)}, f32[48,128]{1,0:T(8,128)S(1)}, u32[]{:S(2)}, u32[]{:S(2)}) collective-permute-start(f32[48,128]{1,0:T(8,128)S(1)} %get-tuple-element.89), channel_id=1, source_target_pairs={{0,4},{1,3},{2,6},{3,1},{4,0},{5,7},{6,2},{7,5},{8,12},{9,11},{10,... | collective-permute-start | bytes 73736 | tf_op jit(solution)/shard_map/ppermute | solution.py:757
  32.3 1.4 %collective-permute-start.7 = (f32[48,128]{1,0:T(8,128)S(1)}, f32[48,128]{1,0:T(8,128)S(1)}, u32[]{:S(2)}, u32[]{:S(2)}) collective-permute-start(f32[48,128]{1,0:T(8,128)S(1)} %get-tuple-element.90), channel_id=1, source_target_pairs={{0,6},{1,5},{2,4},{3,7},{4,2},{5,1},{6,0},{7,3},{8,14},{9,13},{10,... | collective-permute-start | bytes 73736 | tf_op jit(solution)/shard_map/ppermute | solution.py:757
  33.6 1.7 %collective-permute-start.8 = (f32[48,128]{1,0:T(8,128)S(1)}, f32[48,128]{1,0:T(8,128)S(1)}, u32[]{:S(2)}, u32[]{:S(2)}) collective-permute-start(f32[48,128]{1,0:T(8,128)S(1)} %get-tuple-element.91), channel_id=1, source_target_pairs={{0,2},{1,7},{2,0},{3,5},{4,6},{5,3},{6,4},{7,1},{8,10},{9,15},{10,... | collective-permute-start | bytes 73736 | tf_op jit(solution)/shard_map/ppermute | solution.py:757
  35.3 0.3 collective-permute-done.6.refs_5_
  35.6 1.4 %collective-permute-done.7.refs_6_ = f32[48,128]{1,0:T(8,128)S(1)} collective-permute-done((f32[48,128]{1,0:T(8,128)S(1)}, f32[48,128]{1,0:T(8,128)S(1)}, u32[]{:S(2)}, u32[]{:S(2)}) %collective-permute-start.7) | collective-permute-done | bytes 24608 | tf_op jit(solution)/shard_map/ppermute | solution.py:757
  37.0 0.5 collective-permute-done.8.refs_7_
  37.5 2.0 %collective-permute-start.9 = (f32[102,128]{1,0:T(8,128)S(1)}, f32[102,128]{1,0:T(8,128)S(1)}, u32[]{:S(2)}, u32[]{:S(2)}) collective-permute-start(f32[102,128]{1,0:T(8,128)S(1)} %get-tuple-element.93), channel_id=1, source_target_pairs={{0,16},{1,9},{2,18},{3,11},{4,20},{5,13},{6,22},{7,15},{8,24},{9,1... | collective-permute-start | bytes 156680 | tf_op jit(solution)/shard_map/ppermute | solution.py:757
  39.6 1.5 %collective-permute-start.10 = (f32[102,128]{1,0:T(8,128)S(1)}, f32[102,128]{1,0:T(8,128)S(1)}, u32[]{:S(2)}, u32[]{:S(2)}) collective-permute-start(f32[102,128]{1,0:T(8,128)S(1)} %get-tuple-element.94), channel_id=1, source_target_pairs={{0,24},{1,17},{2,26},{3,19},{4,28},{5,21},{6,30},{7,23},{8,16},{9,... | collective-permute-start | bytes 156680 | tf_op jit(solution)/shard_map/ppermute | solution.py:757
  41.1 2.5 %collective-permute-done.9.refs_1_ = f32[102,128]{1,0:T(8,128)S(1)} collective-permute-done((f32[102,128]{1,0:T(8,128)S(1)}, f32[102,128]{1,0:T(8,128)S(1)}, u32[]{:S(2)}, u32[]{:S(2)}) %collective-permute-start.9) | collective-permute-done | bytes 52256 | tf_op jit(solution)/shard_map/ppermute | solution.py:757
  43.6 2.0 %collective-permute-done.10.refs_2_ = f32[102,128]{1,0:T(8,128)S(1)} collective-permute-done((f32[102,128]{1,0:T(8,128)S(1)}, f32[102,128]{1,0:T(8,128)S(1)}, u32[]{:S(2)}, u32[]{:S(2)}) %collective-permute-start.10) | collective-permute-done | bytes 52256 | tf_op jit(solution)/shard_map/ppermute | solution.py:757
  45.8 1.8 %sweeps.1 = f32[4,256]{1,0:T(4,128)} custom-call(f32[102,128]{1,0:T(8,128)S(1)} %get-tuple-element.92.refs_0_, f32[102,128]{1,0:T(8,128)S(1)} %collective-permute-done.9.refs_1_, f32[102,128]{1,0:T(8,128)S(1)} %collective-permute-done.10.refs_2_, f32[102,128]{1,0:T(8,128)S(1)} %collective-permute-done.11.refs_3_), custom_call_target="tpu_custom_call" | custom-call | bytes 7200000 | tf_op jit(solution)/shard_map/sweeps/pallas_call | solution.py:840
  (25 shorter events, 1.0 us)
Async XLA Ops:
  0.6 8.9 %copy-start = (f32[5,64,512]{2,1,0:T(8,128)S(1)}, f32[5,64,512]{2,1,0:T(8,128)}, u32[]{:S(2)}) copy-start(f32[5,64,512]{2,1,0:T(8,128)} %star_ref.3) | copy-start | bytes 1966084
  2.1 7.4 %copy-start.5 = (s32[7,4,64]{2,1,0:T(4,128)S(1)}, s32[7,4,64]{2,1,0:T(4,128)}, u32[]{:S(2)}) copy-start(s32[7,4,64]{2,1,0:T(4,128)} %get-tuple-element.50.facts_ref) | copy-start | bytes 21508
  2.1 15.5 %all-to-all-start = ((f32[32,4,256]{2,1,0:T(4,128)}), f32[32,4,256]{2,1,0:T(4,128)S(1)}, u32[]{:S(2)}, u32[]{:S(2)}) async-start(f32[32,4,256]{2,1,0:T(4,128)} %get-tuple-element.55), calls=%async_computation | async-start | bytes 262144 | tf_op jit(solution)/shard_map/all_to_all | solution.py:789
  9.4 1.0 %copy-start.1 = (f32[4,64,512]{2,1,0:T(8,128)S(1)}, f32[4,64,512]{2,1,0:T(8,128)}, u32[]{:S(2)}) copy-start(f32[4,64,512]{2,1,0:T(8,128)} %axis_ref.1) | copy-start | bytes 1572868
  9.5 1.0 %copy-start.2 = (f32[64,512]{1,0:T(8,128)S(1)}, f32[64,512]{1,0:T(8,128)}, u32[]{:S(2)}) copy-start(f32[64,512]{1,0:T(8,128)} %phase_ref.1) | copy-start | bytes 393220
  9.5 1.0 %copy-start.3 = (s32[64,512]{1,0:T(8,128)S(1)}, s32[64,512]{1,0:T(8,128)}, u32[]{:S(2)}) copy-start(s32[64,512]{1,0:T(8,128)} %offset_ref.1) | copy-start | bytes 393220
  10.6 7.3 %copy-start.4 = (f32[64,512]{1,0:T(8,128)S(1)}, f32[64,512]{1,0:T(8,128)}, u32[]{:S(2)}) copy-start(f32[64,512]{1,0:T(8,128)} %observed_ref.1) | copy-start | bytes 393220
  17.7 3.6 %collective-permute-start = (f32[1440,128]{1,0:T(8,128)S(1)}, f32[1440,128]{1,0:T(8,128)S(1)}, u32[]{:S(2)}, u32[]{:S(2)}) collective-permute-start(f32[1440,128]{1,0:T(8,128)S(1)} %get-tuple-element.62), channel_id=1, source_target_pairs={{0,1},{1,0},{2,3},{3,2},{4,5},{5,4},{6,7},{7,6},{8,9},{9,8},{10,11... | collective-permute-start | bytes 2211848 | tf_op jit(solution)/shard_map/ppermute | solution.py:763
  21.5 7.4 %collective-permute-start.1 = (f32[360,128]{1,0:T(8,128)S(1)}, f32[360,128]{1,0:T(8,128)S(1)}, u32[]{:S(2)}, u32[]{:S(2)}) collective-permute-start(f32[360,128]{1,0:T(8,128)S(1)} %get-tuple-element.72), channel_id=1, source_target_pairs={{0,2},{1,5},{2,0},{3,7},{4,6},{5,1},{6,4},{7,3},{8,10},{9,13},{10,... | collective-permute-start | bytes 552968 | tf_op jit(solution)/shard_map/ppermute | solution.py:763
  21.9 7.0 %collective-permute-start.2 = (f32[360,128]{1,0:T(8,128)S(1)}, f32[360,128]{1,0:T(8,128)S(1)}, u32[]{:S(2)}, u32[]{:S(2)}) collective-permute-start(f32[360,128]{1,0:T(8,128)S(1)} %get-tuple-element.74), channel_id=1, source_target_pairs={{0,4},{1,3},{2,6},{3,1},{4,0},{5,7},{6,2},{7,5},{8,12},{9,11},{10,... | collective-permute-start | bytes 552968 | tf_op jit(solution)/shard_map/ppermute | solution.py:763
  27.6 1.4 %collective-permute-start.3 = (f32[192,128]{1,0:T(8,128)S(1)}, f32[192,128]{1,0:T(8,128)S(1)}, u32[]{:S(2)}, u32[]{:S(2)}) collective-permute-start(f32[192,128]{1,0:T(8,128)S(1)} %get-tuple-element.77), channel_id=1, source_target_pairs={{0,1},{1,0},{2,3},{3,2},{4,5},{5,4},{6,7},{7,6},{8,9},{9,8},{10,11... | collective-permute-start | bytes 294920 | tf_op jit(solution)/shard_map/ppermute | solution.py:763
  29.0 8.4 %collective-permute-start.4 = (f32[180,128]{1,0:T(8,128)S(1)}, f32[180,128]{1,0:T(8,128)S(1)}, u32[]{:S(2)}, u32[]{:S(2)}) collective-permute-start(f32[180,128]{1,0:T(8,128)S(1)} %get-tuple-element.83), channel_id=1, source_target_pairs={{0,4},{1,3},{2,6},{3,1},{4,0},{5,7},{6,2},{7,5},{8,12},{9,11},{10,... | collective-permute-start | bytes 276488 | tf_op jit(solution)/shard_map/ppermute | solution.py:763
  30.0 7.4 %collective-permute-start.5 = (f32[180,128]{1,0:T(8,128)S(1)}, f32[180,128]{1,0:T(8,128)S(1)}, u32[]{:S(2)}, u32[]{:S(2)}) collective-permute-start(f32[180,128]{1,0:T(8,128)S(1)} %get-tuple-element.85), channel_id=1, source_target_pairs={{0,2},{1,5},{2,0},{3,7},{4,6},{5,1},{6,4},{7,3},{8,10},{9,13},{10,... | collective-permute-start | bytes 276488 | tf_op jit(solution)/shard_map/ppermute | solution.py:763
  31.7 3.9 %collective-permute-start.6 = (f32[48,128]{1,0:T(8,128)S(1)}, f32[48,128]{1,0:T(8,128)S(1)}, u32[]{:S(2)}, u32[]{:S(2)}) collective-permute-start(f32[48,128]{1,0:T(8,128)S(1)} %get-tuple-element.89), channel_id=1, source_target_pairs={{0,4},{1,3},{2,6},{3,1},{4,0},{5,7},{6,2},{7,5},{8,12},{9,11},{10,... | collective-permute-start | bytes 73736 | tf_op jit(solution)/shard_map/ppermute | solution.py:757
  32.3 4.7 %collective-permute-start.7 = (f32[48,128]{1,0:T(8,128)S(1)}, f32[48,128]{1,0:T(8,128)S(1)}, u32[]{:S(2)}, u32[]{:S(2)}) collective-permute-start(f32[48,128]{1,0:T(8,128)S(1)} %get-tuple-element.90), channel_id=1, source_target_pairs={{0,6},{1,5},{2,4},{3,7},{4,2},{5,1},{6,0},{7,3},{8,14},{9,13},{10,... | collective-permute-start | bytes 73736 | tf_op jit(solution)/shard_map/ppermute | solution.py:757
  33.6 3.8 %collective-permute-start.8 = (f32[48,128]{1,0:T(8,128)S(1)}, f32[48,128]{1,0:T(8,128)S(1)}, u32[]{:S(2)}, u32[]{:S(2)}) collective-permute-start(f32[48,128]{1,0:T(8,128)S(1)} %get-tuple-element.91), channel_id=1, source_target_pairs={{0,2},{1,7},{2,0},{3,5},{4,6},{5,3},{6,4},{7,1},{8,10},{9,15},{10,... | collective-permute-start | bytes 73736 | tf_op jit(solution)/shard_map/ppermute | solution.py:757
  37.5 6.1 %collective-permute-start.9 = (f32[102,128]{1,0:T(8,128)S(1)}, f32[102,128]{1,0:T(8,128)S(1)}, u32[]{:S(2)}, u32[]{:S(2)}) collective-permute-start(f32[102,128]{1,0:T(8,128)S(1)} %get-tuple-element.93), channel_id=1, source_target_pairs={{0,16},{1,9},{2,18},{3,11},{4,20},{5,13},{6,22},{7,15},{8,24},{9,1... | collective-permute-start | bytes 156680 | tf_op jit(solution)/shard_map/ppermute | solution.py:757
  39.6 6.0 %collective-permute-start.10 = (f32[102,128]{1,0:T(8,128)S(1)}, f32[102,128]{1,0:T(8,128)S(1)}, u32[]{:S(2)}, u32[]{:S(2)}) collective-permute-start(f32[102,128]{1,0:T(8,128)S(1)} %get-tuple-element.94), channel_id=1, source_target_pairs={{0,24},{1,17},{2,26},{3,19},{4,28},{5,21},{6,30},{7,23},{8,16},{9,... | collective-permute-start | bytes 156680 | tf_op jit(solution)/shard_map/ppermute | solution.py:757
  41.0 4.7 %collective-permute-start.11 = (f32[102,128]{1,0:T(8,128)S(1)}, f32[102,128]{1,0:T(8,128)S(1)}, u32[]{:S(2)}, u32[]{:S(2)}) collective-permute-start(f32[102,128]{1,0:T(8,128)S(1)} %get-tuple-element.95), channel_id=1, source_target_pairs={{0,8},{1,25},{2,10},{3,27},{4,12},{5,29},{6,14},{7,31},{8,0},{9,17... | collective-permute-start | bytes 156680 | tf_op jit(solution)/shard_map/ppermute | solution.py:757

commit v6 on v5

--- a/solution.py
+++ b/solution.py
@@ -454,10 +454,10 @@
     step = 40 if rows % 40 == 0 else rows
 
     def add(index, carry):
-        source = pl.ds(start + index * step, step)
-        added = inputs[0][source, :]
-        for ref in inputs[1:]:
-            added = added + ref[source, :]
+        terms = [ref[pl.ds(offset + start + index * step, step), :] for ref, offset in inputs]
+        added = terms[0]
+        for term in terms[1:]:
+            added = added + term
         out_ref[pl.ds(base + index * step, step), :] = added
         return carry
 
@@ -468,7 +468,7 @@
 
 
 def order_of(members):
-    return {2: ((1,), (1,)), 4: ((1, 3, 2), (2, 1, 3))}[members]
+    return {2: ((1,), (1,)), 4: ((3, 2, 1), (1, 3, 2))}[members]
 
 
 def add_kernel(axes, group, families, *refs):
@@ -479,11 +479,11 @@
     outputs = refs[-members:]
     first = 0
     base = 0
-    for counts, rows in families:
+    for offsets, rows in families:
         segments = []
-        for count in counts:
-            segments.append(refs[first : first + count])
-            first += count
+        for begins in offsets:
+            segments.append(list(zip(refs[first : first + len(begins)], begins)))
+            first += len(begins)
         within = members // len(segments)
         for other, out_ref in zip(others, outputs):
             which = mine ^ other
@@ -505,9 +505,28 @@
     outputs = refs[count:]
     for place, (inputs, base, rows, bit) in enumerate(cuts):
         mine = (me >> jnp.where(odd == 1, 3 - bit, bit)) & 1
-        arrays = [refs[index] for index in inputs]
+        arrays = [(refs[index], 0) for index in inputs]
         add_rows(outputs[2 * place], 0, arrays, base + mine * rows, rows)
         add_rows(outputs[2 * place + 1], 0, arrays, base + (1 - mine) * rows, rows)
+
+
+def meet_kernel(axes, size, rows, *refs):
+    low, high, gradients = refs[0:2], refs[2:4], refs[4:6]
+    own_low, own_high, own_rows, first, second, third = refs[6:]
+    me = lax.axis_index(axes)
+    odd = me & 1
+    mine = share_of(axes, [1, 2])
+    zip_low, zip_high, zip_rows = [[(ref, 0) for ref in pair] for pair in (low, high, gradients)]
+    keep_low = (me >> (2 - odd)) & 1
+    keep_high = (me >> (1 + odd)) & 1
+    add_rows(first, 0, zip_rows, (mine ^ (1 + odd)) * rows, rows)
+    add_rows(first, rows, zip_low, (1 - keep_low) * size, size)
+    add_rows(second, 0, zip_rows, (mine ^ (2 - odd)) * rows, rows)
+    add_rows(second, rows, zip_high, (1 - keep_high) * size, size)
+    add_rows(third, 0, zip_rows, (mine ^ 3) * rows, rows)
+    add_rows(own_low, 0, zip_low, keep_low * size, size)
+    add_rows(own_high, 0, zip_high, keep_high * size, size)
+    add_rows(own_rows, 0, zip_rows, mine * rows, rows)
 
 
 def sweep_kernel(spread, axes, *refs):
@@ -663,8 +682,11 @@
     members = 1 << len(group)
     rows = sum(count for segments, count in families)
     out = jax.ShapeDtypeStruct((rows, LANES), jnp.float32)
-    arrays = [array for segments, count in families for segment in segments for array in segment]
-    shapes = [([len(segment) for segment in segments], count) for segments, count in families]
+    arrays = [pair[0] for segments, count in families for segment in segments for pair in segment]
+    shapes = [
+        ([[begin for array, begin in segment] for segment in segments], count)
+        for segments, count in families
+    ]
     return pl.pallas_call(
         functools.partial(add_kernel, axes, group, shapes),
         out_shape=[out] * members,
@@ -688,6 +710,19 @@
         compiler_params=params(sum(out.shape[0] for out in outs) * 3),
         cost_estimate=work(0),
         name="halves",
+    )(*arrays)
+
+
+def call_meet(axes, arrays, size, rows):
+    counts = (size, size, rows, rows + size, rows + size, rows)
+    return pl.pallas_call(
+        functools.partial(meet_kernel, axes, size, rows),
+        out_shape=[jax.ShapeDtypeStruct((count, LANES), jnp.float32) for count in counts],
+        in_specs=in_vmem(len(arrays)),
+        out_specs=in_vmem(len(counts)),
+        compiler_params=params(sum(counts) * 3),
+        cost_estimate=work(0),
+        name="meet",
     )(*arrays)
 
 
@@ -798,7 +833,7 @@
 
     def advance(segments, kind, group):
         kept, *sent = call_add(axes, group, [(segments, rows(kind, group))])
-        return [[kept] + swap(sent, group, axes, devices)]
+        return [[(array, 0) for array in [kept] + swap(sent, group, axes, devices)]]
 
     def turn(array, bit):
         return hop(array, bit, axes, devices)
@@ -827,10 +862,14 @@
     )
     gradients = [kept, turn(sent, 0)]
     both = lax.optimization_barrier((*low, *high, *gradients))
-    halves = call_cut(axes, both[:4], [([0, 1], 0, size // 2, 2), ([2, 3], 0, size // 2, 1)])
-    normals = [[halves[0], turn(halves[1], 2)], [halves[2], turn(halves[3], 1)]]
-    gradients = [both[4:]]
-    for group in groups[1:-1]:
+    count = rows(1, groups[1])
+    own_low, own_high, own_rows, *sent = call_meet(axes, both, size // 2, count)
+    first = turn(sent[0], 2)
+    second = turn(sent[1], 1)
+    third = lax.ppermute(sent[2], axes, [(i, i ^ 6) for i in range(devices)])
+    normals = [[(own_low, 0), (first, count)], [(own_high, 0), (second, count)]]
+    gradients = [[(own_rows, 0), (first, 0), (second, 0), (third, 0)]]
+    for group in later[:-1]:
         gradients = advance(gradients, 1, group)
     for group in later[:-1]:
         normals = advance(normals, 0, group)

time: 47.8 us -> 46.2 us (0.967)
  starting transfers between devices: 18.9 us -> 17.1 us
    ppermute x0 -> x1, waiting for transfers between devices: none -> 3.89 us  [per_device(): third = lax.ppermute(sent[2], axes, [(i, i ^ 6) for i in range(devices)])]
    ppermute x6 -> x3, waiting for transfers between devices: 6.79 us -> 3.2 us  [swap(): arrived.append(lax.ppermute(array, axes, pairs))]
    ppermute x6 -> x3, starting transfers between devices: 7.12 us -> 4.45 us  [swap(): arrived.append(lax.ppermute(array, axes, pairs))]
    ppermute x0 -> x1, starting transfers between devices: none -> 0.84 us  [per_device(): third = lax.ppermute(sent[2], axes, [(i, i ^ 6) for i in range(devices)])]
  transfers between devices with their start and end apart: 13 -> 11, of which waited for: 8 -> 6; matrix products, arithmetic and copies ran while one was open for 0% -> 0% of each run, Pallas kernels for 29% -> 30%
where the time goes in v6:
time: 46.2 us; the launch traced here: 46 us
  Pallas kernels  17.4 us (38%)
  starting transfers between devices  17.1 us (37%)
  waiting for transfers between devices  10.2 us (22%)
  between operations  0.76 us (2%)
  local copies, waits for them, and re-layouts  0.5 us (1%)
    all_to_all x1, starting transfers between devices, per_device(): whole = lax.all_to_all(wide, axes, split_axis=0, concat_axis=0, tiled=True)  7.3 us
    pallas_call x1, Pallas kernels, call_normals(): pl.pallas_call(functools.partial(normal_kernel, axes), out_shape=[half, h...  5.26 us
    pallas_call x1, Pallas kernels, call_gradients(): pl.pallas_call(functools.partial(gradient_kernel, axes), out_shape=[half,...  4.57 us
    ppermute x6, starting transfers between devices, hop(): return lax.ppermute(array, axes, pairs)  4.47 us
    ppermute x3, starting transfers between devices, swap(): arrived.append(lax.ppermute(array, axes, pairs))  4.45 us
    ppermute x1, waiting for transfers between devices, per_device(): third = lax.ppermute(sent[2], axes, [(i, i ^ 6) for i in range(devices)])  3.89 us
    pallas_call x1, Pallas kernels, call_stars(): pl.pallas_call(star_kernel, out_shape=[jax.ShapeDtypeStruct((5, stars), f...  3.43 us
    ppermute x3, waiting for transfers between devices, swap(): arrived.append(lax.ppermute(array, axes, pairs))  3.2 us
  transfers between devices with their start and end apart: 11, of which 6 were waited for; matrix products, arithmetic and copies ran while one was open for 0% of the time, Pallas kernels for 30%

profile of v6, /device:TPU:0, one launch (start us, length us, event | category | flops | bytes accessed | tf_op | source)
XLA Modules:
  0.0 46.0 jit_solution(12093939764156832139)
XLA Ops:
  0.6 1.5 %facts.1 = (s32[7,4,64]{2,1,0:T(4,128)}, f32[32,4,256]{2,1,0:T(4,128)}) custom-call(s32[4]{0:T(128)} %counts.1, f32[4,256]{1,0:T(4,128)} %attitude_ref.1, s32[4,64]{1,0:T(4,128)} %bitcast.1, s32[4,64]{1,0:T(4,128)} %slots_ref.1), custom_call_target="tpu_custom_call" | custom-call | bytes 3600000 | tf_op jit(solution)/shard_map/facts/pallas_call | solution.py:632
  2.1 7.3 %all-to-all-start = ((f32[32,4,256]{2,1,0:T(4,128)}), f32[32,4,256]{2,1,0:T(4,128)S(1)}, u32[]{:S(2)}, u32[]{:S(2)}) async-start(f32[32,4,256]{2,1,0:T(4,128)} %get-tuple-element.53), calls=%async_computation | async-start | bytes 262144 | tf_op jit(solution)/shard_map/all_to_all | solution.py:824
  9.5 0.5 %factors.1.factors_ref = f32[15,8,128]{2,1,0:T(8,128)S(1)} custom-call(s32[7,4,64]{2,1,0:T(4,128)S(1)} %copy-done.5, f32[5,64,512]{2,1,0:T(8,128)S(1)} %copy-done), custom_call_target="tpu_custom_call" | custom-call | bytes 720000000 | tf_op jit(solution)/shard_map/factors/pallas_call | solution.py:730
  10.1 0.4 copy-done.1
  10.6 5.3 %normals.1 = (f32[1440,128]{1,0:T(8,128)S(1)}, f32[1440,128]{1,0:T(8,128)S(1)}, s32[7,4,64]{2,1,0:T(4,128)S(1)}, f32[64,512]{1,0:T(8,128)S(1)}, s32[64,512]{1,0:T(8,128)S(1)}, /*index=5*/f32[4,64,512]{2,1,0:T(8,128)S(1)}) custom-call(s32[7,4,64]{2,1,0:T(4,128)S(1)} %copy-done.5, f32[15,8,128]{2,1,0:T(8,128)S(1)} %factors.1.factors_ref, ...), custom_call_target="tpu_custom_call" | custom-call | bytes 360000000 | tf_op jit(solution)/shard_map/normals/pallas_call | solution.py:661
  15.8 1.8 %all-to-all-done.attitude_ref = f32[32,4,256]{2,1,0:T(4,128)S(1)} async-done(((f32[32,4,256]{2,1,0:T(4,128)}), f32[32,4,256]{2,1,0:T(4,128)S(1)}, u32[]{:S(2)}, u32[]{:S(2)}) %all-to-all-start) | async-done | bytes 131104 | tf_op jit(solution)/shard_map/all_to_all | solution.py:824
  17.7 0.2 collective-permute-start
  17.9 3.4 %stars.1 = (f32[5,512]{1,0:T(8,128)}, f32[64,512]{1,0:T(8,128)S(1)}) custom-call(s32[7,4,64]{2,1,0:T(4,128)S(1)} %get-tuple-element.50.facts, f32[32,4,256]{2,1,0:T(4,128)S(1)} %all-to-all-done.attitude_ref, f32[15,8,128]{2,1,0:T(8,128)S(1)} %factors.1.factors_ref, f32[64,512]{1,0:T(8,128)S(1)} %get-tuple-element.55.phase_ref, ...), custom_call_target="tpu_custom_call" | custom-call | bytes 18000000 | tf_op jit(solution)/shard_map/stars/pallas_call | solution.py:745
  21.3 0.2 halves.1
  21.5 0.4 collective-permute-start.1
  21.9 1.1 %collective-permute-start.2 = (f32[360,128]{1,0:T(8,128)S(1)}, f32[360,128]{1,0:T(8,128)S(1)}, u32[]{:S(2)}, u32[]{:S(2)}) collective-permute-start(f32[360,128]{1,0:T(8,128)S(1)} %get-tuple-element.72), channel_id=1, source_target_pairs={{0,4},{1,3},{2,6},{3,1},{4,0},{5,7},{6,2},{7,5},{8,12},{9,11},{10,... | collective-permute-start | bytes 552968 | tf_op jit(solution)/shard_map/ppermute | solution.py:798
  23.0 4.6 %gradients.1 = (f32[192,128]{1,0:T(8,128)S(1)}, f32[192,128]{1,0:T(8,128)S(1)}) custom-call(s32[7,4,64]{2,1,0:T(4,128)S(1)} %get-tuple-element.50.facts, f32[64,512]{1,0:T(8,128)S(1)} %get-tuple-element.55.phase_ref, s32[64,512]{1,0:T(8,128)S(1)} %get-tuple-element.56.offset_ref, f32[4,64,512]{2,1,0:T(8,128)S(1)} %get-tuple-element.57.axis_ref, ...), custom_call_target="tpu_custom_call" | custom-call | bytes 18000000 | tf_op jit(solution)/shard_map/gradients/pallas_call | solution.py:767
  27.7 1.3 %collective-permute-done.3.refs_5_ = f32[192,128]{1,0:T(8,128)S(1)} collective-permute-done((f32[192,128]{1,0:T(8,128)S(1)}, f32[192,128]{1,0:T(8,128)S(1)}, u32[]{:S(2)}, u32[]{:S(2)}) %collective-permute-start.3) | collective-permute-done | bytes 98336 | tf_op jit(solution)/shard_map/ppermute | solution.py:798
  29.0 1.0 %collective-permute-start.4 = (f32[228,128]{1,0:T(8,128)S(1)}, f32[228,128]{1,0:T(8,128)S(1)}, u32[]{:S(2)}, u32[]{:S(2)}) collective-permute-start(f32[228,128]{1,0:T(8,128)S(1)} %get-tuple-element.83), channel_id=1, source_target_pairs={{0,4},{1,3},{2,6},{3,1},{4,0},{5,7},{6,2},{7,5},{8,12},{9,11},{10,... | collective-permute-start | bytes 350216 | tf_op jit(solution)/shard_map/ppermute | solution.py:798
  30.0 1.7 %collective-permute-start.5 = (f32[228,128]{1,0:T(8,128)S(1)}, f32[228,128]{1,0:T(8,128)S(1)}, u32[]{:S(2)}, u32[]{:S(2)}) collective-permute-start(f32[228,128]{1,0:T(8,128)S(1)} %get-tuple-element.85), channel_id=1, source_target_pairs={{0,2},{1,5},{2,0},{3,7},{4,6},{5,1},{6,4},{7,3},{8,10},{9,13},{10,... | collective-permute-start | bytes 350216 | tf_op jit(solution)/shard_map/ppermute | solution.py:798
  31.7 0.8 %collective-permute-start.6 = (f32[48,128]{1,0:T(8,128)S(1)}, f32[48,128]{1,0:T(8,128)S(1)}, u32[]{:S(2)}, u32[]{:S(2)}) collective-permute-start(f32[48,128]{1,0:T(8,128)S(1)} %get-tuple-element.87), channel_id=1, source_target_pairs={{0,6},{1,7},{2,4},{3,5},{4,2},{5,3},{6,0},{7,1},{8,14},{9,15},{10,... | collective-permute-start | bytes 73736 | tf_op jit(solution)/shard_map/ppermute | solution.py:869
  32.6 3.9 %collective-permute-done.6.refs_7_ = f32[48,128]{1,0:T(8,128)S(1)} collective-permute-done((f32[48,128]{1,0:T(8,128)S(1)}, f32[48,128]{1,0:T(8,128)S(1)}, u32[]{:S(2)}, u32[]{:S(2)}) %collective-permute-start.6) | collective-permute-done | bytes 24608 | tf_op jit(solution)/shard_map/ppermute | solution.py:869
  36.5 0.1 shares.1
  36.6 2.6 %collective-permute-start.7 = (f32[102,128]{1,0:T(8,128)S(1)}, f32[102,128]{1,0:T(8,128)S(1)}, u32[]{:S(2)}, u32[]{:S(2)}) collective-permute-start(f32[102,128]{1,0:T(8,128)S(1)} %get-tuple-element.89), channel_id=1, source_target_pairs={{0,24},{1,17},{2,26},{3,19},{4,28},{5,21},{6,30},{7,23},{8,16},{9,... | collective-permute-start | bytes 156680 | tf_op jit(solution)/shard_map/ppermute | solution.py:792
  39.2 1.8 %collective-permute-start.9 = (f32[102,128]{1,0:T(8,128)S(1)}, f32[102,128]{1,0:T(8,128)S(1)}, u32[]{:S(2)}, u32[]{:S(2)}) collective-permute-start(f32[102,128]{1,0:T(8,128)S(1)} %get-tuple-element.91), channel_id=1, source_target_pairs={{0,16},{1,9},{2,18},{3,11},{4,20},{5,13},{6,22},{7,15},{8,24},{9,1... | collective-permute-start | bytes 156680 | tf_op jit(solution)/shard_map/ppermute | solution.py:792
  41.0 2.0 %collective-permute-done.7.refs_1_ = f32[102,128]{1,0:T(8,128)S(1)} collective-permute-done((f32[102,128]{1,0:T(8,128)S(1)}, f32[102,128]{1,0:T(8,128)S(1)}, u32[]{:S(2)}, u32[]{:S(2)}) %collective-permute-start.7) | collective-permute-done | bytes 52256 | tf_op jit(solution)/shard_map/ppermute | solution.py:792
  43.0 0.4 collective-permute-done.8.refs_2_
  43.5 0.7 %collective-permute-done.9.refs_3_ = f32[102,128]{1,0:T(8,128)S(1)} collective-permute-done((f32[102,128]{1,0:T(8,128)S(1)}, f32[102,128]{1,0:T(8,128)S(1)}, u32[]{:S(2)}, u32[]{:S(2)}) %collective-permute-start.9) | collective-permute-done | bytes 52256 | tf_op jit(solution)/shard_map/ppermute | solution.py:792
  44.2 1.8 %sweeps.1 = f32[4,256]{1,0:T(4,128)} custom-call(f32[102,128]{1,0:T(8,128)S(1)} %get-tuple-element.88.refs_0_, f32[102,128]{1,0:T(8,128)S(1)} %collective-permute-done.7.refs_1_, f32[102,128]{1,0:T(8,128)S(1)} %collective-permute-done.8.refs_2_, f32[102,128]{1,0:T(8,128)S(1)} %collective-permute-done.9.refs_3_), custom_call_target="tpu_custom_call" | custom-call | bytes 7200000 | tf_op jit(solution)/shard_map/sweeps/pallas_call | solution.py:879
  (20 shorter events, 0.3 us)
Async XLA Ops:
  0.6 8.9 %copy-start = (f32[5,64,512]{2,1,0:T(8,128)S(1)}, f32[5,64,512]{2,1,0:T(8,128)}, u32[]{:S(2)}) copy-start(f32[5,64,512]{2,1,0:T(8,128)} %star_ref.3) | copy-start | bytes 1966084
  2.1 7.4 %copy-start.5 = (s32[7,4,64]{2,1,0:T(4,128)S(1)}, s32[7,4,64]{2,1,0:T(4,128)}, u32[]{:S(2)}) copy-start(s32[7,4,64]{2,1,0:T(4,128)} %get-tuple-element.48.facts_ref) | copy-start | bytes 21508
  2.1 15.5 %all-to-all-start = ((f32[32,4,256]{2,1,0:T(4,128)}), f32[32,4,256]{2,1,0:T(4,128)S(1)}, u32[]{:S(2)}, u32[]{:S(2)}) async-start(f32[32,4,256]{2,1,0:T(4,128)} %get-tuple-element.53), calls=%async_computation | async-start | bytes 262144 | tf_op jit(solution)/shard_map/all_to_all | solution.py:824
  9.4 1.0 %copy-start.1 = (f32[4,64,512]{2,1,0:T(8,128)S(1)}, f32[4,64,512]{2,1,0:T(8,128)}, u32[]{:S(2)}) copy-start(f32[4,64,512]{2,1,0:T(8,128)} %axis_ref.1) | copy-start | bytes 1572868
  9.5 1.0 %copy-start.2 = (f32[64,512]{1,0:T(8,128)S(1)}, f32[64,512]{1,0:T(8,128)}, u32[]{:S(2)}) copy-start(f32[64,512]{1,0:T(8,128)} %phase_ref.1) | copy-start | bytes 393220
  9.5 1.0 %copy-start.3 = (s32[64,512]{1,0:T(8,128)S(1)}, s32[64,512]{1,0:T(8,128)}, u32[]{:S(2)}) copy-start(s32[64,512]{1,0:T(8,128)} %offset_ref.1) | copy-start | bytes 393220
  10.6 7.3 %copy-start.4 = (f32[64,512]{1,0:T(8,128)S(1)}, f32[64,512]{1,0:T(8,128)}, u32[]{:S(2)}) copy-start(f32[64,512]{1,0:T(8,128)} %observed_ref.1) | copy-start | bytes 393220
  17.7 3.6 %collective-permute-start = (f32[1440,128]{1,0:T(8,128)S(1)}, f32[1440,128]{1,0:T(8,128)S(1)}, u32[]{:S(2)}, u32[]{:S(2)}) collective-permute-start(f32[1440,128]{1,0:T(8,128)S(1)} %get-tuple-element.60), channel_id=1, source_target_pairs={{0,1},{1,0},{2,3},{3,2},{4,5},{5,4},{6,7},{7,6},{8,9},{9,8},{10,11... | collective-permute-start | bytes 2211848 | tf_op jit(solution)/shard_map/ppermute | solution.py:798
  21.5 7.4 %collective-permute-start.1 = (f32[360,128]{1,0:T(8,128)S(1)}, f32[360,128]{1,0:T(8,128)S(1)}, u32[]{:S(2)}, u32[]{:S(2)}) collective-permute-start(f32[360,128]{1,0:T(8,128)S(1)} %get-tuple-element.70), channel_id=1, source_target_pairs={{0,2},{1,5},{2,0},{3,7},{4,6},{5,1},{6,4},{7,3},{8,10},{9,13},{10,... | collective-permute-start | bytes 552968 | tf_op jit(solution)/shard_map/ppermute | solution.py:798
  21.9 7.0 %collective-permute-start.2 = (f32[360,128]{1,0:T(8,128)S(1)}, f32[360,128]{1,0:T(8,128)S(1)}, u32[]{:S(2)}, u32[]{:S(2)}) collective-permute-start(f32[360,128]{1,0:T(8,128)S(1)} %get-tuple-element.72), channel_id=1, source_target_pairs={{0,4},{1,3},{2,6},{3,1},{4,0},{5,7},{6,2},{7,5},{8,12},{9,11},{10,... | collective-permute-start | bytes 552968 | tf_op jit(solution)/shard_map/ppermute | solution.py:798
  27.6 1.4 %collective-permute-start.3 = (f32[192,128]{1,0:T(8,128)S(1)}, f32[192,128]{1,0:T(8,128)S(1)}, u32[]{:S(2)}, u32[]{:S(2)}) collective-permute-start(f32[192,128]{1,0:T(8,128)S(1)} %get-tuple-element.75), channel_id=1, source_target_pairs={{0,1},{1,0},{2,3},{3,2},{4,5},{5,4},{6,7},{7,6},{8,9},{9,8},{10,11... | collective-permute-start | bytes 294920 | tf_op jit(solution)/shard_map/ppermute | solution.py:798
  29.0 7.4 %collective-permute-start.4 = (f32[228,128]{1,0:T(8,128)S(1)}, f32[228,128]{1,0:T(8,128)S(1)}, u32[]{:S(2)}, u32[]{:S(2)}) collective-permute-start(f32[228,128]{1,0:T(8,128)S(1)} %get-tuple-element.83), channel_id=1, source_target_pairs={{0,4},{1,3},{2,6},{3,1},{4,0},{5,7},{6,2},{7,5},{8,12},{9,11},{10,... | collective-permute-start | bytes 350216 | tf_op jit(solution)/shard_map/ppermute | solution.py:798
  30.0 6.4 %collective-permute-start.5 = (f32[228,128]{1,0:T(8,128)S(1)}, f32[228,128]{1,0:T(8,128)S(1)}, u32[]{:S(2)}, u32[]{:S(2)}) collective-permute-start(f32[228,128]{1,0:T(8,128)S(1)} %get-tuple-element.85), channel_id=1, source_target_pairs={{0,2},{1,5},{2,0},{3,7},{4,6},{5,1},{6,4},{7,3},{8,10},{9,13},{10,... | collective-permute-start | bytes 350216 | tf_op jit(solution)/shard_map/ppermute | solution.py:798
  31.7 4.7 %collective-permute-start.6 = (f32[48,128]{1,0:T(8,128)S(1)}, f32[48,128]{1,0:T(8,128)S(1)}, u32[]{:S(2)}, u32[]{:S(2)}) collective-permute-start(f32[48,128]{1,0:T(8,128)S(1)} %get-tuple-element.87), channel_id=1, source_target_pairs={{0,6},{1,7},{2,4},{3,5},{4,2},{5,3},{6,0},{7,1},{8,14},{9,15},{10,... | collective-permute-start | bytes 73736 | tf_op jit(solution)/shard_map/ppermute | solution.py:869
  36.6 6.5 %collective-permute-start.7 = (f32[102,128]{1,0:T(8,128)S(1)}, f32[102,128]{1,0:T(8,128)S(1)}, u32[]{:S(2)}, u32[]{:S(2)}) collective-permute-start(f32[102,128]{1,0:T(8,128)S(1)} %get-tuple-element.89), channel_id=1, source_target_pairs={{0,24},{1,17},{2,26},{3,19},{4,28},{5,21},{6,30},{7,23},{8,16},{9,... | collective-permute-start | bytes 156680 | tf_op jit(solution)/shard_map/ppermute | solution.py:792
  39.2 4.3 %collective-permute-start.8 = (f32[102,128]{1,0:T(8,128)S(1)}, f32[102,128]{1,0:T(8,128)S(1)}, u32[]{:S(2)}, u32[]{:S(2)}) collective-permute-start(f32[102,128]{1,0:T(8,128)S(1)} %get-tuple-element.90), channel_id=1, source_target_pairs={{0,8},{1,25},{2,10},{3,27},{4,12},{5,29},{6,14},{7,31},{8,0},{9,17... | collective-permute-start | bytes 156680 | tf_op jit(solution)/shard_map/ppermute | solution.py:792
  39.2 5.0 %collective-permute-start.9 = (f32[102,128]{1,0:T(8,128)S(1)}, f32[102,128]{1,0:T(8,128)S(1)}, u32[]{:S(2)}, u32[]{:S(2)}) collective-permute-start(f32[102,128]{1,0:T(8,128)S(1)} %get-tuple-element.91), channel_id=1, source_target_pairs={{0,16},{1,9},{2,18},{3,11},{4,20},{5,13},{6,22},{7,15},{8,24},{9,1... | collective-permute-start | bytes 156680 | tf_op jit(solution)/shard_map/ppermute | solution.py:792

commit v7 on v6

--- a/solution.py
+++ b/solution.py
@@ -12,7 +12,7 @@
 ITERS = 6
 LANES = 128
 PAIRS = tuple((m, n) for m in range(4) for n in range(m, 4))
-HOME, HALO, HOME_LANES, HALO_LANES, OWNER, SLOT, COUNT = range(7)
+HOME, HOME_LANES, OWNER, SLOT, COUNT = range(5)
 ROWS = 5
 UNROLL = 8
 
@@ -97,6 +97,23 @@
     )
 
 
+def reversed_place(owner, levels):
+    place = owner * 0
+    for bit in range(levels):
+        place = place * 2 + ((owner >> bit) & 1)
+    return place
+
+
+def band_place(owner, levels):
+    bits = [(owner >> bit) & 1 for bit in range(levels)]
+    differ = bits[0] ^ bits[3]
+    third = bits[1] ^ (differ * (bits[1] ^ bits[2]))
+    place = owner * 0
+    for bit in [bits[0], bits[3], third, bits[1] ^ bits[2] ^ third] + bits[4:]:
+        place = place * 2 + bit
+    return place
+
+
 def facts_kernel(blocks, counts, attitude_ref, owners_ref, slots_ref, facts_ref, wide_ref):
     devices = wide_ref.shape[0]
     levels = devices.bit_length() - 1
@@ -106,36 +123,8 @@
     slots = slots_ref[...]
     cells = owners.shape[0]
 
-    def reverse(owner):
-        reversed_bits = jnp.zeros_like(owner)
-        for bit in range(levels):
-            reversed_bits = reversed_bits | (((owner >> bit) & 1) << (levels - 1 - bit))
-        return reversed_bits
-
-    def reverse_band(owner):
-        bits = [(owner >> bit) & 1 for bit in range(levels)]
-        swapped = bits[0] != bits[3]
-        order = [bits[0], bits[3], jnp.where(swapped, bits[2], bits[1])]
-        order += [jnp.where(swapped, bits[1], bits[2])] + bits[4:]
-        place = jnp.zeros_like(owner)
-        for bit in order:
-            place = place * 2 + bit
-        return place
-
-    first = slots == 0
-    final = slots == blocks - 1
-    neighbour = owners + jnp.where(first, -1, jnp.where(final, 1, 0))
-    nowhere = (neighbour == owners) | (neighbour < 0) | (neighbour >= devices)
-    home_owner = reverse(owners)
-    halo_owner = jnp.where(nowhere, devices, reverse(neighbour))
-    home_band = reverse_band(owners)
-    halo_band = jnp.where(nowhere, devices, reverse_band(neighbour))
-    home_place = slots + 1
-    halo_place = jnp.where(first & ~nowhere, spread - 1, 0)
-    facts_ref[HOME] = home_band * spread + home_place
-    facts_ref[HALO] = halo_band * spread + halo_place
-    facts_ref[HOME_LANES] = home_owner * lanes + home_place
-    facts_ref[HALO_LANES] = halo_owner * lanes + halo_place
+    facts_ref[HOME] = band_place(owners, levels) * spread + slots + 1
+    facts_ref[HOME_LANES] = reversed_place(owners, levels) * lanes + slots + 1
     facts_ref[OWNER] = owners
     facts_ref[SLOT] = slots
     for cell in range(cells):
@@ -227,12 +216,18 @@
             band = jnp.concatenate(
                 [result[0:8] + result[16:24], result[8:16] + result[24:32]], axis=1
             )
-            for place in (facts[HOME, cell, first + j], facts[HALO, cell, first + j]):
-                block = pl.ds(pl.multiple_of(place * 8, 8), 8)
-                total[block, :] = total[block, :] + band
+            block = pl.ds(pl.multiple_of(facts[HOME, cell, first + j] * 8, 8), 8)
+            total[block, :] = total[block, :] + band
 
     over_groups(cells, groups, group)
 
+    levels = lax.axis_size(axes).bit_length() - 1
+    places = [band_place(owner, levels) for owner in range(1 << levels)]
+    spread = total.shape[0] // 8 // len(places)
+    for lower, upper in zip(places[:-1], places[1:]):
+        start, stop = upper * spread * 8, (lower + 1) * spread * 8
+        total[start : start + 8, :] = total[stop - 16 : stop - 8, :]
+        total[stop - 8 : stop, :] = total[start + 8 : start + 16, :]
     mine = lax.axis_index(axes) & 1
     half = kept_ref.shape[0] // ROWS * 8
 
@@ -371,18 +366,26 @@
 
 def gradient_kernel(
     axes,
-    facts,
+    facts_ref,
     phase_ref,
     offset_ref,
     axis_ref,
     second_ref,
+    step_ref,
     kept_ref,
     sent_ref,
+    step_hbm,
     total,
     weights,
     basis,
     offsets,
+    facts,
+    semaphores,
 ):
+    scalars = pltpu.make_async_copy(facts_ref, facts, semaphores.at[0])
+    scalars.start()
+    result_copy = pltpu.make_async_copy(step_ref, step_hbm, semaphores.at[1])
+    result_copy.start()
     transits, stars = phase_ref.shape
     cells = stars // LANES
     groups = transits // 8
@@ -390,6 +393,7 @@
     lanes_block = lax.broadcasted_iota(jnp.int32, (8, LANES), 1) // KB
     total[...] = jnp.zeros_like(total)
     weights[...] = jnp.zeros_like(weights)
+    scalars.wait()
 
     def group(cell, index, slot):
         first = pl.multiple_of(index * 8, 8)
@@ -420,13 +424,21 @@
                 jnp.concatenate([low] * 4, axis=0),
             )[0:8]
             result = jnp.concatenate([result, result], axis=1)
-            for place in (facts[HOME_LANES, cell, first + j], facts[HALO_LANES, cell, first + j]):
-                chosen = jnp.where(lanes_block == (place & 7), result, 0.0)
-                block = pl.ds(pl.multiple_of((place >> 3) * 8, 8), 8)
-                total[block, :] = total[block, :] + chosen
+            place = facts[HOME_LANES, cell, first + j]
+            chosen = jnp.where(lanes_block == (place & 7), result, 0.0)
+            block = pl.ds(pl.multiple_of((place >> 3) * 8, 8), 8)
+            total[block, :] = total[block, :] + chosen
 
     over_groups(cells, groups, group)
 
+    levels = lax.axis_size(axes).bit_length() - 1
+    places = [reversed_place(owner, levels) for owner in range(1 << levels)]
+    rows = total.shape[0] // len(places)
+    for lower, upper in zip(places[:-1], places[1:]):
+        start, stop = upper * rows, (lower + 1) * rows
+        ending, opening = total[stop - 8 : stop, :], total[start : start + 8, :]
+        total[start : start + 8, :] = opening + jnp.where(lanes_block == 0, ending, 0.0)
+        total[stop - 8 : stop, :] = ending + jnp.where(lanes_block == 1, opening, 0.0)
     mine = lax.axis_index(axes) & 1
     half = kept_ref.shape[0] * 2
 
@@ -440,6 +452,7 @@
         return carry
 
     lax.fori_loop(0, half // 16, pack, 0)
+    result_copy.wait()
 
 
 def share_of(axes, group):
@@ -563,52 +576,73 @@
     def row_of(shift, m, n):
         return band[shift, index[(m, n)] : index[(m, n)] + 1, :]
 
-    ahead = [
-        [jnp.concatenate([row_of(shift, m, n) for n in range(4)], axis=0) for m in range(4)]
-        for shift in range(4)
-    ]
-    behind = [
-        [pltpu.roll(ahead[shift][m], shift, axis=1) if shift else None for m in range(4)]
-        for shift in range(4)
-    ]
-    shifted = 2.0 * smoothing + damping
+    def square(entry):
+        return jnp.concatenate([entry(m, n) for m in range(4) for n in range(4)], axis=0)
+
     diagonal = [
-        [row_of(0, row, column) + (shifted if row == column else 0.0) for column in range(4)]
+        [
+            row_of(0, row, column) + (2.0 * smoothing + damping if row == column else 0.0)
+            for column in range(4)
+        ]
         for row in range(4)
     ]
     lower, inverse = cholesky_factor(diagonal, 4)
-    gradient = jnp.concatenate(
+    one = jnp.ones((1, width), jnp.float32)
+    zero = jnp.zeros((1, width), jnp.float32)
+    columns = [
+        cholesky_solve(lower, inverse, [one if row == column else zero for row in range(4)], 4)
+        for column in range(4)
+    ]
+    solve = square(lambda m, n: columns[n][m])
+    sublane = lax.broadcasted_iota(jnp.int32, (16, width), 0)
+    same = (sublane >> 2) == (sublane & 3)
+    operator = {0: square(lambda m, n: diagonal[m][n])}
+    for shift in range(1, 4):
+        ahead = square(lambda m, n: row_of(shift, m, n))
+        operator[shift] = ahead
+        operator[-shift] = pltpu.roll(ahead, shift, axis=1)
+    for shift in (1, -1):
+        operator[shift] = operator[shift] - jnp.where(same, smoothing, 0.0)
+    own = jnp.concatenate(
         [
             band_ref[spread * ROWS + tile * 4 : spread * ROWS + (tile + 1) * 4, :]
             for tile in range(tiles)
         ],
         axis=1,
     )
-    lane = lax.broadcasted_iota(jnp.int32, (4, width), 1)
+    gradient = square(lambda m, n: own[m : m + 1])
+    lane = lax.broadcasted_iota(jnp.int32, (8, width), 1)
     me = lax.axis_index(axes)
     start = jnp.where(me == 0, KB, 0)
     stop = jnp.where(me == lax.axis_size(axes) - 1, (spread - 1) * KB, spread * KB)
     keep = jnp.where((lane >= start) & (lane < stop), relaxation, 0.0)
-    answer = jnp.zeros((4, width), jnp.float32)
+    place = lax.broadcasted_iota(jnp.int32, (8, width), 0)
+    odd = (place & 1) == 1
+    late = (place & 2) == 2
+
+    def over_columns(value):
+        value = value + jnp.where(odd, pltpu.roll(value, 1, axis=0), pltpu.roll(value, 7, axis=0))
+        return value + jnp.where(late, pltpu.roll(value, 2, axis=0), pltpu.roll(value, 6, axis=0))
+
+    answer = jnp.zeros((8, width), jnp.float32)
     for sweep in range(ITERS):
-        misfit = gradient
+        misfit = [gradient[0:8], gradient[8:16]]
         if sweep:
-            moved = {}
+            moved = {0: answer}
             for shift in range(1, 4):
                 moved[shift] = pltpu.roll(answer, width - shift, axis=1)
                 moved[-shift] = pltpu.roll(answer, shift, axis=1)
-            applied = []
-            for m in range(4):
-                terms = ahead[0][m] * answer
-                for shift in range(1, 4):
-                    terms = terms + ahead[shift][m] * moved[shift]
-                    terms = terms + behind[shift][m] * moved[-shift]
-                applied.append(jnp.sum(terms, axis=0, keepdims=True))
-            regular = smoothing * (2.0 * answer - moved[-1] - moved[1]) + damping * answer
-            misfit = gradient - regular - jnp.concatenate(applied, axis=0)
-        correction = cholesky_solve(lower, inverse, [misfit[m : m + 1] for m in range(4)], 4)
-        answer = answer + keep * jnp.concatenate(correction, axis=0)
-    out_ref[...] = answer[:, KB : KB + out_ref.shape[1]]
+            for half in range(2):
+                rows = slice(half * 8, half * 8 + 8)
+                terms = [operator[shift][rows] * moved[shift] for shift in range(-3, 4)]
+                applied = ((terms[0] + terms[1]) + (terms[2] + terms[3])) + (
+                    (terms[4] + terms[5]) + terms[6]
+                )
+                misfit[half] = misfit[half] - over_columns(applied)
+        correction = solve[0:8] * misfit[0] + solve[8:16] * misfit[1]
+        correction = correction + pltpu.roll(correction, 4, axis=0)
+        answer = answer + keep * correction
+    out_ref[...] = answer[0:4, KB : KB + out_ref.shape[1]]
 
 
 def in_vmem(count):
@@ -665,7 +699,7 @@
         in_specs=in_vmem(6),
         out_specs=in_vmem(6),
         scratch_shapes=[
-            pltpu.VMEM(((blocks + 1) * 8, LANES), f32),
+            pltpu.VMEM((blocks * 8, LANES), f32),
             pltpu.VMEM((UNROLL, 8 * 16, LANES), f32),
             pltpu.VMEM((UNROLL, 16, 8, LANES), f32),
             pltpu.VMEM((UNROLL, 8, LANES), jnp.int32),
@@ -760,25 +794,27 @@
     )(facts, attitude, factors, phase, knot_offset, partials, star_partials, observed)
 
 
-def call_gradients(axes, facts, phase, knot_offset, partials, second, devices, spread):
+def call_gradients(axes, facts, phase, knot_offset, partials, second, step, devices, spread):
     f32 = jnp.float32
     tiles = (spread + 7) // 8
     half = jax.ShapeDtypeStruct((devices // 2 * tiles * 4, LANES), f32)
     return pl.pallas_call(
         functools.partial(gradient_kernel, axes),
-        out_shape=[half, half],
-        in_specs=in_smem(1) + in_vmem(4),
-        out_specs=in_vmem(2),
+        out_shape=[half, half, jax.ShapeDtypeStruct(step.shape, f32)],
+        in_specs=in_vmem(6),
+        out_specs=in_vmem(2) + [pl.BlockSpec(memory_space=pltpu.HBM)],
         scratch_shapes=[
-            pltpu.VMEM(((devices + 1) * tiles * 8, LANES), f32),
+            pltpu.VMEM((devices * tiles * 8, LANES), f32),
             pltpu.VMEM((UNROLL, 8 * 16, LANES), f32),
             pltpu.VMEM((UNROLL, 4, 8, LANES), f32),
             pltpu.VMEM((UNROLL, 8, LANES), jnp.int32),
+            pltpu.SMEM(facts.shape, jnp.int32),
+            pltpu.SemaphoreType.DMA((2,)),
         ],
         compiler_params=params((devices + 1) * tiles * 12),
         cost_estimate=work(5),
         name="gradients",
-    )(facts, phase, knot_offset, partials, second)
+    )(facts, phase, knot_offset, partials, second, step)
 
 
 def swap(arrays, group, axes, devices):
@@ -846,7 +882,7 @@
     )
     kept, sent, whole = lax.optimization_barrier((kept, sent, whole))
     arrived = turn(sent, 0)
-    star_step, second = call_stars(
+    step, second = call_stars(
         facts, whole, factors, phase, knot_offset, attitude_partials, star_partials, observed
     )
     kept, arrived, second = lax.optimization_barrier((kept, arrived, second))
@@ -857,8 +893,8 @@
     second, *halves = lax.optimization_barrier((second, *halves))
     low = [halves[0], turn(halves[1], 1)]
     high = [halves[2], turn(halves[3], 2)]
-    kept, sent = call_gradients(
-        axes, facts, phase, knot_offset, attitude_partials, second, devices, spread
+    kept, sent, star_step = call_gradients(
+        axes, facts, phase, knot_offset, attitude_partials, second, step, devices, spread
     )
     gradients = [kept, turn(sent, 0)]
     both = lax.optimization_barrier((*low, *high, *gradients))

time: 46.2 us -> 44.2 us (0.957)
  Pallas kernels: 17.4 us -> 15.4 us
    ppermute x6, starting transfers between devices: 4.47 us -> 3.82 us  [hop(): return lax.ppermute(array, axes, pairs)]
    ppermute x6, waiting for transfers between devices: 1.3 us -> 1.95 us  [hop(): return lax.ppermute(array, axes, pairs)]
    pallas_call x1, Pallas kernels: 3.43 us -> 2.78 us  [call_stars(): pl.pallas_call(star_kernel, out_shape=[jax.ShapeDtypeStruct((5, stars), f...]
    pallas_call x1, Pallas kernels: 4.57 us -> 3.96 us  [call_gradients(): pl.pallas_call(functools.partial(gradient_kernel, axes), out_shape=[half,...]
    ppermute x1, starting transfers between devices: 0.84 us -> 1.31 us  [per_device(): third = lax.ppermute(sent[2], axes, [(i, i ^ 6) for i in range(devices)])]
    ppermute x1, waiting for transfers between devices: 3.89 us -> 3.41 us  [per_device(): third = lax.ppermute(sent[2], axes, [(i, i ^ 6) for i in range(devices)])]
  transfers between devices with their start and end apart: 11 -> 11, of which waited for: 6 -> 7; matrix products, arithmetic and copies ran while one was open for 0% -> 0% of each run, Pallas kernels for 30% -> 28%
where the time goes in v7:
time: 44.2 us; the launch traced here: 44 us
  starting transfers between devices  16.9 us (38%)
  Pallas kernels  15.4 us (35%)
  waiting for transfers between devices  10.4 us (24%)
  between operations  0.77 us (2%)
  local copies, waits for them, and re-layouts  0.5 us (1%)
    all_to_all x1, starting transfers between devices, per_device(): whole = lax.all_to_all(wide, axes, split_axis=0, concat_axis=0, tiled=True)  7.3 us
    pallas_call x1, Pallas kernels, call_normals(): pl.pallas_call(functools.partial(normal_kernel, axes), out_shape=[half, h...  4.82 us
    ppermute x3, starting transfers between devices, swap(): arrived.append(lax.ppermute(array, axes, pairs))  4.45 us
    pallas_call x1, Pallas kernels, call_gradients(): pl.pallas_call(functools.partial(gradient_kernel, axes), out_shape=[half,...  3.96 us
    ppermute x6, starting transfers between devices, hop(): return lax.ppermute(array, axes, pairs)  3.82 us
    ppermute x1, waiting for transfers between devices, per_device(): third = lax.ppermute(sent[2], axes, [(i, i ^ 6) for i in range(devices)])  3.41 us
    pallas_call x1, Pallas kernels, call_stars(): pl.pallas_call(star_kernel, out_shape=[jax.ShapeDtypeStruct((5, stars), f...  2.78 us
    ppermute x3, waiting for transfers between devices, swap(): arrived.append(lax.ppermute(array, axes, pairs))  2.75 us
  transfers between devices with their start and end apart: 11, of which 7 were waited for; matrix products, arithmetic and copies ran while one was open for 0% of the time, Pallas kernels for 28%

profile of v7, /device:TPU:0, one launch (start us, length us, event | category | flops | bytes accessed | tf_op | source)
XLA Modules:
  0.0 44.0 jit_solution(2614472734088125682)
XLA Ops:
  0.6 1.5 %facts.1 = (s32[5,4,64]{2,1,0:T(4,128)}, f32[32,4,256]{2,1,0:T(4,128)}) custom-call(s32[4]{0:T(128)} %counts.1, f32[4,256]{1,0:T(4,128)} %attitude_ref.1, s32[4,64]{1,0:T(4,128)} %bitcast.1, s32[4,64]{1,0:T(4,128)} %slots_ref.1), custom_call_target="tpu_custom_call" | custom-call | bytes 3600000 | tf_op jit(solution)/shard_map/facts/pallas_call | solution.py:666
  2.1 7.3 %all-to-all-start = ((f32[32,4,256]{2,1,0:T(4,128)}), f32[32,4,256]{2,1,0:T(4,128)S(1)}, u32[]{:S(2)}, u32[]{:S(2)}) async-start(f32[32,4,256]{2,1,0:T(4,128)} %get-tuple-element.57), calls=%async_computation | async-start | bytes 262144 | tf_op jit(solution)/shard_map/all_to_all | solution.py:860
  9.5 0.5 %factors.1.factors_ref = f32[15,8,128]{2,1,0:T(8,128)S(1)} custom-call(s32[5,4,64]{2,1,0:T(4,128)S(1)} %copy-done.5, f32[5,64,512]{2,1,0:T(8,128)S(1)} %copy-done), custom_call_target="tpu_custom_call" | custom-call | bytes 720000000 | tf_op jit(solution)/shard_map/factors/pallas_call | solution.py:764
  10.1 0.4 copy-done.1
  10.6 4.8 %normals.1 = (f32[1440,128]{1,0:T(8,128)S(1)}, f32[1440,128]{1,0:T(8,128)S(1)}, s32[5,4,64]{2,1,0:T(4,128)S(1)}, f32[64,512]{1,0:T(8,128)S(1)}, s32[64,512]{1,0:T(8,128)S(1)}, /*index=5*/f32[4,64,512]{2,1,0:T(8,128)S(1)}) custom-call(s32[5,4,64]{2,1,0:T(4,128)S(1)} %copy-done.5, f32[15,8,128]{2,1,0:T(8,128)S(1)} %factors.1.factors_ref, ...), custom_call_target="tpu_custom_call" | custom-call | bytes 360000000 | tf_op jit(solution)/shard_map/normals/pallas_call | solution.py:695
  15.4 2.3 %all-to-all-done.attitude_ref = f32[32,4,256]{2,1,0:T(4,128)S(1)} async-done(((f32[32,4,256]{2,1,0:T(4,128)}), f32[32,4,256]{2,1,0:T(4,128)S(1)}, u32[]{:S(2)}, u32[]{:S(2)}) %all-to-all-start) | async-done | bytes 131104 | tf_op jit(solution)/shard_map/all_to_all | solution.py:860
  17.7 0.2 collective-permute-start
  17.9 2.8 %stars.1 = (f32[5,512]{1,0:T(8,128)S(1)}, f32[64,512]{1,0:T(8,128)S(1)}) custom-call(s32[5,4,64]{2,1,0:T(4,128)S(1)} %get-tuple-element.51.facts.facts_ref, f32[32,4,256]{2,1,0:T(4,128)S(1)} %all-to-all-done.attitude_ref, f32[15,8,128]{2,1,0:T(8,128)S(1)} %factors.1.factors_ref, f32[64,512]{1,0:T(8,128)S(1)} %get-tuple-element.52.phase_ref, ...), custom_call_target="tpu_custom_call" | custom-call | bytes 18000000 | tf_op jit(solution)/shard_map/stars/pallas_call | solution.py:779
  20.7 0.2 halves.1
  20.9 0.4 collective-permute-start.1
  21.3 0.9 %collective-permute-start.2 = (f32[360,128]{1,0:T(8,128)S(1)}, f32[360,128]{1,0:T(8,128)S(1)}, u32[]{:S(2)}, u32[]{:S(2)}) collective-permute-start(f32[360,128]{1,0:T(8,128)S(1)} %get-tuple-element.75), channel_id=1, source_target_pairs={{0,4},{1,3},{2,6},{3,1},{4,0},{5,7},{6,2},{7,5},{8,12},{9,11},{10,... | collective-permute-start | bytes 552968 | tf_op jit(solution)/shard_map/ppermute | solution.py:834
  22.2 4.0 %gradients.1 = (f32[192,128]{1,0:T(8,128)S(1)}, f32[192,128]{1,0:T(8,128)S(1)}, f32[5,512]{1,0:T(8,128)}) custom-call(s32[5,4,64]{2,1,0:T(4,128)S(1)} %get-tuple-element.51.facts.facts_ref, f32[64,512]{1,0:T(8,128)S(1)} %get-tuple-element.52.phase_ref, s32[64,512]{1,0:T(8,128)S(1)} %get-tuple-element.53.offset_ref, ...), custom_call_target="tpu_custom_call" | custom-call | bytes 18000000 | tf_op jit(solution)/shard_map/gradients/pallas_call | solution.py:801
  26.3 1.3 %collective-permute-done.3.refs_5_ = f32[192,128]{1,0:T(8,128)S(1)} collective-permute-done((f32[192,128]{1,0:T(8,128)S(1)}, f32[192,128]{1,0:T(8,128)S(1)}, u32[]{:S(2)}, u32[]{:S(2)}) %collective-permute-start.3) | collective-permute-done | bytes 98336 | tf_op jit(solution)/shard_map/ppermute | solution.py:834
  27.5 0.7 %collective-permute-done.1.refs_1_ = f32[360,128]{1,0:T(8,128)S(1)} collective-permute-done((f32[360,128]{1,0:T(8,128)S(1)}, f32[360,128]{1,0:T(8,128)S(1)}, u32[]{:S(2)}, u32[]{:S(2)}) %collective-permute-start.1) | collective-permute-done | bytes 184352 | tf_op jit(solution)/shard_map/ppermute | solution.py:834
  28.3 0.6 %collective-permute-start.4 = (f32[228,128]{1,0:T(8,128)S(1)}, f32[228,128]{1,0:T(8,128)S(1)}, u32[]{:S(2)}, u32[]{:S(2)}) collective-permute-start(f32[228,128]{1,0:T(8,128)S(1)} %get-tuple-element.85), channel_id=1, source_target_pairs={{0,4},{1,3},{2,6},{3,1},{4,0},{5,7},{6,2},{7,5},{8,12},{9,11},{10,... | collective-permute-start | bytes 350216 | tf_op jit(solution)/shard_map/ppermute | solution.py:834
  28.8 1.7 %collective-permute-start.5 = (f32[228,128]{1,0:T(8,128)S(1)}, f32[228,128]{1,0:T(8,128)S(1)}, u32[]{:S(2)}, u32[]{:S(2)}) collective-permute-start(f32[228,128]{1,0:T(8,128)S(1)} %get-tuple-element.87), channel_id=1, source_target_pairs={{0,2},{1,5},{2,0},{3,7},{4,6},{5,1},{6,4},{7,3},{8,10},{9,13},{10,... | collective-permute-start | bytes 350216 | tf_op jit(solution)/shard_map/ppermute | solution.py:834
  30.5 1.3 %collective-permute-start.6 = (f32[48,128]{1,0:T(8,128)S(1)}, f32[48,128]{1,0:T(8,128)S(1)}, u32[]{:S(2)}, u32[]{:S(2)}) collective-permute-start(f32[48,128]{1,0:T(8,128)S(1)} %get-tuple-element.89), channel_id=1, source_target_pairs={{0,6},{1,7},{2,4},{3,5},{4,2},{5,3},{6,0},{7,1},{8,14},{9,15},{10,... | collective-permute-start | bytes 73736 | tf_op jit(solution)/shard_map/ppermute | solution.py:905
  31.8 3.4 %collective-permute-done.6.refs_7_ = f32[48,128]{1,0:T(8,128)S(1)} collective-permute-done((f32[48,128]{1,0:T(8,128)S(1)}, f32[48,128]{1,0:T(8,128)S(1)}, u32[]{:S(2)}, u32[]{:S(2)}) %collective-permute-start.6) | collective-permute-done | bytes 24608 | tf_op jit(solution)/shard_map/ppermute | solution.py:905
  35.3 2.2 %collective-permute-start.7 = (f32[102,128]{1,0:T(8,128)S(1)}, f32[102,128]{1,0:T(8,128)S(1)}, u32[]{:S(2)}, u32[]{:S(2)}) collective-permute-start(f32[102,128]{1,0:T(8,128)S(1)} %get-tuple-element.91), channel_id=1, source_target_pairs={{0,24},{1,17},{2,26},{3,19},{4,28},{5,21},{6,30},{7,23},{8,16},{9,... | collective-permute-start | bytes 156680 | tf_op jit(solution)/shard_map/ppermute | solution.py:828
  37.5 2.3 %collective-permute-start.9 = (f32[102,128]{1,0:T(8,128)S(1)}, f32[102,128]{1,0:T(8,128)S(1)}, u32[]{:S(2)}, u32[]{:S(2)}) collective-permute-start(f32[102,128]{1,0:T(8,128)S(1)} %get-tuple-element.93), channel_id=1, source_target_pairs={{0,16},{1,9},{2,18},{3,11},{4,20},{5,13},{6,22},{7,15},{8,24},{9,1... | collective-permute-start | bytes 156680 | tf_op jit(solution)/shard_map/ppermute | solution.py:828
  39.8 1.6 %collective-permute-done.7.refs_1_ = f32[102,128]{1,0:T(8,128)S(1)} collective-permute-done((f32[102,128]{1,0:T(8,128)S(1)}, f32[102,128]{1,0:T(8,128)S(1)}, u32[]{:S(2)}, u32[]{:S(2)}) %collective-permute-start.7) | collective-permute-done | bytes 52256 | tf_op jit(solution)/shard_map/ppermute | solution.py:828
  41.4 0.5 %collective-permute-done.8.refs_2_ = f32[102,128]{1,0:T(8,128)S(1)} collective-permute-done((f32[102,128]{1,0:T(8,128)S(1)}, f32[102,128]{1,0:T(8,128)S(1)}, u32[]{:S(2)}, u32[]{:S(2)}) %collective-permute-start.8) | collective-permute-done | bytes 52256 | tf_op jit(solution)/shard_map/ppermute | solution.py:828
  41.9 0.6 %collective-permute-done.9.refs_3_ = f32[102,128]{1,0:T(8,128)S(1)} collective-permute-done((f32[102,128]{1,0:T(8,128)S(1)}, f32[102,128]{1,0:T(8,128)S(1)}, u32[]{:S(2)}, u32[]{:S(2)}) %collective-permute-start.9) | collective-permute-done | bytes 52256 | tf_op jit(solution)/shard_map/ppermute | solution.py:828
  42.6 1.4 %sweeps.1 = f32[4,256]{1,0:T(4,128)} custom-call(f32[102,128]{1,0:T(8,128)S(1)} %get-tuple-element.90.refs_0_, f32[102,128]{1,0:T(8,128)S(1)} %collective-permute-done.7.refs_1_, f32[102,128]{1,0:T(8,128)S(1)} %collective-permute-done.8.refs_2_, f32[102,128]{1,0:T(8,128)S(1)} %collective-permute-done.9.refs_3_), custom_call_target="tpu_custom_call" | custom-call | bytes 7200000 | tf_op jit(solution)/shard_map/sweeps/pallas_call | solution.py:915
  (20 shorter events, 0.4 us)
Async XLA Ops:
  0.6 8.9 %copy-start = (f32[5,64,512]{2,1,0:T(8,128)S(1)}, f32[5,64,512]{2,1,0:T(8,128)}, u32[]{:S(2)}) copy-start(f32[5,64,512]{2,1,0:T(8,128)} %star_ref.3) | copy-start | bytes 1966084
  2.1 7.4 %copy-start.5 = (s32[5,4,64]{2,1,0:T(4,128)S(1)}, s32[5,4,64]{2,1,0:T(4,128)}, u32[]{:S(2)}) copy-start(s32[5,4,64]{2,1,0:T(4,128)} %get-tuple-element.49.facts_ref) | copy-start | bytes 15364
  2.1 15.5 %all-to-all-start = ((f32[32,4,256]{2,1,0:T(4,128)}), f32[32,4,256]{2,1,0:T(4,128)S(1)}, u32[]{:S(2)}, u32[]{:S(2)}) async-start(f32[32,4,256]{2,1,0:T(4,128)} %get-tuple-element.57), calls=%async_computation | async-start | bytes 262144 | tf_op jit(solution)/shard_map/all_to_all | solution.py:860
  9.4 1.0 %copy-start.1 = (f32[4,64,512]{2,1,0:T(8,128)S(1)}, f32[4,64,512]{2,1,0:T(8,128)}, u32[]{:S(2)}) copy-start(f32[4,64,512]{2,1,0:T(8,128)} %axis_ref.1) | copy-start | bytes 1572868
  9.5 1.0 %copy-start.2 = (f32[64,512]{1,0:T(8,128)S(1)}, f32[64,512]{1,0:T(8,128)}, u32[]{:S(2)}) copy-start(f32[64,512]{1,0:T(8,128)} %phase_ref.1) | copy-start | bytes 393220
  9.5 1.0 %copy-start.3 = (s32[64,512]{1,0:T(8,128)S(1)}, s32[64,512]{1,0:T(8,128)}, u32[]{:S(2)}) copy-start(s32[64,512]{1,0:T(8,128)} %offset_ref.1) | copy-start | bytes 393220
  10.6 7.3 %copy-start.4 = (f32[64,512]{1,0:T(8,128)S(1)}, f32[64,512]{1,0:T(8,128)}, u32[]{:S(2)}) copy-start(f32[64,512]{1,0:T(8,128)} %observed_ref.1) | copy-start | bytes 393220
  17.7 3.0 %collective-permute-start = (f32[1440,128]{1,0:T(8,128)S(1)}, f32[1440,128]{1,0:T(8,128)S(1)}, u32[]{:S(2)}, u32[]{:S(2)}) collective-permute-start(f32[1440,128]{1,0:T(8,128)S(1)} %get-tuple-element.59), channel_id=1, source_target_pairs={{0,1},{1,0},{2,3},{3,2},{4,5},{5,4},{6,7},{7,6},{8,9},{9,8},{10,11... | collective-permute-start | bytes 2211848 | tf_op jit(solution)/shard_map/ppermute | solution.py:834
  20.9 7.3 %collective-permute-start.1 = (f32[360,128]{1,0:T(8,128)S(1)}, f32[360,128]{1,0:T(8,128)S(1)}, u32[]{:S(2)}, u32[]{:S(2)}) collective-permute-start(f32[360,128]{1,0:T(8,128)S(1)} %get-tuple-element.73), channel_id=1, source_target_pairs={{0,2},{1,5},{2,0},{3,7},{4,6},{5,1},{6,4},{7,3},{8,10},{9,13},{10,... | collective-permute-start | bytes 552968 | tf_op jit(solution)/shard_map/ppermute | solution.py:834
  21.3 6.9 %collective-permute-start.2 = (f32[360,128]{1,0:T(8,128)S(1)}, f32[360,128]{1,0:T(8,128)S(1)}, u32[]{:S(2)}, u32[]{:S(2)}) collective-permute-start(f32[360,128]{1,0:T(8,128)S(1)} %get-tuple-element.75), channel_id=1, source_target_pairs={{0,4},{1,3},{2,6},{3,1},{4,0},{5,7},{6,2},{7,5},{8,12},{9,11},{10,... | collective-permute-start | bytes 552968 | tf_op jit(solution)/shard_map/ppermute | solution.py:834
  26.2 1.4 %collective-permute-start.3 = (f32[192,128]{1,0:T(8,128)S(1)}, f32[192,128]{1,0:T(8,128)S(1)}, u32[]{:S(2)}, u32[]{:S(2)}) collective-permute-start(f32[192,128]{1,0:T(8,128)S(1)} %get-tuple-element.77), channel_id=1, source_target_pairs={{0,1},{1,0},{2,3},{3,2},{4,5},{5,4},{6,7},{7,6},{8,9},{9,8},{10,11... | collective-permute-start | bytes 294920 | tf_op jit(solution)/shard_map/ppermute | solution.py:834
  28.3 7.0 %collective-permute-start.4 = (f32[228,128]{1,0:T(8,128)S(1)}, f32[228,128]{1,0:T(8,128)S(1)}, u32[]{:S(2)}, u32[]{:S(2)}) collective-permute-start(f32[228,128]{1,0:T(8,128)S(1)} %get-tuple-element.85), channel_id=1, source_target_pairs={{0,4},{1,3},{2,6},{3,1},{4,0},{5,7},{6,2},{7,5},{8,12},{9,11},{10,... | collective-permute-start | bytes 350216 | tf_op jit(solution)/shard_map/ppermute | solution.py:834
  28.8 6.4 %collective-permute-start.5 = (f32[228,128]{1,0:T(8,128)S(1)}, f32[228,128]{1,0:T(8,128)S(1)}, u32[]{:S(2)}, u32[]{:S(2)}) collective-permute-start(f32[228,128]{1,0:T(8,128)S(1)} %get-tuple-element.87), channel_id=1, source_target_pairs={{0,2},{1,5},{2,0},{3,7},{4,6},{5,1},{6,4},{7,3},{8,10},{9,13},{10,... | collective-permute-start | bytes 350216 | tf_op jit(solution)/shard_map/ppermute | solution.py:834
  30.5 4.7 %collective-permute-start.6 = (f32[48,128]{1,0:T(8,128)S(1)}, f32[48,128]{1,0:T(8,128)S(1)}, u32[]{:S(2)}, u32[]{:S(2)}) collective-permute-start(f32[48,128]{1,0:T(8,128)S(1)} %get-tuple-element.89), channel_id=1, source_target_pairs={{0,6},{1,7},{2,4},{3,5},{4,2},{5,3},{6,0},{7,1},{8,14},{9,15},{10,... | collective-permute-start | bytes 73736 | tf_op jit(solution)/shard_map/ppermute | solution.py:905
  35.3 6.0 %collective-permute-start.7 = (f32[102,128]{1,0:T(8,128)S(1)}, f32[102,128]{1,0:T(8,128)S(1)}, u32[]{:S(2)}, u32[]{:S(2)}) collective-permute-start(f32[102,128]{1,0:T(8,128)S(1)} %get-tuple-element.91), channel_id=1, source_target_pairs={{0,24},{1,17},{2,26},{3,19},{4,28},{5,21},{6,30},{7,23},{8,16},{9,... | collective-permute-start | bytes 156680 | tf_op jit(solution)/shard_map/ppermute | solution.py:828
  37.5 4.4 %collective-permute-start.8 = (f32[102,128]{1,0:T(8,128)S(1)}, f32[102,128]{1,0:T(8,128)S(1)}, u32[]{:S(2)}, u32[]{:S(2)}) collective-permute-start(f32[102,128]{1,0:T(8,128)S(1)} %get-tuple-element.92), channel_id=1, source_target_pairs={{0,8},{1,25},{2,10},{3,27},{4,12},{5,29},{6,14},{7,31},{8,0},{9,17... | collective-permute-start | bytes 156680 | tf_op jit(solution)/shard_map/ppermute | solution.py:828
  37.5 5.0 %collective-permute-start.9 = (f32[102,128]{1,0:T(8,128)S(1)}, f32[102,128]{1,0:T(8,128)S(1)}, u32[]{:S(2)}, u32[]{:S(2)}) collective-permute-start(f32[102,128]{1,0:T(8,128)S(1)} %get-tuple-element.93), channel_id=1, source_target_pairs={{0,16},{1,9},{2,18},{3,11},{4,20},{5,13},{6,22},{7,15},{8,24},{9,1... | collective-permute-start | bytes 156680 | tf_op jit(solution)/shard_map/ppermute | solution.py:828

commit v8 on v7

--- a/solution.py
+++ b/solution.py
@@ -229,17 +229,19 @@
         total[start : start + 8, :] = total[stop - 16 : stop - 8, :]
         total[stop - 8 : stop, :] = total[start + 8 : start + 16, :]
     mine = lax.axis_index(axes) & 1
-    half = kept_ref.shape[0] // ROWS * 8
+    count = len(places) // 2
+    chunk = kept_ref.shape[0] // count
+    filler = jnp.zeros((chunk - spread * ROWS, LANES), jnp.float32)
 
     def pack(index, carry):
-        target = pl.multiple_of(index * 8 * ROWS, 8)
+        target = pl.ds(pl.multiple_of(index * chunk, 8), chunk)
         for out_ref, part in ((kept_ref, mine), (sent_ref, 1 - mine)):
-            source = pl.multiple_of(part * half + index * 64, 64)
-            for j in range(8):
-                out_ref[pl.ds(target + j * ROWS, ROWS), :] = total[pl.ds(source + j * 8, ROWS), :]
+            source = pl.multiple_of((part * count + index) * spread * 8, 8)
+            pieces = [total[pl.ds(source + j * 8, 8), :][0:ROWS] for j in range(spread)]
+            out_ref[target, :] = jnp.concatenate(pieces + [filler], axis=0)
         return carry
 
-    lax.fori_loop(0, half // 64, pack, 0)
+    lax.fori_loop(0, count, pack, 0)
 
 
 ENTRIES = tuple((row, column) for row in range(5) for column in range(row + 1))
@@ -440,18 +442,22 @@
         total[start : start + 8, :] = opening + jnp.where(lanes_block == 0, ending, 0.0)
         total[stop - 8 : stop, :] = ending + jnp.where(lanes_block == 1, opening, 0.0)
     mine = lax.axis_index(axes) & 1
-    half = kept_ref.shape[0] * 2
+    count = len(places) // 2
+    chunk = kept_ref.shape[0] // count
+    filler = jnp.zeros((chunk - rows // 2, LANES), jnp.float32)
 
     def pack(index, carry):
-        target = pl.multiple_of(index * 8, 8)
+        target = pl.ds(pl.multiple_of(index * chunk, 8), chunk)
         for out_ref, part in ((kept_ref, mine), (sent_ref, 1 - mine)):
-            source = pl.multiple_of(part * half + index * 16, 16)
-            for j in range(2):
-                tile = total[pl.ds(source + j * 8, 8), :]
-                out_ref[pl.ds(target + j * 4, 4), :] = tile[0:4] + tile[4:8]
+            source = pl.multiple_of((part * count + index) * rows, 8)
+            tiles = [total[pl.ds(source + j, 8), :] for j in range(0, rows, 8)]
+            pieces = [tile[0:4] + tile[4:8] for tile in tiles]
+            if filler.shape[0]:
+                pieces.append(filler)
+            out_ref[target, :] = jnp.concatenate(pieces, axis=0)
         return carry
 
-    lax.fori_loop(0, half // 16, pack, 0)
+    lax.fori_loop(0, count, pack, 0)
     result_copy.wait()
 
 
@@ -464,20 +470,25 @@
 
 
 def add_rows(out_ref, base, inputs, start, rows):
-    step = 40 if rows % 40 == 0 else rows
+    step = 64 if rows % 64 == 0 else rows
 
     def add(index, carry):
-        terms = [ref[pl.ds(offset + start + index * step, step), :] for ref, offset in inputs]
+        first = pl.multiple_of(start + index * step, 8)
+        terms = [ref[pl.ds(first + offset, step), :] for ref, offset in inputs]
         added = terms[0]
         for term in terms[1:]:
             added = added + term
-        out_ref[pl.ds(base + index * step, step), :] = added
+        out_ref[pl.ds(pl.multiple_of(base + index * step, 8), step), :] = added
         return carry
 
     if step == rows:
         add(0, 0)
     else:
         lax.fori_loop(0, rows // step, add, 0)
+
+
+def whole_tiles(rows):
+    return (rows + 7) // 8 * 8
 
 
 def order_of(members):
@@ -605,7 +616,7 @@
         operator[shift] = operator[shift] - jnp.where(same, smoothing, 0.0)
     own = jnp.concatenate(
         [
-            band_ref[spread * ROWS + tile * 4 : spread * ROWS + (tile + 1) * 4, :]
+            band_ref[whole_tiles(spread * ROWS) + tile * 4 :, :][0:4]
             for tile in range(tiles)
         ],
         axis=1,
@@ -680,7 +691,7 @@
 def call_clear():
     return pl.pallas_call(
         clear_kernel,
-        out_shape=jax.ShapeDtypeStruct((UNROLL, 8 * 16, LANES), jnp.float32),
+        out_shape=jax.ShapeDtypeStruct((UNROLL, 9 * 16, LANES), jnp.float32),
         out_specs=in_vmem(1)[0],
         compiler_params=params(),
         cost_estimate=work(200),
@@ -690,7 +701,7 @@
 
 def call_normals(axes, facts, factors, phase, knot_offset, partials, clear, devices, spread):
     f32 = jnp.float32
-    half = jax.ShapeDtypeStruct((devices // 2 * spread * ROWS, LANES), f32)
+    half = jax.ShapeDtypeStruct((devices // 2 * whole_tiles(spread * ROWS), LANES), f32)
     blocks = devices * spread
     return pl.pallas_call(
         functools.partial(normal_kernel, axes),
@@ -700,7 +711,7 @@
         out_specs=in_vmem(6),
         scratch_shapes=[
             pltpu.VMEM((blocks * 8, LANES), f32),
-            pltpu.VMEM((UNROLL, 8 * 16, LANES), f32),
+            pltpu.VMEM((UNROLL, 9 * 16, LANES), f32),
             pltpu.VMEM((UNROLL, 16, 8, LANES), f32),
             pltpu.VMEM((UNROLL, 8, LANES), jnp.int32),
             pltpu.SMEM(facts.shape, jnp.int32),
@@ -785,7 +796,7 @@
         in_specs=in_smem(1) + in_vmem(7),
         out_specs=in_vmem(2),
         scratch_shapes=[
-            pltpu.VMEM((transits // 8, 32, LANES), f32),
+            pltpu.VMEM((transits // 8, 40, LANES), f32),
             pltpu.VMEM((5, 8, LANES), f32),
         ],
         compiler_params=params(),
@@ -797,7 +808,7 @@
 def call_gradients(axes, facts, phase, knot_offset, partials, second, step, devices, spread):
     f32 = jnp.float32
     tiles = (spread + 7) // 8
-    half = jax.ShapeDtypeStruct((devices // 2 * tiles * 4, LANES), f32)
+    half = jax.ShapeDtypeStruct((devices // 2 * whole_tiles(tiles * 4), LANES), f32)
     return pl.pallas_call(
         functools.partial(gradient_kernel, axes),
         out_shape=[half, half, jax.ShapeDtypeStruct(step.shape, f32)],
@@ -805,7 +816,7 @@
         out_specs=in_vmem(2) + [pl.BlockSpec(memory_space=pltpu.HBM)],
         scratch_shapes=[
             pltpu.VMEM((devices * tiles * 8, LANES), f32),
-            pltpu.VMEM((UNROLL, 8 * 16, LANES), f32),
+            pltpu.VMEM((UNROLL, 9 * 16, LANES), f32),
             pltpu.VMEM((UNROLL, 4, 8, LANES), f32),
             pltpu.VMEM((UNROLL, 8, LANES), jnp.int32),
             pltpu.SMEM(facts.shape, jnp.int32),
@@ -862,7 +873,7 @@
     later = [bits[start : start + 2] for start in range(3, len(bits), 2)]
     groups = [bits[:1], bits[1:3]] + later
     final = later[-1]
-    chunks = (spread * ROWS, tiles * 4)
+    chunks = (whole_tiles(spread * ROWS), whole_tiles(tiles * 4))
 
     def rows(kind, group):
         return chunks[kind] * (devices >> (group[-1] + 1))

time: 44.2 us -> 44.7 us (1.011)
  waiting for transfers between devices: 10.4 us -> 11.1 us
  transfers between devices with their start and end apart: 11 -> 11, of which waited for: 7 -> 6; matrix products, arithmetic and copies ran while one was open for 0% -> 0% of each run, Pallas kernels for 28% -> 27%
where the time goes in v8:
time: 44.7 us; the launch traced here: 44.5 us
  starting transfers between devices  16.9 us (38%)
  Pallas kernels  15.2 us (34%)
  waiting for transfers between devices  11.1 us (25%)
  between operations  0.78 us (2%)
  local copies, waits for them, and re-layouts  0.5 us (1%)
    all_to_all x1, starting transfers between devices, per_device(): whole = lax.all_to_all(wide, axes, split_axis=0, concat_axis=0, tiled=True)  7.3 us
    pallas_call x1, Pallas kernels, call_normals(): pl.pallas_call(functools.partial(normal_kernel, axes), out_shape=[half, h...  4.69 us
    ppermute x3, starting transfers between devices, swap(): arrived.append(lax.ppermute(array, axes, pairs))  4.45 us
    pallas_call x1, Pallas kernels, call_gradients(): pl.pallas_call(functools.partial(gradient_kernel, axes), out_shape=[half,...  3.92 us
    ppermute x1, waiting for transfers between devices, per_device(): third = lax.ppermute(sent[2], axes, [(i, i ^ 6) for i in range(devices)])  3.62 us
    ppermute x6, starting transfers between devices, hop(): return lax.ppermute(array, axes, pairs)  3.58 us
    ppermute x3, waiting for transfers between devices, swap(): arrived.append(lax.ppermute(array, axes, pairs))  2.82 us
    pallas_call x1, Pallas kernels, call_stars(): pl.pallas_call(star_kernel, out_shape=[jax.ShapeDtypeStruct((5, stars), f...  2.78 us
  transfers between devices with their start and end apart: 11, of which 6 were waited for; matrix products, arithmetic and copies ran while one was open for 0% of the time, Pallas kernels for 27%

profile of v8, /device:TPU:0, one launch (start us, length us, event | category | flops | bytes accessed | tf_op | source)
XLA Modules:
  0.0 44.5 jit_solution(18391793921336392103)
XLA Ops:
  0.6 1.5 %facts.1 = (s32[5,4,64]{2,1,0:T(4,128)}, f32[32,4,256]{2,1,0:T(4,128)}) custom-call(s32[4]{0:T(128)} %counts.1, f32[4,256]{1,0:T(4,128)} %attitude_ref.1, s32[4,64]{1,0:T(4,128)} %bitcast.1, s32[4,64]{1,0:T(4,128)} %slots_ref.1), custom_call_target="tpu_custom_call" | custom-call | bytes 3600000 | tf_op jit(solution)/shard_map/facts/pallas_call | solution.py:677
  2.1 7.3 %all-to-all-start = ((f32[32,4,256]{2,1,0:T(4,128)}), f32[32,4,256]{2,1,0:T(4,128)S(1)}, u32[]{:S(2)}, u32[]{:S(2)}) async-start(f32[32,4,256]{2,1,0:T(4,128)} %get-tuple-element.57), calls=%async_computation | async-start | bytes 262144 | tf_op jit(solution)/shard_map/all_to_all | solution.py:871
  9.5 0.5 %factors.1.factors_ref = f32[15,8,128]{2,1,0:T(8,128)S(1)} custom-call(s32[5,4,64]{2,1,0:T(4,128)S(1)} %copy-done.5, f32[5,64,512]{2,1,0:T(8,128)S(1)} %copy-done), custom_call_target="tpu_custom_call" | custom-call | bytes 720000000 | tf_op jit(solution)/shard_map/factors/pallas_call | solution.py:775
  10.1 0.4 copy-done.1
  10.6 4.7 %normals.1 = (f32[1536,128]{1,0:T(8,128)S(1)}, f32[1536,128]{1,0:T(8,128)S(1)}, s32[5,4,64]{2,1,0:T(4,128)S(1)}, f32[64,512]{1,0:T(8,128)S(1)}, s32[64,512]{1,0:T(8,128)S(1)}, /*index=5*/f32[4,64,512]{2,1,0:T(8,128)S(1)}) custom-call(s32[5,4,64]{2,1,0:T(4,128)S(1)} %copy-done.5, f32[15,8,128]{2,1,0:T(8,128)S(1)} %factors.1.factors_ref, ...), custom_call_target="tpu_custom_call" | custom-call | bytes 360000000 | tf_op jit(solution)/shard_map/normals/pallas_call | solution.py:706
  15.2 2.4 %all-to-all-done.attitude_ref = f32[32,4,256]{2,1,0:T(4,128)S(1)} async-done(((f32[32,4,256]{2,1,0:T(4,128)}), f32[32,4,256]{2,1,0:T(4,128)S(1)}, u32[]{:S(2)}, u32[]{:S(2)}) %all-to-all-start) | async-done | bytes 131104 | tf_op jit(solution)/shard_map/all_to_all | solution.py:871
  17.7 0.2 collective-permute-start
  17.9 2.8 %stars.1 = (f32[5,512]{1,0:T(8,128)S(1)}, f32[64,512]{1,0:T(8,128)S(1)}) custom-call(s32[5,4,64]{2,1,0:T(4,128)S(1)} %get-tuple-element.51.facts.facts_ref, f32[32,4,256]{2,1,0:T(4,128)S(1)} %all-to-all-done.attitude_ref, f32[15,8,128]{2,1,0:T(8,128)S(1)} %factors.1.factors_ref, f32[64,512]{1,0:T(8,128)S(1)} %get-tuple-element.52.phase_ref, ...), custom_call_target="tpu_custom_call" | custom-call | bytes 18000000 | tf_op jit(solution)/shard_map/stars/pallas_call | solution.py:790
  20.7 0.2 halves.1
  20.9 0.4 collective-permute-start.1
  21.3 0.9 %collective-permute-start.2 = (f32[384,128]{1,0:T(8,128)S(1)}, f32[384,128]{1,0:T(8,128)S(1)}, u32[]{:S(2)}, u32[]{:S(2)}) collective-permute-start(f32[384,128]{1,0:T(8,128)S(1)} %get-tuple-element.75), channel_id=1, source_target_pairs={{0,4},{1,3},{2,6},{3,1},{4,0},{5,7},{6,2},{7,5},{8,12},{9,11},{10,... | collective-permute-start | bytes 589832 | tf_op jit(solution)/shard_map/ppermute | solution.py:845
  22.2 3.9 %gradients.1 = (f32[256,128]{1,0:T(8,128)S(1)}, f32[256,128]{1,0:T(8,128)S(1)}, f32[5,512]{1,0:T(8,128)}) custom-call(s32[5,4,64]{2,1,0:T(4,128)S(1)} %get-tuple-element.51.facts.facts_ref, f32[64,512]{1,0:T(8,128)S(1)} %get-tuple-element.52.phase_ref, s32[64,512]{1,0:T(8,128)S(1)} %get-tuple-element.53.offset_ref, ...), custom_call_target="tpu_custom_call" | custom-call | bytes 18000000 | tf_op jit(solution)/shard_map/gradients/pallas_call | solution.py:812
  26.2 1.3 %collective-permute-done.3.refs_5_ = f32[256,128]{1,0:T(8,128)S(1)} collective-permute-done((f32[256,128]{1,0:T(8,128)S(1)}, f32[256,128]{1,0:T(8,128)S(1)}, u32[]{:S(2)}, u32[]{:S(2)}) %collective-permute-start.3) | collective-permute-done | bytes 131104 | tf_op jit(solution)/shard_map/ppermute | solution.py:845
  27.5 0.9 %collective-permute-done.1.refs_1_ = f32[384,128]{1,0:T(8,128)S(1)} collective-permute-done((f32[384,128]{1,0:T(8,128)S(1)}, f32[384,128]{1,0:T(8,128)S(1)}, u32[]{:S(2)}, u32[]{:S(2)}) %collective-permute-start.1) | collective-permute-done | bytes 196640 | tf_op jit(solution)/shard_map/ppermute | solution.py:845
  28.4 0.1 meet.1
  28.5 0.3 collective-permute-start.4
  28.9 1.7 %collective-permute-start.5 = (f32[256,128]{1,0:T(8,128)S(1)}, f32[256,128]{1,0:T(8,128)S(1)}, u32[]{:S(2)}, u32[]{:S(2)}) collective-permute-start(f32[256,128]{1,0:T(8,128)S(1)} %get-tuple-element.87), channel_id=1, source_target_pairs={{0,2},{1,5},{2,0},{3,7},{4,6},{5,1},{6,4},{7,3},{8,10},{9,13},{10,... | collective-permute-start | bytes 393224 | tf_op jit(solution)/shard_map/ppermute | solution.py:845
  30.5 1.5 %collective-permute-start.6 = (f32[64,128]{1,0:T(8,128)S(1)}, f32[64,128]{1,0:T(8,128)S(1)}, u32[]{:S(2)}, u32[]{:S(2)}) collective-permute-start(f32[64,128]{1,0:T(8,128)S(1)} %get-tuple-element.89), channel_id=1, source_target_pairs={{0,6},{1,7},{2,4},{3,5},{4,2},{5,3},{6,0},{7,1},{8,14},{9,15},{10,... | collective-permute-start | bytes 98312 | tf_op jit(solution)/shard_map/ppermute | solution.py:916
  32.1 3.6 %collective-permute-done.6.refs_7_ = f32[64,128]{1,0:T(8,128)S(1)} collective-permute-done((f32[64,128]{1,0:T(8,128)S(1)}, f32[64,128]{1,0:T(8,128)S(1)}, u32[]{:S(2)}, u32[]{:S(2)}) %collective-permute-start.6) | collective-permute-done | bytes 32800 | tf_op jit(solution)/shard_map/ppermute | solution.py:916
  35.8 2.0 %collective-permute-start.7 = (f32[112,128]{1,0:T(8,128)S(1)}, f32[112,128]{1,0:T(8,128)S(1)}, u32[]{:S(2)}, u32[]{:S(2)}) collective-permute-start(f32[112,128]{1,0:T(8,128)S(1)} %get-tuple-element.91), channel_id=1, source_target_pairs={{0,24},{1,17},{2,26},{3,19},{4,28},{5,21},{6,30},{7,23},{8,16},{9,... | collective-permute-start | bytes 172040 | tf_op jit(solution)/shard_map/ppermute | solution.py:839
  37.8 2.5 %collective-permute-start.9 = (f32[112,128]{1,0:T(8,128)S(1)}, f32[112,128]{1,0:T(8,128)S(1)}, u32[]{:S(2)}, u32[]{:S(2)}) collective-permute-start(f32[112,128]{1,0:T(8,128)S(1)} %get-tuple-element.93), channel_id=1, source_target_pairs={{0,16},{1,9},{2,18},{3,11},{4,20},{5,13},{6,22},{7,15},{8,24},{9,1... | collective-permute-start | bytes 172040 | tf_op jit(solution)/shard_map/ppermute | solution.py:839
  40.2 1.6 %collective-permute-done.7.refs_1_ = f32[112,128]{1,0:T(8,128)S(1)} collective-permute-done((f32[112,128]{1,0:T(8,128)S(1)}, f32[112,128]{1,0:T(8,128)S(1)}, u32[]{:S(2)}, u32[]{:S(2)}) %collective-permute-start.7) | collective-permute-done | bytes 57376 | tf_op jit(solution)/shard_map/ppermute | solution.py:839
  41.9 1.2 %collective-permute-done.8.refs_2_ = f32[112,128]{1,0:T(8,128)S(1)} collective-permute-done((f32[112,128]{1,0:T(8,128)S(1)}, f32[112,128]{1,0:T(8,128)S(1)}, u32[]{:S(2)}, u32[]{:S(2)}) %collective-permute-start.8) | collective-permute-done | bytes 57376 | tf_op jit(solution)/shard_map/ppermute | solution.py:839
  43.1 1.4 %sweeps.1 = f32[4,256]{1,0:T(4,128)} custom-call(f32[112,128]{1,0:T(8,128)S(1)} %get-tuple-element.90.refs_0_, f32[112,128]{1,0:T(8,128)S(1)} %collective-permute-done.7.refs_1_, f32[112,128]{1,0:T(8,128)S(1)} %collective-permute-done.8.refs_2_, f32[112,128]{1,0:T(8,128)S(1)} %collective-permute-done.9.refs_3_), custom_call_target="tpu_custom_call" | custom-call | bytes 7200000 | tf_op jit(solution)/shard_map/sweeps/pallas_call | solution.py:926
  (20 shorter events, 0.3 us)
Async XLA Ops:
  0.6 8.9 %copy-start = (f32[5,64,512]{2,1,0:T(8,128)S(1)}, f32[5,64,512]{2,1,0:T(8,128)}, u32[]{:S(2)}) copy-start(f32[5,64,512]{2,1,0:T(8,128)} %star_ref.3) | copy-start | bytes 1966084
  2.1 7.4 %copy-start.5 = (s32[5,4,64]{2,1,0:T(4,128)S(1)}, s32[5,4,64]{2,1,0:T(4,128)}, u32[]{:S(2)}) copy-start(s32[5,4,64]{2,1,0:T(4,128)} %get-tuple-element.49.facts_ref) | copy-start | bytes 15364
  2.1 15.5 %all-to-all-start = ((f32[32,4,256]{2,1,0:T(4,128)}), f32[32,4,256]{2,1,0:T(4,128)S(1)}, u32[]{:S(2)}, u32[]{:S(2)}) async-start(f32[32,4,256]{2,1,0:T(4,128)} %get-tuple-element.57), calls=%async_computation | async-start | bytes 262144 | tf_op jit(solution)/shard_map/all_to_all | solution.py:871
  9.4 1.0 %copy-start.1 = (f32[4,64,512]{2,1,0:T(8,128)S(1)}, f32[4,64,512]{2,1,0:T(8,128)}, u32[]{:S(2)}) copy-start(f32[4,64,512]{2,1,0:T(8,128)} %axis_ref.1) | copy-start | bytes 1572868
  9.5 1.0 %copy-start.2 = (f32[64,512]{1,0:T(8,128)S(1)}, f32[64,512]{1,0:T(8,128)}, u32[]{:S(2)}) copy-start(f32[64,512]{1,0:T(8,128)} %phase_ref.1) | copy-start | bytes 393220
  9.5 1.0 %copy-start.3 = (s32[64,512]{1,0:T(8,128)S(1)}, s32[64,512]{1,0:T(8,128)}, u32[]{:S(2)}) copy-start(s32[64,512]{1,0:T(8,128)} %offset_ref.1) | copy-start | bytes 393220
  10.6 7.3 %copy-start.4 = (f32[64,512]{1,0:T(8,128)S(1)}, f32[64,512]{1,0:T(8,128)}, u32[]{:S(2)}) copy-start(f32[64,512]{1,0:T(8,128)} %observed_ref.1) | copy-start | bytes 393220
  17.7 3.0 %collective-permute-start = (f32[1536,128]{1,0:T(8,128)S(1)}, f32[1536,128]{1,0:T(8,128)S(1)}, u32[]{:S(2)}, u32[]{:S(2)}) collective-permute-start(f32[1536,128]{1,0:T(8,128)S(1)} %get-tuple-element.59), channel_id=1, source_target_pairs={{0,1},{1,0},{2,3},{3,2},{4,5},{5,4},{6,7},{7,6},{8,9},{9,8},{10,11... | collective-permute-start | bytes 2359304 | tf_op jit(solution)/shard_map/ppermute | solution.py:845
  20.9 7.5 %collective-permute-start.1 = (f32[384,128]{1,0:T(8,128)S(1)}, f32[384,128]{1,0:T(8,128)S(1)}, u32[]{:S(2)}, u32[]{:S(2)}) collective-permute-start(f32[384,128]{1,0:T(8,128)S(1)} %get-tuple-element.73), channel_id=1, source_target_pairs={{0,2},{1,5},{2,0},{3,7},{4,6},{5,1},{6,4},{7,3},{8,10},{9,13},{10,... | collective-permute-start | bytes 589832 | tf_op jit(solution)/shard_map/ppermute | solution.py:845
  21.3 7.1 %collective-permute-start.2 = (f32[384,128]{1,0:T(8,128)S(1)}, f32[384,128]{1,0:T(8,128)S(1)}, u32[]{:S(2)}, u32[]{:S(2)}) collective-permute-start(f32[384,128]{1,0:T(8,128)S(1)} %get-tuple-element.75), channel_id=1, source_target_pairs={{0,4},{1,3},{2,6},{3,1},{4,0},{5,7},{6,2},{7,5},{8,12},{9,11},{10,... | collective-permute-start | bytes 589832 | tf_op jit(solution)/shard_map/ppermute | solution.py:845
  26.1 1.4 %collective-permute-start.3 = (f32[256,128]{1,0:T(8,128)S(1)}, f32[256,128]{1,0:T(8,128)S(1)}, u32[]{:S(2)}, u32[]{:S(2)}) collective-permute-start(f32[256,128]{1,0:T(8,128)S(1)} %get-tuple-element.77), channel_id=1, source_target_pairs={{0,1},{1,0},{2,3},{3,2},{4,5},{5,4},{6,7},{7,6},{8,9},{9,8},{10,11... | collective-permute-start | bytes 393224 | tf_op jit(solution)/shard_map/ppermute | solution.py:845
  28.5 7.2 %collective-permute-start.4 = (f32[256,128]{1,0:T(8,128)S(1)}, f32[256,128]{1,0:T(8,128)S(1)}, u32[]{:S(2)}, u32[]{:S(2)}) collective-permute-start(f32[256,128]{1,0:T(8,128)S(1)} %get-tuple-element.85), channel_id=1, source_target_pairs={{0,4},{1,3},{2,6},{3,1},{4,0},{5,7},{6,2},{7,5},{8,12},{9,11},{10,... | collective-permute-start | bytes 393224 | tf_op jit(solution)/shard_map/ppermute | solution.py:845
  28.9 6.8 %collective-permute-start.5 = (f32[256,128]{1,0:T(8,128)S(1)}, f32[256,128]{1,0:T(8,128)S(1)}, u32[]{:S(2)}, u32[]{:S(2)}) collective-permute-start(f32[256,128]{1,0:T(8,128)S(1)} %get-tuple-element.87), channel_id=1, source_target_pairs={{0,2},{1,5},{2,0},{3,7},{4,6},{5,1},{6,4},{7,3},{8,10},{9,13},{10,... | collective-permute-start | bytes 393224 | tf_op jit(solution)/shard_map/ppermute | solution.py:845
  30.5 5.2 %collective-permute-start.6 = (f32[64,128]{1,0:T(8,128)S(1)}, f32[64,128]{1,0:T(8,128)S(1)}, u32[]{:S(2)}, u32[]{:S(2)}) collective-permute-start(f32[64,128]{1,0:T(8,128)S(1)} %get-tuple-element.89), channel_id=1, source_target_pairs={{0,6},{1,7},{2,4},{3,5},{4,2},{5,3},{6,0},{7,1},{8,14},{9,15},{10,... | collective-permute-start | bytes 98312 | tf_op jit(solution)/shard_map/ppermute | solution.py:916
  35.8 6.1 %collective-permute-start.7 = (f32[112,128]{1,0:T(8,128)S(1)}, f32[112,128]{1,0:T(8,128)S(1)}, u32[]{:S(2)}, u32[]{:S(2)}) collective-permute-start(f32[112,128]{1,0:T(8,128)S(1)} %get-tuple-element.91), channel_id=1, source_target_pairs={{0,24},{1,17},{2,26},{3,19},{4,28},{5,21},{6,30},{7,23},{8,16},{9,... | collective-permute-start | bytes 172040 | tf_op jit(solution)/shard_map/ppermute | solution.py:839
  37.8 5.3 %collective-permute-start.8 = (f32[112,128]{1,0:T(8,128)S(1)}, f32[112,128]{1,0:T(8,128)S(1)}, u32[]{:S(2)}, u32[]{:S(2)}) collective-permute-start(f32[112,128]{1,0:T(8,128)S(1)} %get-tuple-element.92), channel_id=1, source_target_pairs={{0,8},{1,25},{2,10},{3,27},{4,12},{5,29},{6,14},{7,31},{8,0},{9,17... | collective-permute-start | bytes 172040 | tf_op jit(solution)/shard_map/ppermute | solution.py:839
  37.8 5.3 %collective-permute-start.9 = (f32[112,128]{1,0:T(8,128)S(1)}, f32[112,128]{1,0:T(8,128)S(1)}, u32[]{:S(2)}, u32[]{:S(2)}) collective-permute-start(f32[112,128]{1,0:T(8,128)S(1)} %get-tuple-element.93), channel_id=1, source_target_pairs={{0,16},{1,9},{2,18},{3,11},{4,20},{5,13},{6,22},{7,15},{8,24},{9,1... | collective-permute-start | bytes 172040 | tf_op jit(solution)/shard_map/ppermute | solution.py:839

commit v9 on v8

--- a/solution.py
+++ b/solution.py
@@ -523,6 +523,35 @@
         base += rows
 
 
+def final_kernel(axes, group, families, *refs):
+    mine = share_of(axes, group)
+    members = 1 << len(group)
+    odd = lax.axis_index(axes) & 1
+    others = [0] + [jnp.where(odd == 1, second, first) for first, second in zip(*order_of(members))]
+    outputs = refs[-members:]
+    for other, out_ref in zip(others, outputs):
+        which = mine ^ other
+        pieces = []
+        first = 0
+        for offsets, rows, valid in families:
+            within = members // len(offsets)
+            parts = []
+            for begins in offsets:
+                inputs = list(zip(refs[first : first + len(begins)], begins))
+                first += len(begins)
+                start = pl.multiple_of((which % within) * rows, 8)
+                terms = [ref[pl.ds(start + offset, rows), :] for ref, offset in inputs]
+                parts.append(functools.reduce(jnp.add, terms))
+            value = parts[0]
+            for number, part in enumerate(parts[1:], start=1):
+                value = jnp.where(which // within == number, part, value)
+            pieces.append(value[0:valid])
+        filler = out_ref.shape[0] - sum(piece.shape[0] for piece in pieces)
+        if filler:
+            pieces.append(jnp.zeros((filler, LANES), jnp.float32))
+        out_ref[...] = jnp.concatenate(pieces, axis=0)
+
+
 def cut_kernel(axes, cuts, count, *refs):
     me = lax.axis_index(axes)
     odd = me & 1
@@ -616,7 +645,7 @@
         operator[shift] = operator[shift] - jnp.where(same, smoothing, 0.0)
     own = jnp.concatenate(
         [
-            band_ref[whole_tiles(spread * ROWS) + tile * 4 :, :][0:4]
+            band_ref[...][spread * ROWS + tile * 4 : spread * ROWS + (tile + 1) * 4]
             for tile in range(tiles)
         ],
         axis=1,
@@ -723,17 +752,23 @@
     )(facts, factors, phase, knot_offset, partials, clear)
 
 
-def call_add(axes, group, families):
+def call_add(axes, group, families, valid=None):
     members = 1 << len(group)
     rows = sum(count for segments, count in families)
+    if valid:
+        rows = whole_tiles(sum(valid))
     out = jax.ShapeDtypeStruct((rows, LANES), jnp.float32)
     arrays = [pair[0] for segments, count in families for segment in segments for pair in segment]
     shapes = [
         ([[begin for array, begin in segment] for segment in segments], count)
         for segments, count in families
     ]
+    kernel = add_kernel
+    if valid:
+        kernel = final_kernel
+        shapes = [(offsets, count, kept) for (offsets, count), kept in zip(shapes, valid)]
     return pl.pallas_call(
-        functools.partial(add_kernel, axes, group, shapes),
+        functools.partial(kernel, axes, group, shapes),
         out_shape=[out] * members,
         in_specs=in_vmem(len(arrays)),
         out_specs=in_vmem(members),
@@ -921,7 +956,7 @@
     for group in later[:-1]:
         normals = advance(normals, 0, group)
     families = [(normals, rows(0, final)), (gradients, rows(1, final))]
-    kept, *sent = call_add(axes, final, families)
+    kept, *sent = call_add(axes, final, families, (spread * ROWS, tiles * 4))
     parts = [kept] + swap(sent, final, axes, devices)
     attitude_step = pl.pallas_call(
         functools.partial(sweep_kernel, spread, axes),

time: 44.7 us -> 44.6 us (level)
  no operation moved by 1% of the time
where the time goes in v9:
time: 44.6 us; the launch traced here: 44.3 us
  starting transfers between devices  16.9 us (38%)
  Pallas kernels  15.2 us (34%)
  waiting for transfers between devices  11 us (25%)
  between operations  0.78 us (2%)
  local copies, waits for them, and re-layouts  0.5 us (1%)
    all_to_all x1, starting transfers between devices, per_device(): whole = lax.all_to_all(wide, axes, split_axis=0, concat_axis=0, tiled=True)  7.3 us
    pallas_call x1, Pallas kernels, call_normals(): pl.pallas_call(functools.partial(normal_kernel, axes), out_shape=[half, h...  4.69 us
    ppermute x3, starting transfers between devices, swap(): arrived.append(lax.ppermute(array, axes, pairs))  4.45 us
    pallas_call x1, Pallas kernels, call_gradients(): pl.pallas_call(functools.partial(gradient_kernel, axes), out_shape=[half,...  3.92 us
    ppermute x1, waiting for transfers between devices, per_device(): third = lax.ppermute(sent[2], axes, [(i, i ^ 6) for i in range(devices)])  3.61 us
    ppermute x6, starting transfers between devices, hop(): return lax.ppermute(array, axes, pairs)  3.58 us
    pallas_call x1, Pallas kernels, call_stars(): pl.pallas_call(star_kernel, out_shape=[jax.ShapeDtypeStruct((5, stars), f...  2.78 us
    ppermute x3, waiting for transfers between devices, swap(): arrived.append(lax.ppermute(array, axes, pairs))  2.69 us
  transfers between devices with their start and end apart: 11, of which 6 were waited for; matrix products, arithmetic and copies ran while one was open for 0% of the time, Pallas kernels for 27%

profile of v9, /device:TPU:0, one launch (start us, length us, event | category | flops | bytes accessed | tf_op | source)
XLA Modules:
  0.0 44.3 jit_solution(17206744084902438149)
XLA Ops:
  0.6 1.5 %facts.1 = (s32[5,4,64]{2,1,0:T(4,128)}, f32[32,4,256]{2,1,0:T(4,128)}) custom-call(s32[4]{0:T(128)} %counts.1, f32[4,256]{1,0:T(4,128)} %attitude_ref.1, s32[4,64]{1,0:T(4,128)} %bitcast.1, s32[4,64]{1,0:T(4,128)} %slots_ref.1), custom_call_target="tpu_custom_call" | custom-call | bytes 3600000 | tf_op jit(solution)/shard_map/facts/pallas_call | solution.py:706
  2.1 7.3 %all-to-all-start = ((f32[32,4,256]{2,1,0:T(4,128)}), f32[32,4,256]{2,1,0:T(4,128)S(1)}, u32[]{:S(2)}, u32[]{:S(2)}) async-start(f32[32,4,256]{2,1,0:T(4,128)} %get-tuple-element.57), calls=%async_computation | async-start | bytes 262144 | tf_op jit(solution)/shard_map/all_to_all | solution.py:906
  9.5 0.5 %factors.1.factors_ref = f32[15,8,128]{2,1,0:T(8,128)S(1)} custom-call(s32[5,4,64]{2,1,0:T(4,128)S(1)} %copy-done.5, f32[5,64,512]{2,1,0:T(8,128)S(1)} %copy-done), custom_call_target="tpu_custom_call" | custom-call | bytes 720000000 | tf_op jit(solution)/shard_map/factors/pallas_call | solution.py:810
  10.1 0.4 copy-done.1
  10.6 4.7 %normals.1 = (f32[1536,128]{1,0:T(8,128)S(1)}, f32[1536,128]{1,0:T(8,128)S(1)}, s32[5,4,64]{2,1,0:T(4,128)S(1)}, f32[64,512]{1,0:T(8,128)S(1)}, s32[64,512]{1,0:T(8,128)S(1)}, /*index=5*/f32[4,64,512]{2,1,0:T(8,128)S(1)}) custom-call(s32[5,4,64]{2,1,0:T(4,128)S(1)} %copy-done.5, f32[15,8,128]{2,1,0:T(8,128)S(1)} %factors.1.factors_ref, ...), custom_call_target="tpu_custom_call" | custom-call | bytes 360000000 | tf_op jit(solution)/shard_map/normals/pallas_call | solution.py:735
  15.3 2.4 %all-to-all-done.attitude_ref = f32[32,4,256]{2,1,0:T(4,128)S(1)} async-done(((f32[32,4,256]{2,1,0:T(4,128)}), f32[32,4,256]{2,1,0:T(4,128)S(1)}, u32[]{:S(2)}, u32[]{:S(2)}) %all-to-all-start) | async-done | bytes 131104 | tf_op jit(solution)/shard_map/all_to_all | solution.py:906
  17.7 0.2 collective-permute-start
  17.9 2.8 %stars.1 = (f32[5,512]{1,0:T(8,128)S(1)}, f32[64,512]{1,0:T(8,128)S(1)}) custom-call(s32[5,4,64]{2,1,0:T(4,128)S(1)} %get-tuple-element.51.facts.facts_ref, f32[32,4,256]{2,1,0:T(4,128)S(1)} %all-to-all-done.attitude_ref, f32[15,8,128]{2,1,0:T(8,128)S(1)} %factors.1.factors_ref, f32[64,512]{1,0:T(8,128)S(1)} %get-tuple-element.52.phase_ref, ...), custom_call_target="tpu_custom_call" | custom-call | bytes 18000000 | tf_op jit(solution)/shard_map/stars/pallas_call | solution.py:825
  20.7 0.2 halves.1
  20.9 0.4 collective-permute-start.1
  21.3 0.9 %collective-permute-start.2 = (f32[384,128]{1,0:T(8,128)S(1)}, f32[384,128]{1,0:T(8,128)S(1)}, u32[]{:S(2)}, u32[]{:S(2)}) collective-permute-start(f32[384,128]{1,0:T(8,128)S(1)} %get-tuple-element.75), channel_id=1, source_target_pairs={{0,4},{1,3},{2,6},{3,1},{4,0},{5,7},{6,2},{7,5},{8,12},{9,11},{10,... | collective-permute-start | bytes 589832 | tf_op jit(solution)/shard_map/ppermute | solution.py:880
  22.2 3.9 %gradients.1 = (f32[256,128]{1,0:T(8,128)S(1)}, f32[256,128]{1,0:T(8,128)S(1)}, f32[5,512]{1,0:T(8,128)}) custom-call(s32[5,4,64]{2,1,0:T(4,128)S(1)} %get-tuple-element.51.facts.facts_ref, f32[64,512]{1,0:T(8,128)S(1)} %get-tuple-element.52.phase_ref, s32[64,512]{1,0:T(8,128)S(1)} %get-tuple-element.53.offset_ref, ...), custom_call_target="tpu_custom_call" | custom-call | bytes 18000000 | tf_op jit(solution)/shard_map/gradients/pallas_call | solution.py:847
  26.2 1.3 %collective-permute-done.3.refs_5_ = f32[256,128]{1,0:T(8,128)S(1)} collective-permute-done((f32[256,128]{1,0:T(8,128)S(1)}, f32[256,128]{1,0:T(8,128)S(1)}, u32[]{:S(2)}, u32[]{:S(2)}) %collective-permute-start.3) | collective-permute-done | bytes 131104 | tf_op jit(solution)/shard_map/ppermute | solution.py:880
  27.5 0.9 %collective-permute-done.1.refs_1_ = f32[384,128]{1,0:T(8,128)S(1)} collective-permute-done((f32[384,128]{1,0:T(8,128)S(1)}, f32[384,128]{1,0:T(8,128)S(1)}, u32[]{:S(2)}, u32[]{:S(2)}) %collective-permute-start.1) | collective-permute-done | bytes 196640 | tf_op jit(solution)/shard_map/ppermute | solution.py:880
  28.4 0.1 meet.1
  28.5 0.3 collective-permute-start.4
  28.9 1.7 %collective-permute-start.5 = (f32[256,128]{1,0:T(8,128)S(1)}, f32[256,128]{1,0:T(8,128)S(1)}, u32[]{:S(2)}, u32[]{:S(2)}) collective-permute-start(f32[256,128]{1,0:T(8,128)S(1)} %get-tuple-element.87), channel_id=1, source_target_pairs={{0,2},{1,5},{2,0},{3,7},{4,6},{5,1},{6,4},{7,3},{8,10},{9,13},{10,... | collective-permute-start | bytes 393224 | tf_op jit(solution)/shard_map/ppermute | solution.py:880
  30.5 1.5 %collective-permute-start.6 = (f32[64,128]{1,0:T(8,128)S(1)}, f32[64,128]{1,0:T(8,128)S(1)}, u32[]{:S(2)}, u32[]{:S(2)}) collective-permute-start(f32[64,128]{1,0:T(8,128)S(1)} %get-tuple-element.89), channel_id=1, source_target_pairs={{0,6},{1,7},{2,4},{3,5},{4,2},{5,3},{6,0},{7,1},{8,14},{9,15},{10,... | collective-permute-start | bytes 98312 | tf_op jit(solution)/shard_map/ppermute | solution.py:951
  32.1 3.6 %collective-permute-done.6.refs_7_ = f32[64,128]{1,0:T(8,128)S(1)} collective-permute-done((f32[64,128]{1,0:T(8,128)S(1)}, f32[64,128]{1,0:T(8,128)S(1)}, u32[]{:S(2)}, u32[]{:S(2)}) %collective-permute-start.6) | collective-permute-done | bytes 32800 | tf_op jit(solution)/shard_map/ppermute | solution.py:951
  35.8 2.0 %collective-permute-start.7 = (f32[104,128]{1,0:T(8,128)S(1)}, f32[104,128]{1,0:T(8,128)S(1)}, u32[]{:S(2)}, u32[]{:S(2)}) collective-permute-start(f32[104,128]{1,0:T(8,128)S(1)} %get-tuple-element.91), channel_id=1, source_target_pairs={{0,24},{1,17},{2,26},{3,19},{4,28},{5,21},{6,30},{7,23},{8,16},{9,... | collective-permute-start | bytes 159752 | tf_op jit(solution)/shard_map/ppermute | solution.py:874
  37.7 2.5 %collective-permute-start.9 = (f32[104,128]{1,0:T(8,128)S(1)}, f32[104,128]{1,0:T(8,128)S(1)}, u32[]{:S(2)}, u32[]{:S(2)}) collective-permute-start(f32[104,128]{1,0:T(8,128)S(1)} %get-tuple-element.93), channel_id=1, source_target_pairs={{0,16},{1,9},{2,18},{3,11},{4,20},{5,13},{6,22},{7,15},{8,24},{9,1... | collective-permute-start | bytes 159752 | tf_op jit(solution)/shard_map/ppermute | solution.py:874
  40.2 1.6 %collective-permute-done.7.refs_1_ = f32[104,128]{1,0:T(8,128)S(1)} collective-permute-done((f32[104,128]{1,0:T(8,128)S(1)}, f32[104,128]{1,0:T(8,128)S(1)}, u32[]{:S(2)}, u32[]{:S(2)}) %collective-permute-start.7) | collective-permute-done | bytes 53280 | tf_op jit(solution)/shard_map/ppermute | solution.py:874
  41.8 1.1 %collective-permute-done.8.refs_2_ = f32[104,128]{1,0:T(8,128)S(1)} collective-permute-done((f32[104,128]{1,0:T(8,128)S(1)}, f32[104,128]{1,0:T(8,128)S(1)}, u32[]{:S(2)}, u32[]{:S(2)}) %collective-permute-start.8) | collective-permute-done | bytes 53280 | tf_op jit(solution)/shard_map/ppermute | solution.py:874
  42.9 1.4 %sweeps.1 = f32[4,256]{1,0:T(4,128)} custom-call(f32[104,128]{1,0:T(8,128)S(1)} %get-tuple-element.90.refs_0_, f32[104,128]{1,0:T(8,128)S(1)} %collective-permute-done.7.refs_1_, f32[104,128]{1,0:T(8,128)S(1)} %collective-permute-done.8.refs_2_, f32[104,128]{1,0:T(8,128)S(1)} %collective-permute-done.9.refs_3_), custom_call_target="tpu_custom_call" | custom-call | bytes 7200000 | tf_op jit(solution)/shard_map/sweeps/pallas_call | solution.py:961
  (20 shorter events, 0.3 us)
Async XLA Ops:
  0.6 8.9 %copy-start = (f32[5,64,512]{2,1,0:T(8,128)S(1)}, f32[5,64,512]{2,1,0:T(8,128)}, u32[]{:S(2)}) copy-start(f32[5,64,512]{2,1,0:T(8,128)} %star_ref.3) | copy-start | bytes 1966084
  2.1 7.4 %copy-start.5 = (s32[5,4,64]{2,1,0:T(4,128)S(1)}, s32[5,4,64]{2,1,0:T(4,128)}, u32[]{:S(2)}) copy-start(s32[5,4,64]{2,1,0:T(4,128)} %get-tuple-element.49.facts_ref) | copy-start | bytes 15364
  2.1 15.5 %all-to-all-start = ((f32[32,4,256]{2,1,0:T(4,128)}), f32[32,4,256]{2,1,0:T(4,128)S(1)}, u32[]{:S(2)}, u32[]{:S(2)}) async-start(f32[32,4,256]{2,1,0:T(4,128)} %get-tuple-element.57), calls=%async_computation | async-start | bytes 262144 | tf_op jit(solution)/shard_map/all_to_all | solution.py:906
  9.4 1.0 %copy-start.1 = (f32[4,64,512]{2,1,0:T(8,128)S(1)}, f32[4,64,512]{2,1,0:T(8,128)}, u32[]{:S(2)}) copy-start(f32[4,64,512]{2,1,0:T(8,128)} %axis_ref.1) | copy-start | bytes 1572868
  9.5 1.0 %copy-start.2 = (f32[64,512]{1,0:T(8,128)S(1)}, f32[64,512]{1,0:T(8,128)}, u32[]{:S(2)}) copy-start(f32[64,512]{1,0:T(8,128)} %phase_ref.1) | copy-start | bytes 393220
  9.5 1.0 %copy-start.3 = (s32[64,512]{1,0:T(8,128)S(1)}, s32[64,512]{1,0:T(8,128)}, u32[]{:S(2)}) copy-start(s32[64,512]{1,0:T(8,128)} %offset_ref.1) | copy-start | bytes 393220
  10.6 7.3 %copy-start.4 = (f32[64,512]{1,0:T(8,128)S(1)}, f32[64,512]{1,0:T(8,128)}, u32[]{:S(2)}) copy-start(f32[64,512]{1,0:T(8,128)} %observed_ref.1) | copy-start | bytes 393220
  17.7 3.0 %collective-permute-start = (f32[1536,128]{1,0:T(8,128)S(1)}, f32[1536,128]{1,0:T(8,128)S(1)}, u32[]{:S(2)}, u32[]{:S(2)}) collective-permute-start(f32[1536,128]{1,0:T(8,128)S(1)} %get-tuple-element.59), channel_id=1, source_target_pairs={{0,1},{1,0},{2,3},{3,2},{4,5},{5,4},{6,7},{7,6},{8,9},{9,8},{10,11... | collective-permute-start | bytes 2359304 | tf_op jit(solution)/shard_map/ppermute | solution.py:880
  20.9 7.5 %collective-permute-start.1 = (f32[384,128]{1,0:T(8,128)S(1)}, f32[384,128]{1,0:T(8,128)S(1)}, u32[]{:S(2)}, u32[]{:S(2)}) collective-permute-start(f32[384,128]{1,0:T(8,128)S(1)} %get-tuple-element.73), channel_id=1, source_target_pairs={{0,2},{1,5},{2,0},{3,7},{4,6},{5,1},{6,4},{7,3},{8,10},{9,13},{10,... | collective-permute-start | bytes 589832 | tf_op jit(solution)/shard_map/ppermute | solution.py:880
  21.3 7.1 %collective-permute-start.2 = (f32[384,128]{1,0:T(8,128)S(1)}, f32[384,128]{1,0:T(8,128)S(1)}, u32[]{:S(2)}, u32[]{:S(2)}) collective-permute-start(f32[384,128]{1,0:T(8,128)S(1)} %get-tuple-element.75), channel_id=1, source_target_pairs={{0,4},{1,3},{2,6},{3,1},{4,0},{5,7},{6,2},{7,5},{8,12},{9,11},{10,... | collective-permute-start | bytes 589832 | tf_op jit(solution)/shard_map/ppermute | solution.py:880
  26.1 1.4 %collective-permute-start.3 = (f32[256,128]{1,0:T(8,128)S(1)}, f32[256,128]{1,0:T(8,128)S(1)}, u32[]{:S(2)}, u32[]{:S(2)}) collective-permute-start(f32[256,128]{1,0:T(8,128)S(1)} %get-tuple-element.77), channel_id=1, source_target_pairs={{0,1},{1,0},{2,3},{3,2},{4,5},{5,4},{6,7},{7,6},{8,9},{9,8},{10,11... | collective-permute-start | bytes 393224 | tf_op jit(solution)/shard_map/ppermute | solution.py:880
  28.5 7.2 %collective-permute-start.4 = (f32[256,128]{1,0:T(8,128)S(1)}, f32[256,128]{1,0:T(8,128)S(1)}, u32[]{:S(2)}, u32[]{:S(2)}) collective-permute-start(f32[256,128]{1,0:T(8,128)S(1)} %get-tuple-element.85), channel_id=1, source_target_pairs={{0,4},{1,3},{2,6},{3,1},{4,0},{5,7},{6,2},{7,5},{8,12},{9,11},{10,... | collective-permute-start | bytes 393224 | tf_op jit(solution)/shard_map/ppermute | solution.py:880
  28.9 6.8 %collective-permute-start.5 = (f32[256,128]{1,0:T(8,128)S(1)}, f32[256,128]{1,0:T(8,128)S(1)}, u32[]{:S(2)}, u32[]{:S(2)}) collective-permute-start(f32[256,128]{1,0:T(8,128)S(1)} %get-tuple-element.87), channel_id=1, source_target_pairs={{0,2},{1,5},{2,0},{3,7},{4,6},{5,1},{6,4},{7,3},{8,10},{9,13},{10,... | collective-permute-start | bytes 393224 | tf_op jit(solution)/shard_map/ppermute | solution.py:880
  30.5 5.2 %collective-permute-start.6 = (f32[64,128]{1,0:T(8,128)S(1)}, f32[64,128]{1,0:T(8,128)S(1)}, u32[]{:S(2)}, u32[]{:S(2)}) collective-permute-start(f32[64,128]{1,0:T(8,128)S(1)} %get-tuple-element.89), channel_id=1, source_target_pairs={{0,6},{1,7},{2,4},{3,5},{4,2},{5,3},{6,0},{7,1},{8,14},{9,15},{10,... | collective-permute-start | bytes 98312 | tf_op jit(solution)/shard_map/ppermute | solution.py:951
  35.8 6.0 %collective-permute-start.7 = (f32[104,128]{1,0:T(8,128)S(1)}, f32[104,128]{1,0:T(8,128)S(1)}, u32[]{:S(2)}, u32[]{:S(2)}) collective-permute-start(f32[104,128]{1,0:T(8,128)S(1)} %get-tuple-element.91), channel_id=1, source_target_pairs={{0,24},{1,17},{2,26},{3,19},{4,28},{5,21},{6,30},{7,23},{8,16},{9,... | collective-permute-start | bytes 159752 | tf_op jit(solution)/shard_map/ppermute | solution.py:874
  37.7 5.2 %collective-permute-start.8 = (f32[104,128]{1,0:T(8,128)S(1)}, f32[104,128]{1,0:T(8,128)S(1)}, u32[]{:S(2)}, u32[]{:S(2)}) collective-permute-start(f32[104,128]{1,0:T(8,128)S(1)} %get-tuple-element.92), channel_id=1, source_target_pairs={{0,8},{1,25},{2,10},{3,27},{4,12},{5,29},{6,14},{7,31},{8,0},{9,17... | collective-permute-start | bytes 159752 | tf_op jit(solution)/shard_map/ppermute | solution.py:874
  37.7 5.2 %collective-permute-start.9 = (f32[104,128]{1,0:T(8,128)S(1)}, f32[104,128]{1,0:T(8,128)S(1)}, u32[]{:S(2)}, u32[]{:S(2)}) collective-permute-start(f32[104,128]{1,0:T(8,128)S(1)} %get-tuple-element.93), channel_id=1, source_target_pairs={{0,16},{1,9},{2,18},{3,11},{4,20},{5,13},{6,22},{7,15},{8,24},{9,1... | collective-permute-start | bytes 159752 | tf_op jit(solution)/shard_map/ppermute | solution.py:874
